TPU v7x, 256 devices: a whole 4x4x8 slice. The times are simulated.
256 devices in a mesh: section: 4 (over y_lo, core), ctx: 64 (over y_hi, x, z).
Axes of the slice: x: 4, y: 4 (y_hi: 2, y_lo: 2; y = y_hi * 2 + y_lo), z: 8, core: 2. Of those that a mesh axis runs over, the one named last changes fastest.
Arguments:
- tokens: bfloat16 [2, 8192, 2048], P(None, 'ctx'), may hold values from -6 to 6
- qkv_weight: bfloat16 [4, 2048, 3072], P('section', 'ctx'), may hold values from -0.125 to 0.125
- out_weight: bfloat16 [4, 1024, 2048], P('section', 'ctx'), may hold values from -0.1875 to 0.1875
- log_decay: float32 [4, 2, 8192, 16], P('section', None, 'ctx'), may hold values from -1.5 to 0, as said below
Outputs:
- hidden_states: bfloat16 [4, 2, 8192, 2048], P('section', None, 'ctx')
Inputs may be any that keep to these rules, and one draw needn't show every extreme that they name: `log_decay`: every value is negative.
All inputs are finite; a program needn't handle non-finite values.
Results may differ from a plain program's by a relative error of at most 0.025.
Values may be sent and summed in bfloat16 or wider, within the bound.
No kernel may reach another device: no remote copies, remote signals or barrier semaphores. Data moves between devices by JAX's collectives and lax.ppermute only.
A program may use at most 128 MiB of HBM per device.

v0:
```python
import jax
import jax.numpy as jnp
from jax import lax
from jax.sharding import PartitionSpec as P


def passed_along(value, axis, by):
    devices = lax.axis_size(axis)
    pairs = [(i, i + by) for i in range(devices) if 0 <= i + by < devices]
    return lax.ppermute(value, axis, pairs)


def entering(value, axis, join, neutral):
    place = lax.axis_index(axis)
    gathered = jax.tree.map(
        lambda a, kind: lax.all_gather(a.astype(kind), axis), value, (jnp.bfloat16, jnp.bfloat16)
    )
    state = jax.tree.map(lambda a, e: jnp.zeros_like(a) + jnp.asarray(e, a.dtype), value, neutral)

    def one(hop, state):
        return join(
            state,
            jax.tree.map(
                lambda a, own: lax.dynamic_index_in_dim(a, hop, 0, False).astype(own.dtype),
                gathered,
                value,
            ),
        )

    return lax.fori_loop(0, place, one, state)


def normalize_rows(value_rows):
    return value_rows * lax.rsqrt(jnp.mean(value_rows * value_rows, axis=-1, keepdims=True) + 1e-05)


def local_terms(incoming, weight_full, decay):
    row_count = incoming.shape[0]
    head_count = decay.shape[1]
    normed = normalize_rows(incoming.astype(jnp.float32)).astype(jnp.bfloat16)
    projected = jnp.dot(normed, weight_full, preferred_element_type=jnp.float32).astype(
        jnp.bfloat16
    )
    inner = projected.shape[1] // 3
    head_dim = inner // head_count
    query_rows = projected[:, :inner].reshape(row_count, head_count, head_dim)
    key_block = projected[:, inner : 2 * inner].reshape(row_count, head_count, head_dim)
    value_rows = projected[:, 2 * inner :].reshape(row_count, head_count, head_dim)
    cumulative = jnp.cumsum(decay, axis=0)
    ending = cumulative[-1]
    key_rows_scaled = (
        key_block.astype(jnp.float32) * jnp.exp(ending[None, :] - cumulative)[:, :, None]
    ).astype(jnp.bfloat16)
    block_state = jnp.einsum(
        "yao,yau->aou", key_rows_scaled, value_rows, preferred_element_type=jnp.float32
    )
    return (query_rows, key_block, value_rows, cumulative, block_state, jnp.exp(ending))


def block_attention(query_rows, key_block, value_rows, cumulative):
    row_count = query_rows.shape[0]
    scores = jnp.einsum("thk,jhk->htj", query_rows, key_block, preferred_element_type=jnp.float32)
    per_head = cumulative.T
    decay_gap = per_head[:, :, None] - per_head[:, None, :]
    position_index = jnp.arange(row_count, dtype=jnp.int32)
    causal = position_index[:, None] >= position_index[None, :]
    weights = jnp.where(causal, scores * jnp.exp(jnp.where(causal, decay_gap, 0.0)), 0.0).astype(
        jnp.bfloat16
    )
    return jnp.einsum("htj,jhv->thv", weights, value_rows, preferred_element_type=jnp.float32)


def combine_states(earlier, later):
    return (earlier[0] * later[0], later[0][:, None, None] * earlier[1] + later[1])


def shards(tokens, qkv_weight, out_weight, log_decay):
    sections = lax.axis_size("section")
    section_id = lax.axis_index("section")
    weight_full, out_full = (
        lax.all_gather(qkv_weight[0], "ctx", axis=0, tiled=True),
        lax.all_gather(out_weight[0], "ctx", axis=0, tiled=True),
    )
    micro_count, row_count, model_width = tokens.shape
    head_count = log_decay.shape[3]
    inner = qkv_weight.shape[2] // 3
    head_dim = inner // head_count
    buffer = jnp.zeros((micro_count, row_count, model_width), jnp.bfloat16)
    previous = jnp.zeros((row_count, model_width), jnp.bfloat16)
    for time_step in range(micro_count + sections - 1):
        if time_step > 0:
            received = passed_along(previous, "section", 1)
        else:
            received = jnp.zeros((row_count, model_width), jnp.bfloat16)
        micro_index = time_step - section_id
        active = jnp.logical_and(micro_index >= 0, micro_index < micro_count)
        mb_clip = jnp.clip(micro_index, 0, micro_count - 1)
        own_input = lax.dynamic_index_in_dim(tokens, mb_clip, 0, keepdims=False)
        incoming = jnp.where(section_id == 0, own_input, received)
        decay = lax.dynamic_index_in_dim(log_decay[0], mb_clip, 0, keepdims=False)
        query_rows, key_block, value_rows, cumulative, block_state, block_total = local_terms(
            incoming, weight_full, decay
        )
        intra_out = block_attention(query_rows, key_block, value_rows, cumulative)
        identity = (
            jnp.ones((head_count,), jnp.float32),
            jnp.zeros((head_count, head_dim, head_dim), jnp.float32),
        )
        prefix_total, carried = entering(
            (block_total, block_state), "ctx", combine_states, identity
        )
        carried_state_low = carried.astype(jnp.bfloat16)
        inter_out = (
            jnp.einsum(
                "npc,pco->npo", query_rows, carried_state_low, preferred_element_type=jnp.float32
            )
            * jnp.exp(cumulative)[:, :, None]
        )
        mixture = intra_out + inter_out
        mixed_low = normalize_rows(mixture).reshape(row_count, inner).astype(jnp.bfloat16)
        mixed = jnp.dot(mixed_low, out_full, preferred_element_type=jnp.float32)
        result = (incoming.astype(jnp.float32) + mixed).astype(jnp.bfloat16)
        current_row = lax.dynamic_index_in_dim(buffer, mb_clip, 0, keepdims=False)
        buffer = lax.dynamic_update_index_in_dim(
            buffer, jnp.where(active, result, current_row), mb_clip, 0
        )
        previous = result
    return buffer[None]


def solution(mesh):
    in_specs = (
        P(None, "ctx", None),
        P("section", "ctx", None),
        P("section", "ctx", None),
        P("section", None, "ctx", None),
    )
    out_specs = P("section", None, "ctx", None)
    return jax.shard_map(shards, mesh=mesh, in_specs=in_specs, out_specs=out_specs, check_vma=False)
```

profile of v0, /device:TPU:254, one launch (start us, length us, event | category | flops | bytes accessed | tf_op | source)
XLA Modules:
  0.0 1814.2 jit_solution(4220933567526693187)
XLA Ops:
  10.4 169.2 %all-gather.20.cloned.1.call-done = bf16[1,2048,3072]{2,1,0:T(8,128)(2,1)} async-done(((bf16[1,32,3072]{2,1,0:T(8,128)(2,1)}), bf16[1,2048,3072]{2,1,0:T(8,128)(2,1)}) %all-gather.20.cloned.1.call-update) | async-done | bytes 12582928 | tf_op jit(solution)/shard_map/all_gather | solution.py:81
  179.6 6.7 fusion.20
  188.5 173.0 %all-gather.7 = bf16[64,1,16]{2,1,0:T(2,128)(2,1)S(1)} all-gather(bf16[1,1,16]{2,1,0:T(2,128)(2,1)S(1)} %get-tuple-element.372), channel_id=1, replica_groups=mesh['section'=4,'ctx'=64] {'ctx'}, dimensions={0}, use_global_device_ids=true | all-gather | bytes 2080 | tf_op jit(solution)/shard_map/all_gather | solution.py:16
  362.6 21.5 %all-gather.22.cloned.1.call-done = bf16[1024,64,64]{2,1,0:T(8,128)(2,1)} async-done(((bf16[16,64,64]{2,1,0:T(8,128)(2,1)}), bf16[1024,64,64]{2,1,0:T(8,128)(2,1)}) %all-gather.22.cloned.1.call-update) | async-done | bytes 8388624 | tf_op jit(solution)/shard_map/all_gather | solution.py:16
  384.2 73.1 %while.60 = (s32[]{:T(128)}, f32[16,64,64]{2,1,0:T(8,128)S(1)}, s32[]{:T(128)}, bf16[64,16]{1,0:T(8,128)(2,1)S(1)}, bf16[64,16,64,64]{3,2,1,0:T(8,128)(2,1)}, /*index=5*/s32[]{:T(128)}, s32[]{:T(128)}, s32[]{:T(128)}) while((s32[]{:T(128)}, f32[16,64,64]{2,1,0:T(8,128)S(1)}, s32[]{:T(128)}, bf16[64,16]{1,0:T(8,128)(2,1)S(1)}, ...), condition=%wide.region_3.4_spmd, body=%wide.region_2.3_spmd.sunk | while | flops 196629 | bytes 655647 | solution.py:30
  457.6 54.9 %all-gather.24.cloned.1.call-done = bf16[1,1024,2048]{2,1,0:T(8,128)(2,1)} async-done(((bf16[1,16,2048]{2,1,0:T(8,128)(2,1)}), bf16[1,1024,2048]{2,1,0:T(8,128)(2,1)}) %all-gather.24.cloned.1.call-update) | async-done | bytes 4194320 | tf_op jit(solution)/shard_map/all_gather | solution.py:82
  512.7 3.7 bitcast_dynamic-update-slice_fusion.3
  519.2 7.9 collective-permute-done
  527.4 6.5 fusion.23
  536.1 173.2 %all-gather.8 = bf16[64,1,16]{2,1,0:T(2,128)(2,1)S(1)} all-gather(bf16[1,1,16]{2,1,0:T(2,128)(2,1)} %get-tuple-element.368), channel_id=1, replica_groups=mesh['section'=4,'ctx'=64] {'ctx'}, dimensions={0}, use_global_device_ids=true | all-gather | bytes 2080 | tf_op jit(solution)/shard_map/all_gather | solution.py:16
  715.0 17.0 all-gather.26.cloned.1.call-done
  732.1 113.4 %while.61 = (s32[]{:T(128)}, f32[16,64,64]{2,1,0:T(8,128)S(1)}, s32[]{:T(128)}, bf16[64,16]{1,0:T(8,128)(2,1)}, bf16[64,16,64,64]{3,2,1,0:T(8,128)(2,1)}, /*index=5*/s32[]{:T(128)}, s32[]{:T(128)}, s32[]{:T(128)}) while((s32[]{:T(128)}, f32[16,64,64]{2,1,0:T(8,128)S(1)}, s32[]{:T(128)}, bf16[64,16]{1,0:T(8,128)(2,1)}, ...), condition=%wide.region_8.9_spmd, body=%wide.region_7.8_spmd.sunk | while | flops 196629 | bytes 655647 | solution.py:30
  846.9 3.9 bitcast_dynamic-update-slice_fusion.2
  853.8 7.7 collective-permute-done.1
  861.8 6.5 fusion.26
  870.5 173.2 %all-gather.9 = bf16[64,1,16]{2,1,0:T(2,128)(2,1)S(1)} all-gather(bf16[1,1,16]{2,1,0:T(2,128)(2,1)} %get-tuple-element.364), channel_id=1, replica_groups=mesh['section'=4,'ctx'=64] {'ctx'}, dimensions={0}, use_global_device_ids=true | all-gather | bytes 2080 | tf_op jit(solution)/shard_map/all_gather | solution.py:16
  1047.0 2.4 convolution_bitcast_fusion.5
  1049.4 15.5 all-gather.28.cloned.1.call-done
  1064.9 113.5 %while.62 = (s32[]{:T(128)}, f32[16,64,64]{2,1,0:T(8,128)S(1)}, s32[]{:T(128)}, bf16[64,16]{1,0:T(8,128)(2,1)}, bf16[64,16,64,64]{3,2,1,0:T(8,128)(2,1)}, /*index=5*/s32[]{:T(128)}, s32[]{:T(128)}, s32[]{:T(128)}) while((s32[]{:T(128)}, f32[16,64,64]{2,1,0:T(8,128)S(1)}, s32[]{:T(128)}, bf16[64,16]{1,0:T(8,128)(2,1)}, ...), condition=%wide.region_13.14_spmd, body=%wide.region_12.13_spmd.sunk | while | flops 196629 | bytes 655647 | solution.py:30
  1179.9 3.9 bitcast_dynamic-update-slice_fusion.1
  1186.6 7.9 collective-permute-done.2
  1194.8 6.5 fusion.29
  1203.4 173.2 %all-gather.10 = bf16[64,1,16]{2,1,0:T(2,128)(2,1)S(1)} all-gather(bf16[1,1,16]{2,1,0:T(2,128)(2,1)} %get-tuple-element.360), channel_id=1, replica_groups=mesh['section'=4,'ctx'=64] {'ctx'}, dimensions={0}, use_global_device_ids=true | all-gather | bytes 2080 | tf_op jit(solution)/shard_map/all_gather | solution.py:16
  1381.7 16.1 all-gather.30.cloned.1.call-done
  1397.9 113.5 %while.63 = (s32[]{:T(128)}, f32[16,64,64]{2,1,0:T(8,128)S(1)}, s32[]{:T(128)}, bf16[64,16]{1,0:T(8,128)(2,1)}, bf16[64,16,64,64]{3,2,1,0:T(8,128)(2,1)}, /*index=5*/s32[]{:T(128)}, s32[]{:T(128)}, s32[]{:T(128)}) while((s32[]{:T(128)}, f32[16,64,64]{2,1,0:T(8,128)S(1)}, s32[]{:T(128)}, bf16[64,16]{1,0:T(8,128)(2,1)}, ...), condition=%wide.region_18.19_spmd, body=%wide.region_17.18_spmd.sunk | while | flops 196629 | bytes 655647 | solution.py:30
  1512.8 3.9 bitcast_dynamic-update-slice_fusion
  1519.2 8.2 collective-permute-done.3
  1527.8 6.5 fusion.32
  1535.7 173.0 %all-gather.11 = bf16[64,1,16]{2,1,0:T(2,128)(2,1)S(1)} all-gather(bf16[1,1,16]{2,1,0:T(2,128)(2,1)S(1)} %get-tuple-element.356), channel_id=1, replica_groups=mesh['section'=4,'ctx'=64] {'ctx'}, dimensions={0}, use_global_device_ids=true | all-gather | bytes 2080 | tf_op jit(solution)/shard_map/all_gather | solution.py:16
  1710.8 19.4 %all-gather.32.cloned.1.call-done = bf16[1024,64,64]{2,1,0:T(8,128)(2,1)} async-done(((bf16[16,64,64]{2,1,0:T(8,128)(2,1)}), bf16[1024,64,64]{2,1,0:T(8,128)(2,1)}) %all-gather.32.cloned.1.call-update) | async-done | bytes 8388624 | tf_op jit(solution)/shard_map/all_gather | solution.py:16
  1730.2 73.0 %while.64 = (s32[]{:T(128)}, f32[16,64,64]{2,1,0:T(8,128)S(1)}, s32[]{:T(128)}, bf16[64,16]{1,0:T(8,128)(2,1)S(1)}, bf16[64,16,64,64]{3,2,1,0:T(8,128)(2,1)}, /*index=5*/s32[]{:T(128)}, s32[]{:T(128)}, s32[]{:T(128)}) while((s32[]{:T(128)}, f32[16,64,64]{2,1,0:T(8,128)S(1)}, s32[]{:T(128)}, bf16[64,16]{1,0:T(8,128)(2,1)S(1)}, ...), condition=%wide.region_23.24_spmd, body=%wide.region_22.23_spmd.sunk | while | flops 196629 | bytes 655647 | solution.py:30
  1803.6 3.8 fusion.71
  (764 shorter events, 524.6 us)
Async XLA Ops:
  6.5 173.0 %all-gather.20.cloned.1.call-start = ((), (), s32[]{:S(2)}) async-start(), calls=%async_computation | async-start | bytes 12779520 | tf_op jit(solution)/shard_map/all_gather | solution.py:81
  7.3 376.9 %all-gather.22.cloned.1.call-start = ((), (), s32[]{:S(2)}) async-start(), calls=%async_computation.1 | async-start | bytes 17039360 | tf_op jit(solution)/shard_map/all_gather | solution.py:16
  186.2 326.4 %copy-start = (bf16[2,128,2048]{2,1,0:T(8,128)(2,1)S(1)}, bf16[2,128,2048]{2,1,0:T(8,128)(2,1)}, u32[]{:S(2)}) copy-start(bf16[2,128,2048]{2,1,0:T(8,128)(2,1)} %param.14) | copy-start | bytes 3145732
  187.7 324.9 %all-gather.24.cloned.1.call-start = ((), (), s32[]{:S(2)}) async-start(), calls=%async_computation.2 | async-start | bytes 4259840 | tf_op jit(solution)/shard_map/all_gather | solution.py:82
  188.4 543.6 %all-gather.26.cloned.1.call-start = ((), (), s32[]{:S(2)}) async-start(), calls=%async_computation.3 | async-start | bytes 17039360 | tf_op jit(solution)/shard_map/all_gather | solution.py:16
  361.6 95.6 %copy-start.3 = (pred[128,128]{1,0:T(8,128)(4,1)}, pred[128,128]{1,0:T(8,128)(4,1)S(1)}, u32[]{:S(2)}) copy-start(pred[128,128]{1,0:T(8,128)(4,1)S(1)} %iota_compare_fusion) | copy-start | bytes 49156
  516.4 10.7 collective-permute-start
  536.0 316.9 %copy-start.2 = (f32[128,16]{0,1:T(8,128)S(1)}, f32[128,16]{0,1:T(8,128)}, u32[]{:S(2)}) copy-start(f32[128,16]{0,1:T(8,128)} %get-tuple-element.374) | copy-start | bytes 24580
  536.0 528.8 %all-gather.28.cloned.1.call-start = ((), (), s32[]{:S(2)}) async-start(), calls=%async_computation.4 | async-start | bytes 17039360 | tf_op jit(solution)/shard_map/all_gather | solution.py:16
  850.8 10.7 collective-permute-start.1
  870.4 315.3 %copy-start.1 = (f32[128,16]{0,1:T(8,128)S(1)}, f32[128,16]{0,1:T(8,128)}, u32[]{:S(2)}) copy-start(f32[128,16]{0,1:T(8,128)} %get-tuple-element.377) | copy-start | bytes 24580
  870.4 527.4 %all-gather.30.cloned.1.call-start = ((), (), s32[]{:S(2)}) async-start(), calls=%async_computation.5 | async-start | bytes 17039360 | tf_op jit(solution)/shard_map/all_gather | solution.py:16
  1183.8 10.7 collective-permute-start.2
  1203.4 526.7 %all-gather.32.cloned.1.call-start = ((), (), s32[]{:S(2)}) async-start(), calls=%async_computation.6 | async-start | bytes 17039360 | tf_op jit(solution)/shard_map/all_gather | solution.py:16
  1516.7 10.7 collective-permute-start.3
  1527.7 182.2 %copy-start.4 = (pred[128,128]{1,0:T(8,128)(4,1)S(1)}, pred[128,128]{1,0:T(8,128)(4,1)}, u32[]{:S(2)}) copy-start(pred[128,128]{1,0:T(8,128)(4,1)} %copy-done.3) | copy-start | bytes 49156
Sparse Core Ops, SparseCore 0:
  11.0 168.4 all-gather.19
  187.8 196.2 all-gather.21
  387.8 124.7 all-gather.23
  536.2 195.8 all-gather.25
  870.5 194.2 all-gather.27
  1203.5 194.2 all-gather.29
  1535.8 194.2 all-gather.31
where the time goes:
time: 1830 us; the launch traced here: 1810 us
  blocking collectives  866 us (47%)
  other arithmetic  481 us (26%)
  waiting for transfers between devices  347 us (19%)
  matrix products  70 us (4%)
    all_gather x5, blocking collectives, entering(): lax.all_gather(a.astype(kind), axis)  866 us
    add x315, other arithmetic, combine_states(): later[0][:, None, None] * earlier[1] + later[1]  349 us
    all_gather x1, waiting for transfers between devices, shards(): lax.all_gather(qkv_weight[0], 'ctx', axis=0, tiled=True)  169 us
    convert_element_type x315, other arithmetic, one(): lax.dynamic_index_in_dim(a, hop, 0, False).astype(own.dtype)  127 us
    all_gather x5, waiting for transfers between devices, entering(): lax.all_gather(a.astype(kind), axis)  89.5 us
    all_gather x1, waiting for transfers between devices, shards(): lax.all_gather(out_weight[0], 'ctx', axis=0, tiled=True)  54.9 us
  transfers between devices with their start and end apart: 11, of which 11 were waited for; matrix products, arithmetic and copies ran while one was open for 5% of the time, Pallas kernels for 0%

commit v1 on v0

v1 whole, which is shorter than its diff:
```python
import functools

import jax
import jax.numpy as jnp
from jax import lax
from jax.experimental import pallas as pl
from jax.experimental.pallas import tpu as pltpu
from jax.sharding import Mesh, PartitionSpec as P

CTX = ("yhi", "x", "z")
SPREAD = ("core", "x", "z")
NB = 512
EPS = 1e-05


def swap(value, axis):
    return lax.ppermute(value, axis, [(0, 1), (1, 0)])


def half_mask(rows, lanes, half):
    return lax.broadcasted_iota(jnp.int32, (rows, lanes), 1) < half


def by_head(low, table, p):
    return jnp.where(low, table[:, 2 * p : 2 * p + 1], table[:, 2 * p + 1 : 2 * p + 2])


def project_kernel(x_ref, w_ref, scale_ref, proj_ref, state_ref, normed_ref):
    n = pl.program_id(0)
    rows, width = x_ref.shape
    half = width // 2
    inner = proj_ref.shape[1] // 3
    part = w_ref.shape[2] // 2

    @pl.when(n == 0)
    def _():
        x = x_ref[...].astype(jnp.float32)
        scale = lax.rsqrt(jnp.mean(x * x, axis=-1, keepdims=True) + EPS)
        normed_ref[...] = (x * scale).astype(jnp.bfloat16)

    acc = jnp.dot(
        normed_ref[:, :half],
        w_ref[0, :, :part, :].reshape(half, NB),
        preferred_element_type=jnp.float32,
    )
    acc += jnp.dot(
        normed_ref[:, half:],
        w_ref[0, :, part:, :].reshape(half, NB),
        preferred_element_type=jnp.float32,
    )
    proj_ref[:, pl.ds(pl.multiple_of(n * NB, NB), NB)] = acc.astype(jnp.bfloat16)

    @pl.when(n == pl.num_programs(0) - 1)
    def _():
        low = half_mask(rows, 128, 64)
        scale = scale_ref[...]
        for p in range(inner // 128):
            keys = proj_ref[:, inner + 128 * p : inner + 128 * (p + 1)].astype(jnp.float32)
            values = proj_ref[:, 2 * inner + 128 * p : 2 * inner + 128 * (p + 1)]
            scaled = (keys * by_head(low, scale, p)).astype(jnp.bfloat16)
            outer = lax.dot_general(
                scaled, values, (((0,), (0,)), ((), ())), preferred_element_type=jnp.float32
            )
            state_ref[64 * p : 64 * (p + 1), :] = jnp.where(
                low[:64], outer[:64], outer[64:]
            ).astype(jnp.bfloat16)


def project(x, weights, scale):
    rows, width = x.shape
    groups = weights.shape[1]
    share = width // groups
    inner = 1024
    blocks = 3 * inner // NB
    per_core = blocks // 2
    return pl.pallas_call(
        project_kernel,
        grid=(blocks,),
        in_specs=[
            pl.BlockSpec((rows, width), lambda n: (0, 0)),
            pl.BlockSpec((1, groups, share, NB), lambda n: (n // per_core, 0, n % per_core, 0)),
            pl.BlockSpec(scale.shape, lambda n: (0, 0)),
        ],
        out_specs=[
            pl.BlockSpec((rows, 3 * inner), lambda n: (0, 0)),
            pl.BlockSpec((inner // 2, 128), lambda n: (0, 0)),
        ],
        out_shape=[
            jax.ShapeDtypeStruct((rows, 3 * inner), jnp.bfloat16),
            jax.ShapeDtypeStruct((inner // 2, 128), jnp.bfloat16),
        ],
        scratch_shapes=[pltpu.VMEM((rows, width), jnp.bfloat16)],
        compiler_params=pltpu.CompilerParams(vmem_limit_bytes=24 * 2**20),
        cost_estimate=pl.CostEstimate(
            flops=2 * rows * width * 3 * inner, bytes_accessed=6 * width * inner, transcendentals=0
        ),
        name="project",
    )(x, weights, scale)


def within_kernel(proj_ref, cum_ref, cum_t_ref, out_ref):
    rows = proj_ref.shape[0]
    inner = proj_ref.shape[1] // 3
    low = half_mask(rows, 128, 64)
    causal = lax.broadcasted_iota(jnp.int32, (rows, rows), 0) >= lax.broadcasted_iota(
        jnp.int32, (rows, rows), 1
    )
    cum = cum_ref[...]
    cum_t = cum_t_ref[...]
    zero = jnp.zeros((rows, 128), jnp.bfloat16)
    for p in range(inner // 128):
        queries = proj_ref[:, 128 * p : 128 * (p + 1)]
        keys = proj_ref[:, inner + 128 * p : inner + 128 * (p + 1)]
        values = proj_ref[:, 2 * inner + 128 * p : 2 * inner + 128 * (p + 1)]
        weights = []
        for k in range(2):
            h = 2 * p + k
            own = jnp.where(low, queries, zero) if k == 0 else jnp.where(low, zero, queries)
            scores = lax.dot_general(
                own, keys, (((1,), (1,)), ((), ())), preferred_element_type=jnp.float32
            )
            gap = cum[:, h : h + 1] - cum_t[h : h + 1, :]
            decay = jnp.exp(jnp.where(causal, gap, 0.0))
            weights.append(jnp.where(causal, scores * decay, 0.0).astype(jnp.bfloat16))
        both = jnp.concatenate(
            [jnp.where(low, values, zero), jnp.where(low, zero, values)], axis=0
        )
        out_ref[:, 128 * p : 128 * (p + 1)] = jnp.dot(
            jnp.concatenate(weights, axis=1), both, preferred_element_type=jnp.float32
        )


def within(proj, cum, cum_t):
    rows, cols = proj.shape
    return pl.pallas_call(
        within_kernel,
        out_shape=jax.ShapeDtypeStruct((rows, cols // 3), jnp.float32),
        compiler_params=pltpu.CompilerParams(vmem_limit_bytes=16 * 2**20),
        cost_estimate=pl.CostEstimate(
            flops=2 * rows * rows * cols, bytes_accessed=4 * rows * cols, transcendentals=16 * rows * rows
        ),
        name="within",
    )(proj, cum, cum_t)


def carry_kernel(state_ref, total_ref, out_ref):
    carried = jnp.zeros(state_ref.shape[1:], jnp.float32)
    for c in range(state_ref.shape[0]):
        out_ref[c] = carried.astype(jnp.bfloat16)
        carried = total_ref[c : c + 1, :] * carried + state_ref[c].astype(jnp.float32)


def carry(states, totals):
    return pl.pallas_call(
        carry_kernel,
        out_shape=jax.ShapeDtypeStruct(states.shape, jnp.bfloat16),
        cost_estimate=pl.CostEstimate(flops=2 * states.size, bytes_accessed=4 * states.size, transcendentals=0),
        name="carry",
    )(states, totals)


def output_kernel(q_ref, carried_ref, grow_ref, within_ref, x_ref, w_ref, out_ref, mixed_ref):
    n = pl.program_id(0)
    rows, inner = within_ref.shape
    half = inner // 2
    part = w_ref.shape[2] // 2

    @pl.when(n == 0)
    def _():
        low = half_mask(rows, 128, 64)
        low64 = low[:64]
        zero = jnp.zeros((64, 128), jnp.bfloat16)
        grow = grow_ref[...]
        for p in range(inner // 128):
            cols = slice(128 * p, 128 * (p + 1))
            state = carried_ref[64 * p : 64 * (p + 1), :]
            both = jnp.concatenate(
                [jnp.where(low64, state, zero), jnp.where(low64, zero, state)], axis=0
            )
            earlier = jnp.dot(q_ref[:, cols], both, preferred_element_type=jnp.float32)
            mixture = within_ref[:, cols] + earlier * by_head(low, grow, p)
            square = mixture * mixture
            first = jnp.sum(jnp.where(low, square, 0.0), axis=-1, keepdims=True)
            second = jnp.sum(jnp.where(low, 0.0, square), axis=-1, keepdims=True)
            scale = jnp.where(
                low, lax.rsqrt(first * (1.0 / 64.0) + EPS), lax.rsqrt(second * (1.0 / 64.0) + EPS)
            )
            mixed_ref[:, cols] = (mixture * scale).astype(jnp.bfloat16)

    acc = jnp.dot(
        mixed_ref[:, :half],
        w_ref[0, :, :part, :].reshape(half, NB),
        preferred_element_type=jnp.float32,
    )
    acc += jnp.dot(
        mixed_ref[:, half:],
        w_ref[0, :, part:, :].reshape(half, NB),
        preferred_element_type=jnp.float32,
    )
    out_ref[...] = (x_ref[...].astype(jnp.float32) + acc).astype(jnp.bfloat16)


def output(proj, carried, grow, inside, x, weights):
    rows, width = x.shape
    inner = inside.shape[1]
    groups = weights.shape[1]
    share = inner // groups
    blocks = width // NB
    per_core = blocks // 2
    first = 3 * inner // 2 // NB * (width // groups) // share
    return pl.pallas_call(
        output_kernel,
        grid=(blocks,),
        in_specs=[
            pl.BlockSpec((rows, inner), lambda n: (0, 0)),
            pl.BlockSpec(carried.shape, lambda n: (0, 0)),
            pl.BlockSpec(grow.shape, lambda n: (0, 0)),
            pl.BlockSpec((rows, inner), lambda n: (0, 0)),
            pl.BlockSpec((rows, NB), lambda n: (0, n)),
            pl.BlockSpec(
                (1, groups, share, NB), lambda n: (n // per_core, 0, first + n % per_core, 0)
            ),
        ],
        out_specs=pl.BlockSpec((rows, NB), lambda n: (0, n)),
        out_shape=jax.ShapeDtypeStruct((rows, width), jnp.bfloat16),
        scratch_shapes=[pltpu.VMEM((rows, inner), jnp.bfloat16)],
        compiler_params=pltpu.CompilerParams(vmem_limit_bytes=24 * 2**20),
        cost_estimate=pl.CostEstimate(
            flops=2 * rows * width * inner, bytes_accessed=2 * width * inner, transcendentals=0
        ),
        name="output",
    )(proj, carried, grow, inside, x, weights)


def in_blocks(value):
    rows, cols = value.shape[-2:]
    split = value.reshape(value.shape[:-1] + (cols // NB, NB))
    return jnp.moveaxis(split, -2, -3)


def shared_weights(qkv, out, core):
    def halves(value):
        cols = value.shape[1] // 2
        low, high = value[:, :cols], value[:, cols:]
        keep = jnp.where(core == 0, low, high)
        other = swap(jnp.where(core == 0, high, low), "core")
        layers = jnp.stack([jnp.where(core == 0, keep, other), jnp.where(core == 0, other, keep)])
        return in_blocks(layers)

    parts = [halves(qkv), halves(out)]
    place = lax.axis_index("yhi")
    flat = []
    for part in parts:
        far = swap(part, "yhi")
        pair = jnp.stack(
            [jnp.where(place == 0, part, far), jnp.where(place == 0, far, part)], axis=2
        )
        flat.append(pair.reshape(2, -1, NB))
    own = jnp.concatenate(flat, axis=1)
    return [
        lax.all_gather(own[k], SPREAD, axis=0).reshape(2, -1, own.shape[1], NB) for k in range(2)
    ]


def decays(log_decay, core):
    keep = jnp.where(core == 0, log_decay[0], log_decay[1])
    other = swap(jnp.where(core == 0, log_decay[1], log_decay[0]), "core")
    both = [jnp.where(core == 0, keep, other), jnp.where(core == 0, other, keep)]
    rows, heads = keep.shape
    lower = jnp.tril(jnp.ones((rows, rows), jnp.float32))
    blocks = lax.axis_size(CTX)
    per_pair = blocks // (heads // 2)
    out, rows_sent = [], []
    for d in both:
        cum = jnp.dot(lower, d, precision=lax.Precision.HIGHEST)
        ending = cum[-1:]
        total = jnp.exp(ending[0])
        lanes = jnp.repeat(total.reshape(heads // 2, 2), 64, axis=1)
        rows_sent.append(jnp.repeat(lanes, per_pair, axis=0))
        out.append([cum, cum.T, jnp.exp(ending - cum), jnp.exp(cum)])
    sent = jnp.stack(rows_sent + [jnp.zeros_like(rows_sent[0])] * 6, axis=1)
    received = lax.all_to_all(sent, CTX, 0, 0, tiled=True)
    for k in range(2):
        out[k].append(received[:, k, :])
    return out


def shards(tokens, qkv_weight, out_weight, log_decay):
    core = lax.axis_index("core")
    level = lax.axis_index("ylo")
    blocks = lax.axis_size(CTX)
    x = lax.dynamic_index_in_dim(tokens, core, 0, False)
    weights = shared_weights(qkv_weight[0], out_weight[0], core)
    tables = decays(log_decay[0], core)
    kept = []
    for step in range(4):
        cum, cum_t, scale, grow, totals = tables[step % 2]
        w = weights[step % 2]
        if step == 2:
            x = lax.ppermute(x, "ylo", [(0, 1)])
        proj, state = project(x, w, scale)
        slices = lax.all_to_all(state.reshape(blocks, -1, 128), CTX, 0, 0, tiled=True)
        inside = within(proj, cum, cum_t)
        mine = carry(slices, totals)
        carried = lax.all_to_all(mine, CTX, 0, 0, tiled=True).reshape(state.shape)
        x = output(proj, carried, grow, inside, x, w)
        kept.append(x)
    first = jnp.where(level == 0, kept[0], kept[2])
    second = jnp.where(level == 0, kept[1], kept[3])
    other = swap(jnp.where(core == 0, second, first), "core")
    result = jnp.stack([jnp.where(core == 0, first, other), jnp.where(core == 0, other, second)])
    return result[None]


def solution(mesh):
    fine = Mesh(mesh.devices.reshape(2, 2, 2, 4, 8), ("ylo", "core") + CTX)
    section = ("ylo", "core")
    in_specs = (
        P(None, CTX, None),
        P(section, CTX, None),
        P(section, CTX, None),
        P(section, None, CTX, None),
    )
    return jax.shard_map(
        shards, mesh=fine, in_specs=in_specs, out_specs=P(section, None, CTX, None), check_vma=False
    )
```

time: 1830 us -> 435 us (0.24)
  the two profiles are of different devices: /device:TPU:254 before, /device:TPU:1 now
where the time goes in v1:
time: 435 us; the launch traced here: 433 us
  waiting for transfers between devices  188 us (43%)
  local copies, waits for them, and re-layouts  61.2 us (14%)
  starting transfers between devices  61.2 us (14%)
  blocking collectives  52.3 us (12%)
  Pallas kernels  44.9 us (10%)
  between operations  13.8 us (3%)
  other arithmetic  9.49 us (2%)
    all_gather x2, waiting for transfers between devices, shared_weights(): lax.all_gather(own[k], SPREAD, axis=0).reshape(2, -1, own.shape[1], NB)  122 us
    unnamed x56, local copies, waits for them, and re-layouts  58.9 us
    all_to_all x3, blocking collectives, shards(): lax.all_to_all(state.reshape(blocks, -1, 128), CTX, 0, 0, tiled=True)  52.3 us
    all_to_all x4, waiting for transfers between devices, shards(): carried = lax.all_to_all(mine, CTX, 0, 0, tiled=True).reshape(state.shape)  37.3 us
    all_to_all x4, starting transfers between devices, shards(): carried = lax.all_to_all(mine, CTX, 0, 0, tiled=True).reshape(state.shape)  22.2 us
    pallas_call x4, Pallas kernels, project(): pl.pallas_call(project_kernel, grid=(blocks,), in_specs=[pl.BlockSpec((ro...  19.2 us
    ppermute x6, starting transfers between devices, swap(): return lax.ppermute(value, axis, [(0, 1), (1, 0)])  16.7 us
    pallas_call x4, Pallas kernels, output(): pl.pallas_call(output_kernel, grid=(blocks,), in_specs=[pl.BlockSpec((row...  13.4 us
  transfers between devices with their start and end apart: 15, of which 12 were waited for; matrix products, arithmetic and copies ran while one was open for 2% of the time, Pallas kernels for 4%

profile of v1, /device:TPU:1, one launch (start us, length us, event | category | flops | bytes accessed | tf_op | source)
XLA Modules:
  0.0 433.1 jit_solution(9936061276105841696)
XLA Ops:
  17.4 6.5 %collective-permute-done.1 = bf16[2,3,32,512]{3,1,2,0:T(4,128)(2,1)S(1)} collective-permute-done((bf16[2,3,32,512]{3,1,2,0:T(4,128)(2,1)S(1)}, bf16[2,3,32,512]{3,1,2,0:T(4,128)(2,1)S(1)}, u32[]{:S(2)}, u32[]{:S(2)}) %collective-permute-start.1) | collective-permute-done | bytes 196640 | tf_op jit(solution)/shard_map/ppermute | solution.py:17
  33.0 11.7 %all-to-all-start.1 = ((f32[64,8,128]{2,1,0:T(8,128)}), f32[64,8,128]{2,1,0:T(8,128)S(1)}, u32[]{:S(2)}, u32[]{:S(2)}) async-start(f32[64,8,128]{2,1,0:T(8,128)} %maximum_maximum_fusion), calls=%async_computation.1 | async-start | bytes 524288 | tf_op jit(solution)/shard_map/all_to_all | solution.py:282
  45.5 84.2 %all-gather.3.cloned.1.call-done = bf16[64,256,512]{2,1,0:T(8,128)(2,1)} async-done(((bf16[1,256,512]{2,1,0:T(8,128)(2,1)}), bf16[64,256,512]{2,1,0:T(8,128)(2,1)}) %all-gather.3.cloned.1.call-update) | async-done | bytes 16777232 | tf_op jit(solution)/shard_map/all_gather | solution.py:261
  129.7 5.8 %copy-done.5 = bf16[64,256,512]{2,1,0:T(8,128)(2,1)S(1)} copy-done((bf16[64,256,512]{2,1,0:T(8,128)(2,1)S(1)}, bf16[64,256,512]{2,1,0:T(8,128)(2,1)}, u32[]{:S(2)}) %copy-start.5) | copy-done | bytes 16777240
  135.5 5.3 %project.4 = (bf16[128,3072]{1,0:T(8,128)(2,1)S(1)}, bf16[512,128]{1,0:T(8,128)(2,1)}) custom-call(bf16[128,2048]{1,0:T(8,128)(2,1)S(1)} %dynamic-slice_bitcast_fusion.x_ref, bf16[2,32,256,512]{3,2,1,0:T(8,128)(2,1)S(1)} %bitcast.65, f32[128,16]{1,0:T(8,128)S(1)} %get-tuple-element.42.scale_ref), custom_call_target="tpu_custom_call" | custom-call | flops 1610612736 | bytes 12582912 | tf_op jit(solution)/shard_map/project/pallas_call | solution.py:76
  140.8 8.3 %all-to-all-start = ((bf16[64,8,128]{2,1,0:T(8,128)(2,1)}), bf16[64,8,128]{2,1,0:T(8,128)(2,1)S(1)}, u32[]{:S(2)}, u32[]{:S(2)}) async-start(bf16[64,8,128]{2,1,0:T(8,128)(2,1)} %bitcast.15), calls=%async_computation | async-start | bytes 262144 | tf_op jit(solution)/shard_map/all_to_all | solution.py:302
  149.8 11.3 %all-to-all-done.state_ref = bf16[64,8,128]{2,1,0:T(8,128)(2,1)S(1)} async-done(((bf16[64,8,128]{2,1,0:T(8,128)(2,1)}), bf16[64,8,128]{2,1,0:T(8,128)(2,1)S(1)}, u32[]{:S(2)}, u32[]{:S(2)}) %all-to-all-start) | async-done | bytes 131104 | tf_op jit(solution)/shard_map/all_to_all | solution.py:302
  163.4 6.2 %all-to-all-start.2 = ((bf16[64,8,128]{2,1,0:T(8,128)(2,1)}), bf16[64,8,128]{2,1,0:T(8,128)(2,1)S(1)}, u32[]{:S(2)}, u32[]{:S(2)}) async-start(bf16[64,8,128]{2,1,0:T(8,128)(2,1)} %carry.4), calls=%async_computation.2 | async-start | bytes 262144 | tf_op jit(solution)/shard_map/all_to_all | solution.py:305
  171.8 9.2 %all-to-all-done.2 = bf16[64,8,128]{2,1,0:T(8,128)(2,1)S(1)} async-done(((bf16[64,8,128]{2,1,0:T(8,128)(2,1)}), bf16[64,8,128]{2,1,0:T(8,128)(2,1)S(1)}, u32[]{:S(2)}, u32[]{:S(2)}) %all-to-all-start.2) | async-done | bytes 131104 | tf_op jit(solution)/shard_map/all_to_all | solution.py:305
  181.7 5.9 %copy-done.6 = bf16[64,256,512]{2,1,0:T(8,128)(2,1)S(1)} copy-done((bf16[64,256,512]{2,1,0:T(8,128)(2,1)S(1)}, bf16[64,256,512]{2,1,0:T(8,128)(2,1)}, u32[]{:S(2)}) %copy-start.6) | copy-done | bytes 16777240
  192.2 37.6 %all-gather.5.cloned.1.call-done = bf16[64,256,512]{2,1,0:T(8,128)(2,1)} async-done(((bf16[1,256,512]{2,1,0:T(8,128)(2,1)}), bf16[64,256,512]{2,1,0:T(8,128)(2,1)}) %all-gather.5.cloned.1.call-update) | async-done | bytes 16777232 | tf_op jit(solution)/shard_map/all_gather | solution.py:261
  229.9 5.8 %copy-done.1 = bf16[64,256,512]{2,1,0:T(8,128)(2,1)S(1)} copy-done((bf16[64,256,512]{2,1,0:T(8,128)(2,1)S(1)}, bf16[64,256,512]{2,1,0:T(8,128)(2,1)}, u32[]{:S(2)}) %copy-start.1) | copy-done | bytes 16777240
  236.5 4.6 %project.5 = (bf16[128,3072]{1,0:T(8,128)(2,1)S(1)}, bf16[512,128]{1,0:T(8,128)(2,1)S(1)}) custom-call(bf16[128,2048]{1,0:T(8,128)(2,1)S(1)} %output.4.x_ref, bf16[2,32,256,512]{3,2,1,0:T(8,128)(2,1)S(1)} %bitcast.61, f32[128,16]{1,0:T(8,128)S(1)} %copy-done.21), custom_call_target="tpu_custom_call" | custom-call | flops 1610612736 | bytes 12582912 | tf_op jit(solution)/shard_map/project/pallas_call | solution.py:76
  241.1 19.9 %all_to_all.45.state_ref = bf16[64,8,128]{2,1,0:T(8,128)(2,1)} all-to-all(bf16[64,8,128]{2,1,0:T(8,128)(2,1)S(1)} %bitcast.77), channel_id=1, replica_groups=mesh['ylo'=2,'core'=2,'yhi'=2,'x'=4,'z'=8] {'yhi','x','z'}, dimensions={0} | all-to-all | bytes 262144 | tf_op jit(solution)/shard_map/all_to_all | solution.py:302
  262.7 4.8 %all-to-all-start.4 = ((bf16[64,8,128]{2,1,0:T(8,128)(2,1)}), bf16[64,8,128]{2,1,0:T(8,128)(2,1)S(1)}, u32[]{:S(2)}, u32[]{:S(2)}) async-start(bf16[64,8,128]{2,1,0:T(8,128)(2,1)} %carry.5), calls=%async_computation.4 | async-start | bytes 262144 | tf_op jit(solution)/shard_map/all_to_all | solution.py:305
  268.9 10.1 %all-to-all-done.4 = bf16[64,8,128]{2,1,0:T(8,128)(2,1)S(1)} async-done(((bf16[64,8,128]{2,1,0:T(8,128)(2,1)}), bf16[64,8,128]{2,1,0:T(8,128)(2,1)S(1)}, u32[]{:S(2)}, u32[]{:S(2)}) %all-to-all-start.4) | async-done | bytes 131104 | tf_op jit(solution)/shard_map/all_to_all | solution.py:305
  279.7 5.8 %copy-done.2 = bf16[64,256,512]{2,1,0:T(8,128)(2,1)S(1)} copy-done((bf16[64,256,512]{2,1,0:T(8,128)(2,1)S(1)}, bf16[64,256,512]{2,1,0:T(8,128)(2,1)}, u32[]{:S(2)}) %copy-start.2) | copy-done | bytes 16777240
  292.4 8.4 %collective-permute-done.5.x_ref = bf16[128,2048]{1,0:T(8,128)(2,1)S(1)} collective-permute-done((bf16[128,2048]{1,0:T(8,128)(2,1)S(1)}, bf16[128,2048]{1,0:T(8,128)(2,1)S(1)}, u32[]{:S(2)}, u32[]{:S(2)}) %collective-permute-start.5) | collective-permute-done | bytes 524320 | tf_op jit(solution)/shard_map/ppermute | solution.py:300
  300.7 5.8 %copy-done.7 = bf16[64,256,512]{2,1,0:T(8,128)(2,1)S(1)} copy-done((bf16[64,256,512]{2,1,0:T(8,128)(2,1)S(1)}, bf16[64,256,512]{2,1,0:T(8,128)(2,1)}, u32[]{:S(2)}) %copy-start.7) | copy-done | bytes 16777240
  307.3 4.6 %project.6 = (bf16[128,3072]{1,0:T(8,128)(2,1)S(1)}, bf16[512,128]{1,0:T(8,128)(2,1)S(1)}) custom-call(bf16[128,2048]{1,0:T(8,128)(2,1)S(1)} %collective-permute-done.5.x_ref, bf16[2,32,256,512]{3,2,1,0:T(8,128)(2,1)S(1)} %bitcast.67, f32[128,16]{1,0:T(8,128)S(1)} %copy-done.20), custom_call_target="tpu_custom_call" | custom-call | flops 1610612736 | bytes 12582912 | tf_op jit(solution)/shard_map/project/pallas_call | solution.py:76
  312.0 16.4 %all_to_all.46.state_ref = bf16[64,8,128]{2,1,0:T(8,128)(2,1)} all-to-all(bf16[64,8,128]{2,1,0:T(8,128)(2,1)S(1)} %bitcast.75), channel_id=1, replica_groups=mesh['ylo'=2,'core'=2,'yhi'=2,'x'=4,'z'=8] {'yhi','x','z'}, dimensions={0} | all-to-all | bytes 262144 | tf_op jit(solution)/shard_map/all_to_all | solution.py:302
  330.1 5.7 %all-to-all-start.6 = ((bf16[64,8,128]{2,1,0:T(8,128)(2,1)}), bf16[64,8,128]{2,1,0:T(8,128)(2,1)}, u32[]{:S(2)}, u32[]{:S(2)}) async-start(bf16[64,8,128]{2,1,0:T(8,128)(2,1)} %carry.6), calls=%async_computation.6 | async-start | bytes 262144 | tf_op jit(solution)/shard_map/all_to_all | solution.py:305
  338.0 8.8 %all-to-all-done.6 = bf16[64,8,128]{2,1,0:T(8,128)(2,1)} async-done(((bf16[64,8,128]{2,1,0:T(8,128)(2,1)}), bf16[64,8,128]{2,1,0:T(8,128)(2,1)}, u32[]{:S(2)}, u32[]{:S(2)}) %all-to-all-start.6) | async-done | bytes 131104 | tf_op jit(solution)/shard_map/all_to_all | solution.py:305
  346.8 5.8 %copy-done.8 = bf16[64,256,512]{2,1,0:T(8,128)(2,1)S(1)} copy-done((bf16[64,256,512]{2,1,0:T(8,128)(2,1)S(1)}, bf16[64,256,512]{2,1,0:T(8,128)(2,1)}, u32[]{:S(2)}) %copy-start.8) | copy-done | bytes 16777240
  359.3 5.8 %copy-done.3 = bf16[64,256,512]{2,1,0:T(8,128)(2,1)S(1)} copy-done((bf16[64,256,512]{2,1,0:T(8,128)(2,1)S(1)}, bf16[64,256,512]{2,1,0:T(8,128)(2,1)}, u32[]{:S(2)}) %copy-start.3) | copy-done | bytes 16777240
  365.0 4.6 %project.7 = (bf16[128,3072]{1,0:T(8,128)(2,1)S(1)}, bf16[512,128]{1,0:T(8,128)(2,1)S(1)}) custom-call(bf16[128,2048]{1,0:T(8,128)(2,1)S(1)} %output.6.x_ref, bf16[2,32,256,512]{3,2,1,0:T(8,128)(2,1)S(1)} %bitcast.63, f32[128,16]{1,0:T(8,128)S(1)} %copy-done.22), custom_call_target="tpu_custom_call" | custom-call | flops 1610612736 | bytes 12582912 | tf_op jit(solution)/shard_map/project/pallas_call | solution.py:76
  369.7 16.0 %all_to_all.47.state_ref = bf16[64,8,128]{2,1,0:T(8,128)(2,1)} all-to-all(bf16[64,8,128]{2,1,0:T(8,128)(2,1)S(1)} %bitcast.76), channel_id=1, replica_groups=mesh['ylo'=2,'core'=2,'yhi'=2,'x'=4,'z'=8] {'yhi','x','z'}, dimensions={0} | all-to-all | bytes 262144 | tf_op jit(solution)/shard_map/all_to_all | solution.py:302
  387.4 5.5 %all-to-all-start.8 = ((bf16[64,8,128]{2,1,0:T(8,128)(2,1)}), bf16[64,8,128]{2,1,0:T(8,128)(2,1)}, u32[]{:S(2)}, u32[]{:S(2)}) async-start(bf16[64,8,128]{2,1,0:T(8,128)(2,1)} %carry.7), calls=%async_computation.8 | async-start | bytes 262144 | tf_op jit(solution)/shard_map/all_to_all | solution.py:305
  395.0 9.1 %all-to-all-done.8 = bf16[64,8,128]{2,1,0:T(8,128)(2,1)} async-done(((bf16[64,8,128]{2,1,0:T(8,128)(2,1)}), bf16[64,8,128]{2,1,0:T(8,128)(2,1)}, u32[]{:S(2)}, u32[]{:S(2)}) %all-to-all-start.8) | async-done | bytes 131104 | tf_op jit(solution)/shard_map/all_to_all | solution.py:305
  404.2 5.8 %copy-done.4 = bf16[64,256,512]{2,1,0:T(8,128)(2,1)S(1)} copy-done((bf16[64,256,512]{2,1,0:T(8,128)(2,1)S(1)}, bf16[64,256,512]{2,1,0:T(8,128)(2,1)}, u32[]{:S(2)}) %copy-start.4) | copy-done | bytes 16777240
  411.0 3.8 output.7
  414.9 8.6 %collective-permute-start.6 = (bf16[128,2048]{1,0:T(8,128)(2,1)S(1)}, bf16[128,2048]{1,0:T(8,128)(2,1)S(1)}, u32[]{:S(2)}, u32[]{:S(2)}) collective-permute-start(bf16[128,2048]{1,0:T(8,128)(2,1)S(1)} %broadcast_select_fusion.2), channel_id=1, source_target_pairs={{0,64},{64,0},{1,65},{65,1},{2,66},{66,2},{3,67},{67,3},{4,68},{68... | collective-permute-start | bytes 1572872 | tf_op jit(solution)/shard_map/ppermute | solution.py:17
  (120 shorter events, 61.8 us)
Async XLA Ops:
  6.5 38.1 %copy-start = (bf16[2,128,2048]{2,1,0:T(8,128)(2,1)S(1)}, bf16[2,128,2048]{2,1,0:T(8,128)(2,1)}, u32[]{:S(2)}) copy-start(bf16[2,128,2048]{2,1,0:T(8,128)(2,1)} %param.4) | copy-start | bytes 3145732
  6.5 123.2 %all-gather.3.cloned.1.call-start = ((), (), s32[]{:S(2)}) async-start(), calls=%async_computation.9 | async-start | bytes 17039360 | tf_op jit(solution)/shard_map/all_gather | solution.py:261
  7.4 4.3 collective-permute-start.2
  11.6 2.3 collective-permute-start
  12.6 4.7 %collective-permute-start.3 = (bf16[2,2,16,512]{3,2,1,0:T(8,128)(2,1)S(1)}, bf16[2,2,16,512]{3,2,1,0:T(8,128)(2,1)S(1)}, u32[]{:S(2)}, u32[]{:S(2)}) collective-permute-start(bf16[2,2,16,512]{3,2,1,0:T(8,128)(2,1)S(1)} %maximum_bitcast_fusion.2), channel_id=1, source_target_pairs={{0,32},{32,0},{1,33},{33,1},{2,34},{34,2},{3,35},{35,3},{4,36},{36... | collective-permute-start | bytes 196616 | tf_op jit(solution)/shard_map/ppermute | solution.py:17
  15.2 8.7 %collective-permute-start.1 = (bf16[2,3,32,512]{3,1,2,0:T(4,128)(2,1)S(1)}, bf16[2,3,32,512]{3,1,2,0:T(4,128)(2,1)S(1)}, u32[]{:S(2)}, u32[]{:S(2)}) collective-permute-start(bf16[2,3,32,512]{3,1,2,0:T(4,128)(2,1)S(1)} %maximum_bitcast_fusion.1), channel_id=1, source_target_pairs={{0,32},{32,0},{1,33},{33,1},{2,34},{34,2},{3,35},{35,3},{4,36},{36... | collective-permute-start | bytes 589832 | tf_op jit(solution)/shard_map/ppermute | solution.py:17
  25.5 204.4 %all-gather.5.cloned.1.call-start = ((), (), s32[]{:S(2)}) async-start(), calls=%async_computation.10 | async-start | bytes 17039360 | tf_op jit(solution)/shard_map/all_gather | solution.py:261
  27.0 2.5 collective-permute-start.4
  33.0 107.8 %all-to-all-start.1 = ((f32[64,8,128]{2,1,0:T(8,128)}), f32[64,8,128]{2,1,0:T(8,128)S(1)}, u32[]{:S(2)}, u32[]{:S(2)}) async-start(f32[64,8,128]{2,1,0:T(8,128)} %maximum_maximum_fusion), calls=%async_computation.1 | async-start | bytes 524288 | tf_op jit(solution)/shard_map/all_to_all | solution.py:282
  45.5 136.2 %copy-start.19 = (f32[128,16]{1,0:T(8,128)}, f32[128,16]{1,0:T(8,128)S(1)}, u32[]{:S(2)}) copy-start(f32[128,16]{1,0:T(8,128)S(1)} %get-tuple-element.42.scale_ref) | copy-start | bytes 24580
  129.7 5.8 %copy-start.5 = (bf16[64,256,512]{2,1,0:T(8,128)(2,1)S(1)}, bf16[64,256,512]{2,1,0:T(8,128)(2,1)}, u32[]{:S(2)}) copy-start(bf16[64,256,512]{2,1,0:T(8,128)(2,1)} %all-gather.3.cloned.1.call-done) | copy-start | bytes 50331652
  140.8 20.3 %all-to-all-start = ((bf16[64,8,128]{2,1,0:T(8,128)(2,1)}), bf16[64,8,128]{2,1,0:T(8,128)(2,1)S(1)}, u32[]{:S(2)}, u32[]{:S(2)}) async-start(bf16[64,8,128]{2,1,0:T(8,128)(2,1)} %bitcast.15), calls=%async_computation | async-start | bytes 262144 | tf_op jit(solution)/shard_map/all_to_all | solution.py:302
  163.4 17.6 %all-to-all-start.2 = ((bf16[64,8,128]{2,1,0:T(8,128)(2,1)}), bf16[64,8,128]{2,1,0:T(8,128)(2,1)S(1)}, u32[]{:S(2)}, u32[]{:S(2)}) async-start(bf16[64,8,128]{2,1,0:T(8,128)(2,1)} %carry.4), calls=%async_computation.2 | async-start | bytes 262144 | tf_op jit(solution)/shard_map/all_to_all | solution.py:305
  181.7 5.9 %copy-start.6 = (bf16[64,256,512]{2,1,0:T(8,128)(2,1)S(1)}, bf16[64,256,512]{2,1,0:T(8,128)(2,1)}, u32[]{:S(2)}) copy-start(bf16[64,256,512]{2,1,0:T(8,128)(2,1)} %all-gather.3.cloned.1.call-done) | copy-start | bytes 50331652
  229.9 5.8 %copy-start.1 = (bf16[64,256,512]{2,1,0:T(8,128)(2,1)S(1)}, bf16[64,256,512]{2,1,0:T(8,128)(2,1)}, u32[]{:S(2)}) copy-start(bf16[64,256,512]{2,1,0:T(8,128)(2,1)} %all-gather.5.cloned.1.call-done) | copy-start | bytes 50331652
  262.7 16.3 %all-to-all-start.4 = ((bf16[64,8,128]{2,1,0:T(8,128)(2,1)}), bf16[64,8,128]{2,1,0:T(8,128)(2,1)S(1)}, u32[]{:S(2)}, u32[]{:S(2)}) async-start(bf16[64,8,128]{2,1,0:T(8,128)(2,1)} %carry.5), calls=%async_computation.4 | async-start | bytes 262144 | tf_op jit(solution)/shard_map/all_to_all | solution.py:305
  279.7 5.8 %copy-start.2 = (bf16[64,256,512]{2,1,0:T(8,128)(2,1)S(1)}, bf16[64,256,512]{2,1,0:T(8,128)(2,1)}, u32[]{:S(2)}) copy-start(bf16[64,256,512]{2,1,0:T(8,128)(2,1)} %all-gather.5.cloned.1.call-done) | copy-start | bytes 50331652
  286.3 0.9 copy-start.26
  290.1 10.6 %collective-permute-start.5 = (bf16[128,2048]{1,0:T(8,128)(2,1)S(1)}, bf16[128,2048]{1,0:T(8,128)(2,1)S(1)}, u32[]{:S(2)}, u32[]{:S(2)}) collective-permute-start(bf16[128,2048]{1,0:T(8,128)(2,1)S(1)} %output.5), channel_id=1, source_target_pairs={{0,128},{1,129},{2,130},{3,131},{4,132},{5,133},{6,134},{7,135},{8... | collective-permute-start | bytes 1572872 | tf_op jit(solution)/shard_map/ppermute | solution.py:300
  300.7 5.8 %copy-start.7 = (bf16[64,256,512]{2,1,0:T(8,128)(2,1)S(1)}, bf16[64,256,512]{2,1,0:T(8,128)(2,1)}, u32[]{:S(2)}) copy-start(bf16[64,256,512]{2,1,0:T(8,128)(2,1)} %all-gather.3.cloned.1.call-done) | copy-start | bytes 50331652
  307.3 39.4 %copy-start.9 = (bf16[128,2048]{1,0:T(8,128)(2,1)}, bf16[128,2048]{1,0:T(8,128)(2,1)S(1)}, u32[]{:S(2)}) copy-start(bf16[128,2048]{1,0:T(8,128)(2,1)S(1)} %collective-permute-done.5.x_ref) | copy-start | bytes 1572868
  330.1 16.7 %all-to-all-start.6 = ((bf16[64,8,128]{2,1,0:T(8,128)(2,1)}), bf16[64,8,128]{2,1,0:T(8,128)(2,1)}, u32[]{:S(2)}, u32[]{:S(2)}) async-start(bf16[64,8,128]{2,1,0:T(8,128)(2,1)} %carry.6), calls=%async_computation.6 | async-start | bytes 262144 | tf_op jit(solution)/shard_map/all_to_all | solution.py:305
  346.8 5.8 %copy-start.8 = (bf16[64,256,512]{2,1,0:T(8,128)(2,1)S(1)}, bf16[64,256,512]{2,1,0:T(8,128)(2,1)}, u32[]{:S(2)}) copy-start(bf16[64,256,512]{2,1,0:T(8,128)(2,1)} %all-gather.3.cloned.1.call-done) | copy-start | bytes 50331652
  352.6 1.0 copy-start.10
  353.6 1.0 copy-start.12
  355.5 3.8 copy-start.22
  355.5 48.7 %copy-start.16 = (f32[128,16]{1,0:T(8,128)S(1)}, f32[128,16]{1,0:T(8,128)}, u32[]{:S(2)}) copy-start(f32[128,16]{1,0:T(8,128)} %get-tuple-element.39.grow_ref) | copy-start | bytes 24580
  359.3 5.8 %copy-start.3 = (bf16[64,256,512]{2,1,0:T(8,128)(2,1)S(1)}, bf16[64,256,512]{2,1,0:T(8,128)(2,1)}, u32[]{:S(2)}) copy-start(bf16[64,256,512]{2,1,0:T(8,128)(2,1)} %all-gather.5.cloned.1.call-done) | copy-start | bytes 50331652
  387.4 16.8 %all-to-all-start.8 = ((bf16[64,8,128]{2,1,0:T(8,128)(2,1)}), bf16[64,8,128]{2,1,0:T(8,128)(2,1)}, u32[]{:S(2)}, u32[]{:S(2)}) async-start(bf16[64,8,128]{2,1,0:T(8,128)(2,1)} %carry.7), calls=%async_computation.8 | async-start | bytes 262144 | tf_op jit(solution)/shard_map/all_to_all | solution.py:305
  404.2 5.8 %copy-start.4 = (bf16[64,256,512]{2,1,0:T(8,128)(2,1)S(1)}, bf16[64,256,512]{2,1,0:T(8,128)(2,1)}, u32[]{:S(2)}) copy-start(bf16[64,256,512]{2,1,0:T(8,128)(2,1)} %all-gather.5.cloned.1.call-done) | copy-start | bytes 50331652
  410.0 1.0 copy-start.14
  414.9 10.1 %collective-permute-start.6 = (bf16[128,2048]{1,0:T(8,128)(2,1)S(1)}, bf16[128,2048]{1,0:T(8,128)(2,1)S(1)}, u32[]{:S(2)}, u32[]{:S(2)}) collective-permute-start(bf16[128,2048]{1,0:T(8,128)(2,1)S(1)} %broadcast_select_fusion.2), channel_id=1, source_target_pairs={{0,64},{64,0},{1,65},{65,1},{2,66},{66,2},{3,67},{67,3},{4,68},{68... | collective-permute-start | bytes 1572872 | tf_op jit(solution)/shard_map/ppermute | solution.py:17
  (11 other events, 8.7 us)
Sparse Core Ops, SparseCore 0:
  25.6 104.0 all-gather.2
  132.5 97.3 all-gather.4

commit v2 on v1

v2 whole, which is shorter than its diff:
```python
import functools

import jax
import jax.numpy as jnp
from jax import lax
from jax.experimental import pallas as pl
from jax.experimental.pallas import tpu as pltpu
from jax.sharding import Mesh, PartitionSpec as P

CTX = ("yhi", "x", "z")
SPREAD = ("core", "x", "z")
NB = 512
EPS = 1e-05
VMEM_KEPT = 36 * 2**20


def swap(value, axis):
    return lax.ppermute(value, axis, [(0, 1), (1, 0)])


def half_mask(rows, lanes, half):
    return lax.broadcasted_iota(jnp.int32, (rows, lanes), 1) < half


def by_head(low, table, p):
    return jnp.where(low, table[:, 2 * p : 2 * p + 1], table[:, 2 * p + 1 : 2 * p + 2])


def share_copies(blocks, layer, w_ref, buffer, sems):
    copies = []
    for k, (parts, rows) in enumerate(blocks):
        block, at = [], 0
        for i, (first, column, count) in enumerate(parts):
            for far in range(2):
                block.append(
                    pltpu.make_async_copy(
                        w_ref.at[layer, :, pl.ds(first + far * rows, rows), pl.ds(column, count)],
                        buffer.at[k, far, :, :, pl.ds(at, count)],
                        sems.at[k, 2 * i + far],
                    )
                )
            at += count
        copies.append(block)
    return copies


def start_all(copies):
    for block in copies:
        for copy in block:
            copy.start()


def block_dot(left, copies, buffer, k):
    for copy in copies[k]:
        copy.wait()
    return jnp.dot(left, buffer[k].reshape(left.shape[1], NB), preferred_element_type=jnp.float32)


def keys_kernel(blocks, layer, x_ref, w_ref, table_ref, kv_ref, state_ref, normed_ref, buffer, sems):
    copies = share_copies(blocks, layer, w_ref, buffer, sems)
    start_all(copies)
    rows = x_ref.shape[0]
    inner = kv_ref.shape[1] // 2
    x = x_ref[...].astype(jnp.float32)
    normed = (x * lax.rsqrt(jnp.mean(x * x, axis=-1, keepdims=True) + EPS)).astype(jnp.bfloat16)
    normed_ref[...] = normed
    low = half_mask(rows, 128, 64)
    scale = table_ref[:rows, 16:32]
    half = NB // 2
    for k in range(len(blocks)):
        part = block_dot(normed, copies, buffer, k).astype(jnp.bfloat16)
        kv_ref[:, half * k : half * (k + 1)] = part[:, :half]
        kv_ref[:, inner + half * k : inner + half * (k + 1)] = part[:, half:]
        for c in range(half // 128):
            p = half * k // 128 + c
            keys = part[:, 128 * c : 128 * (c + 1)].astype(jnp.float32) * by_head(low, scale, p)
            outer = lax.dot_general(
                keys.astype(jnp.bfloat16),
                part[:, half + 128 * c : half + 128 * (c + 1)],
                (((0,), (0,)), ((), ())),
                preferred_element_type=jnp.float32,
            )
            state_ref[64 * p : 64 * (p + 1), :] = jnp.where(
                low[:64], outer[:64], outer[64:]
            ).astype(jnp.bfloat16)


def project_keys(x, weights, layer, table):
    rows, width = x.shape
    inner = 1024
    share, half = width // 64, NB // 2
    row = 2 * share
    blocks = [
        ([(row * (2 + g // 2), half * (g % 2), half), (row * (4 + g // 2), half * (g % 2), half)], share)
        for g in range(4)
    ]
    vmem = pl.BlockSpec(memory_space=pltpu.VMEM)
    return pl.pallas_call(
        functools.partial(keys_kernel, blocks, layer),
        in_specs=[vmem, pl.BlockSpec(memory_space=pl.ANY), vmem],
        out_specs=[vmem] * 3,
        out_shape=[
            jax.ShapeDtypeStruct((rows, 2 * inner), jnp.bfloat16),
            jax.ShapeDtypeStruct((inner // 2, 128), jnp.bfloat16),
            jax.ShapeDtypeStruct((rows, width), jnp.bfloat16),
        ],
        scratch_shapes=[
            pltpu.VMEM((len(blocks), 2, 32, share, NB), jnp.bfloat16),
            pltpu.SemaphoreType.DMA((len(blocks), 4)),
        ],
        compiler_params=pltpu.CompilerParams(vmem_limit_bytes=VMEM_KEPT),
        cost_estimate=pl.CostEstimate(
            flops=4 * rows * width * inner, bytes_accessed=4 * width * inner, transcendentals=0
        ),
        name="keys",
    )(x, weights, table)


def within_kernel(blocks, layer, normed_ref, w_ref, kv_ref, table_ref, q_ref, out_ref, buffer, sems):
    copies = share_copies(blocks, layer, w_ref, buffer, sems)
    start_all(copies)
    rows = kv_ref.shape[0]
    inner = kv_ref.shape[1] // 2
    low = half_mask(rows, 128, 64)
    causal = lax.broadcasted_iota(jnp.int32, (rows, rows), 0) >= lax.broadcasted_iota(
        jnp.int32, (rows, rows), 1
    )
    cum = table_ref[:rows, :16]
    cum_t = table_ref[rows:, :]
    zero = jnp.zeros((rows, 128), jnp.bfloat16)
    normed = normed_ref[...]
    for p in range(inner // 128):
        if p % (NB // 128) == 0:
            k = 128 * p // NB
            part = block_dot(normed, copies, buffer, k).astype(jnp.bfloat16)
            q_ref[:, NB * k : NB * (k + 1)] = part
        at = 128 * p % NB
        queries = part[:, at : at + 128]
        keys = kv_ref[:, 128 * p : 128 * (p + 1)]
        values = kv_ref[:, inner + 128 * p : inner + 128 * (p + 1)]
        weights = []
        for k in range(2):
            h = 2 * p + k
            own = jnp.where(low, queries, zero) if k == 0 else jnp.where(low, zero, queries)
            scores = lax.dot_general(
                own, keys, (((1,), (1,)), ((), ())), preferred_element_type=jnp.float32
            )
            gap = cum[:, h : h + 1] - cum_t[h : h + 1, :]
            decay = jnp.exp(jnp.where(causal, gap, 0.0))
            weights.append(jnp.where(causal, scores * decay, 0.0).astype(jnp.bfloat16))
        both = jnp.concatenate(
            [jnp.where(low, values, zero), jnp.where(low, zero, values)], axis=0
        )
        out_ref[:, 128 * p : 128 * (p + 1)] = jnp.dot(
            jnp.concatenate(weights, axis=1), both, preferred_element_type=jnp.float32
        )


def within(normed, weights, layer, kv, table):
    rows, width = normed.shape
    inner = kv.shape[1] // 2
    share = width // 64
    blocks = [([(2 * share * n, 0, NB)], share) for n in range(2)]
    vmem = pl.BlockSpec(memory_space=pltpu.VMEM)
    return pl.pallas_call(
        functools.partial(within_kernel, blocks, layer),
        in_specs=[vmem, pl.BlockSpec(memory_space=pl.ANY), vmem, vmem],
        out_specs=[vmem] * 2,
        out_shape=[
            jax.ShapeDtypeStruct((rows, inner), jnp.bfloat16),
            jax.ShapeDtypeStruct((rows, inner), jnp.float32),
        ],
        scratch_shapes=[
            pltpu.VMEM((len(blocks), 2, 32, share, NB), jnp.bfloat16),
            pltpu.SemaphoreType.DMA((len(blocks), 2)),
        ],
        compiler_params=pltpu.CompilerParams(vmem_limit_bytes=VMEM_KEPT),
        cost_estimate=pl.CostEstimate(
            flops=2 * rows * width * inner + 6 * rows * rows * inner,
            bytes_accessed=2 * width * inner + 16 * rows * inner,
            transcendentals=16 * rows * rows,
        ),
        name="within",
    )(normed, weights, kv, table)


def carry_kernel(layer, state_ref, total_ref, out_ref):
    carried = jnp.zeros(state_ref.shape[1:], jnp.float32)
    for c in range(state_ref.shape[0]):
        out_ref[c] = carried.astype(jnp.bfloat16)
        carried = total_ref[c, layer : layer + 1, :] * carried + state_ref[c].astype(jnp.float32)


def carry(states, totals, layer):
    return pl.pallas_call(
        functools.partial(carry_kernel, layer),
        out_shape=jax.ShapeDtypeStruct(states.shape, jnp.bfloat16),
        compiler_params=pltpu.CompilerParams(vmem_limit_bytes=4 * 2**20),
        cost_estimate=pl.CostEstimate(
            flops=2 * states.size, bytes_accessed=4 * states.size, transcendentals=0
        ),
        name="carry",
    )(states, totals)


def output_kernel(
    blocks, layer, q_ref, carried_ref, table_ref, within_ref, x_ref, w_ref, out_ref, buffer, sems
):
    copies = share_copies(blocks, layer, w_ref, buffer, sems)
    start_all(copies)
    rows, inner = within_ref.shape
    low = half_mask(rows, 128, 64)
    low64 = low[:64]
    zero = jnp.zeros((64, 128), jnp.bfloat16)
    grow = table_ref[:rows, 32:48]
    mixed = []
    for p in range(inner // 128):
        cols = slice(128 * p, 128 * (p + 1))
        state = carried_ref[64 * p : 64 * (p + 1), :]
        both = jnp.concatenate(
            [jnp.where(low64, state, zero), jnp.where(low64, zero, state)], axis=0
        )
        earlier = jnp.dot(q_ref[:, cols], both, preferred_element_type=jnp.float32)
        mixture = within_ref[:, cols] + earlier * by_head(low, grow, p)
        square = mixture * mixture
        first = jnp.sum(jnp.where(low, square, 0.0), axis=-1, keepdims=True)
        second = jnp.sum(jnp.where(low, 0.0, square), axis=-1, keepdims=True)
        scale = jnp.where(
            low, lax.rsqrt(first * (1.0 / 64.0) + EPS), lax.rsqrt(second * (1.0 / 64.0) + EPS)
        )
        mixed.append((mixture * scale).astype(jnp.bfloat16))
    mixed = jnp.concatenate(mixed, axis=1)
    for k in range(len(blocks)):
        cols = slice(NB * k, NB * (k + 1))
        acc = block_dot(mixed, copies, buffer, k)
        out_ref[:, cols] = (x_ref[:, cols].astype(jnp.float32) + acc).astype(jnp.bfloat16)


def output(q, carried, table, inside, x, weights, layer):
    rows, width = x.shape
    inner = inside.shape[1]
    share = inner // 64
    first = 3 * inner // NB * (width // 64) * 2
    blocks = [([(first + 2 * share * n, 0, NB)], share) for n in range(4)]
    vmem = pl.BlockSpec(memory_space=pltpu.VMEM)
    return pl.pallas_call(
        functools.partial(output_kernel, blocks, layer),
        in_specs=[vmem] * 5 + [pl.BlockSpec(memory_space=pl.ANY)],
        out_specs=vmem,
        out_shape=jax.ShapeDtypeStruct((rows, width), jnp.bfloat16),
        scratch_shapes=[
            pltpu.VMEM((len(blocks), 2, 32, share, NB), jnp.bfloat16),
            pltpu.SemaphoreType.DMA((len(blocks), 2)),
        ],
        compiler_params=pltpu.CompilerParams(vmem_limit_bytes=VMEM_KEPT),
        cost_estimate=pl.CostEstimate(
            flops=2 * rows * width * inner, bytes_accessed=2 * width * inner, transcendentals=0
        ),
        name="output",
    )(q, carried, table, inside, x, weights)


def in_blocks(value):
    rows, cols = value.shape
    return jnp.moveaxis(value.reshape(rows, cols // NB, NB), 1, 0)


def shared_weights(qkv, out):
    place = lax.axis_index("yhi")
    flat = []
    for part in (in_blocks(qkv), in_blocks(out)):
        far = swap(part, "yhi")
        pair = [jnp.where(place == 0, part, far), jnp.where(place == 0, far, part)]
        flat.append(jnp.stack(pair, axis=1).reshape(-1, NB))
    own = jnp.concatenate(flat, axis=0)
    gathered = lax.all_gather(own, SPREAD, axis=0)
    return gathered.reshape(2, -1, own.shape[0], NB)


def decays(log_decay, core):
    keep = jnp.where(core == 0, log_decay[0], log_decay[1])
    other = swap(jnp.where(core == 0, log_decay[1], log_decay[0]), "core")
    both = [jnp.where(core == 0, keep, other), jnp.where(core == 0, other, keep)]
    rows, heads = keep.shape
    lower = jnp.tril(jnp.ones((rows, rows), jnp.float32))
    blocks = lax.axis_size(CTX)
    per_pair = blocks // (heads // 2)
    tables, rows_sent = [], []
    for d in both:
        cum = jnp.dot(lower, d, precision=lax.Precision.HIGHEST)
        ending = cum[-1:]
        total = jnp.exp(ending[0])
        lanes = jnp.repeat(total.reshape(heads // 2, 2), 64, axis=1)
        rows_sent.append(jnp.repeat(lanes, per_pair, axis=0))
        wide = jnp.concatenate([cum, jnp.exp(ending - cum), jnp.exp(cum)], axis=1)
        wide = jnp.pad(wide, ((0, 0), (0, rows - wide.shape[1])))
        tables.append(jnp.concatenate([wide, cum.T], axis=0))
    sent = jnp.stack(rows_sent + [jnp.zeros_like(rows_sent[0])] * 6, axis=1)
    return tables, lax.all_to_all(sent, CTX, 0, 0, tiled=True)


def shards(tokens, qkv_weight, out_weight, log_decay):
    core = lax.axis_index("core")
    level = lax.axis_index("ylo")
    blocks = lax.axis_size(CTX)
    x = lax.dynamic_index_in_dim(tokens, core, 0, False)
    weights = shared_weights(qkv_weight[0], out_weight[0])
    tables, totals = decays(log_decay[0], core)
    x, totals, tables = lax.optimization_barrier((x, totals, tables))
    kept = []
    for step in range(4):
        layer = step % 2
        table = tables[layer]
        if step == 2:
            x = lax.ppermute(x, "ylo", [(0, 1)])
        kv, state, normed = project_keys(x, weights, layer, table)
        slices = lax.all_to_all(state.reshape(blocks, -1, 128), CTX, 0, 0, tiled=True)
        q, inside = within(normed, weights, layer, kv, table)
        slices, inside = lax.optimization_barrier((slices, inside))
        mine = carry(slices, totals, layer)
        carried = lax.all_to_all(mine, CTX, 0, 0, tiled=True).reshape(state.shape)
        x = output(q, carried, table, inside, x, weights, layer)
        kept.append(x)
    first = jnp.where(level == 0, kept[0], kept[2])
    second = jnp.where(level == 0, kept[1], kept[3])
    other = swap(jnp.where(core == 0, second, first), "core")
    result = jnp.stack([jnp.where(core == 0, first, other), jnp.where(core == 0, other, second)])
    return result[None]


def solution(mesh):
    fine = Mesh(mesh.devices.reshape(2, 2, 2, 4, 8), ("ylo", "core") + CTX)
    section = ("ylo", "core")
    in_specs = (
        P(None, CTX, None),
        P(section, CTX, None),
        P(section, CTX, None),
        P(section, None, CTX, None),
    )
    return jax.shard_map(
        shards, mesh=fine, in_specs=in_specs, out_specs=P(section, None, CTX, None), check_vma=False
    )
```

time: 435 us -> 388 us (0.89)
  local copies, waits for them, and re-layouts: 61.2 us -> 19.9 us
  Pallas kernels: 44.9 us -> 52.3 us
  waiting for transfers between devices: 188 us -> 181 us
  other arithmetic: 9.49 us -> 4.13 us
    unnamed x56 -> x42, local copies, waits for them, and re-layouts: 58.9 us -> 16.3 us
    all_to_all x4 -> x1, waiting for transfers between devices: 37.3 us -> 11.5 us  [shards(): carried = lax.all_to_all(mine, CTX, 0, 0, tiled=True).reshape(state.shape)]
    all_to_all x1 -> x4, starting transfers between devices: 8.34 us -> 25.2 us  [shards(): lax.all_to_all(state.reshape(blocks, -1, 128), CTX, 0, 0, tiled=True)]
    all_to_all x1, waiting for transfers between devices: 0.01 us -> 16.2 us  [decays(): return (tables, lax.all_to_all(sent, CTX, 0, 0, tiled=True))]
    all_to_all x4 -> x1, starting transfers between devices: 22.2 us -> 7.75 us  [shards(): carried = lax.all_to_all(mine, CTX, 0, 0, tiled=True).reshape(state.shape)]
    all_to_all x1 -> x4, waiting for transfers between devices: 11.3 us -> 22.3 us  [shards(): lax.all_to_all(state.reshape(blocks, -1, 128), CTX, 0, 0, tiled=True)]
    all_gather x2 -> x1, waiting for transfers between devices: 122 us -> 113 us  [shared_weights(): gathered = lax.all_gather(own, SPREAD, axis=0)]
    pallas_call x16, Pallas kernels: 44.9 us -> 52.3 us  [the longest x4 19.1 us: project_keys(): pl.pallas_call(functools.partial(keys_kernel, blocks, layer), in_specs=[v...]
  transfers between devices with their start and end apart: 15 -> 12, of which waited for: 12 -> 12; matrix products, arithmetic and copies ran while one was open for 2% -> 2% of each run, Pallas kernels for 4% -> 4%
where the time goes in v2:
time: 388 us; the launch traced here: 386 us
  waiting for transfers between devices  181 us (47%)
  starting transfers between devices  61.3 us (16%)
  blocking collectives  52.5 us (14%)
  Pallas kernels  52.3 us (13%)
  local copies, waits for them, and re-layouts  19.9 us (5%)
  between operations  13.7 us (4%)
  other arithmetic  4.13 us (1%)
    all_gather x1, waiting for transfers between devices, shared_weights(): gathered = lax.all_gather(own, SPREAD, axis=0)  113 us
    all_to_all x3, blocking collectives, shards(): carried = lax.all_to_all(mine, CTX, 0, 0, tiled=True).reshape(state.shape)  52.5 us
    all_to_all x4, starting transfers between devices, shards(): lax.all_to_all(state.reshape(blocks, -1, 128), CTX, 0, 0, tiled=True)  25.2 us
    all_to_all x4, waiting for transfers between devices, shards(): lax.all_to_all(state.reshape(blocks, -1, 128), CTX, 0, 0, tiled=True)  22.3 us
    pallas_call x4, Pallas kernels, project_keys(): pl.pallas_call(functools.partial(keys_kernel, blocks, layer), in_specs=[v...  19.1 us
    unnamed x42, local copies, waits for them, and re-layouts  16.3 us
    all_to_all x1, waiting for transfers between devices, decays(): return (tables, lax.all_to_all(sent, CTX, 0, 0, tiled=True))  16.2 us
    pallas_call x4, Pallas kernels, within(): pl.pallas_call(functools.partial(within_kernel, blocks, layer), in_specs=...  15.6 us
  transfers between devices with their start and end apart: 12, of which 12 were waited for; matrix products, arithmetic and copies ran while one was open for 2% of the time, Pallas kernels for 4%

profile of v2, /device:TPU:1, one launch (start us, length us, event | category | flops | bytes accessed | tf_op | source)
XLA Modules:
  0.0 386.3 jit_solution(8117997921183446836)
XLA Ops:
  7.5 3.8 collective-permute-start.2
  13.1 7.9 %collective-permute-done.1 = bf16[6,32,512]{2,0,1:T(8,128)(2,1)S(1)} collective-permute-done((bf16[6,32,512]{2,0,1:T(8,128)(2,1)S(1)}, bf16[6,32,512]{2,0,1:T(8,128)(2,1)S(1)}, u32[]{:S(2)}, u32[]{:S(2)}) %collective-permute-start.1) | collective-permute-done | bytes 196640 | tf_op jit(solution)/shard_map/ppermute | solution.py:18
  29.1 11.9 %all-to-all-start = ((f32[64,8,128]{2,1,0:T(8,128)}), f32[64,8,128]{2,1,0:T(8,128)S(1)}, u32[]{:S(2)}, u32[]{:S(2)}) async-start(f32[64,8,128]{2,1,0:T(8,128)} %maximum_maximum_fusion), calls=%async_computation | async-start | bytes 524288 | tf_op jit(solution)/shard_map/all_to_all | solution.py:299
  41.5 16.2 %all-to-all-done.total_ref = f32[64,8,128]{2,1,0:T(8,128)S(1)} async-done(((f32[64,8,128]{2,1,0:T(8,128)}), f32[64,8,128]{2,1,0:T(8,128)S(1)}, u32[]{:S(2)}, u32[]{:S(2)}) %all-to-all-start) | async-done | bytes 262176 | tf_op jit(solution)/shard_map/all_to_all | solution.py:299
  57.6 113.0 %all-gather.3.cloned.1.call-done = bf16[32768,512]{1,0:T(8,128)(2,1)} async-done(((bf16[512,512]{1,0:T(8,128)(2,1)}), bf16[32768,512]{1,0:T(8,128)(2,1)}) %all-gather.3.cloned.1.call-update) | async-done | bytes 33554448 | tf_op jit(solution)/shard_map/all_gather | solution.py:276
  170.6 4.9 %keys.4 = (bf16[128,2048]{1,0:T(8,128)(2,1)S(1)}, bf16[512,128]{1,0:T(8,128)(2,1)}, bf16[128,2048]{1,0:T(8,128)(2,1)S(1)}) custom-call(bf16[128,2048]{1,0:T(8,128)(2,1)S(1)} %dynamic-slice_bitcast_fusion.x_ref, bf16[2,32,512,512]{3,2,1,0:T(8,128)(2,1)} %bitcast.55, f32[144,128]{1,0:T(8,128)S(1)} %get-tuple-element.38.table_ref), custom_call_target="tpu_custom_call" | custom-call | flops 1073741824 | bytes 8388608 | tf_op jit(solution)/shard_map/keys/pallas_call | solution.py:98
  175.6 8.6 %all-to-all-start.1 = ((bf16[64,8,128]{2,1,0:T(8,128)(2,1)}), bf16[64,8,128]{2,1,0:T(8,128)(2,1)}, u32[]{:S(2)}, u32[]{:S(2)}) async-start(bf16[64,8,128]{2,1,0:T(8,128)(2,1)} %bitcast.17), calls=%async_computation.1 | async-start | bytes 262144 | tf_op jit(solution)/shard_map/all_to_all | solution.py:317
  184.2 3.9 %within.4 = (bf16[128,1024]{1,0:T(8,128)(2,1)S(1)}, f32[128,1024]{1,0:T(8,128)S(1)}) custom-call(bf16[128,2048]{1,0:T(8,128)(2,1)S(1)} %get-tuple-element.39.normed_ref, bf16[2,32,512,512]{3,2,1,0:T(8,128)(2,1)} %bitcast.56, bf16[128,2048]{1,0:T(8,128)(2,1)S(1)} %get-tuple-element.40.kv_ref, f32[144,128]{1,0:T(8,128)S(1)} %get-tuple-element.38.table_ref), custom_call_target="tpu_custom_call" | custom-call | flops 637534208 | bytes 6291456 | tf_op jit(solution)/shard_map/within/pallas_call | solution.py:165
  188.8 6.8 %all-to-all-done.1.state_ref = bf16[64,8,128]{2,1,0:T(8,128)(2,1)} async-done(((bf16[64,8,128]{2,1,0:T(8,128)(2,1)}), bf16[64,8,128]{2,1,0:T(8,128)(2,1)}, u32[]{:S(2)}, u32[]{:S(2)}) %all-to-all-start.1) | async-done | bytes 131104 | tf_op jit(solution)/shard_map/all_to_all | solution.py:317
  196.7 16.6 %all_to_all.45 = bf16[64,8,128]{2,1,0:T(8,128)(2,1)S(1)} all-to-all(bf16[64,8,128]{2,1,0:T(8,128)(2,1)S(1)} %carry.4), channel_id=1, replica_groups=mesh['ylo'=2,'core'=2,'yhi'=2,'x'=4,'z'=8] {'yhi','x','z'}, dimensions={0} | all-to-all | bytes 262144 | tf_op jit(solution)/shard_map/all_to_all | solution.py:321
  214.2 3.4 output.4.x_ref
  217.6 5.0 %keys.5 = (bf16[128,2048]{1,0:T(8,128)(2,1)S(1)}, bf16[512,128]{1,0:T(8,128)(2,1)}, bf16[128,2048]{1,0:T(8,128)(2,1)S(1)}) custom-call(bf16[128,2048]{1,0:T(8,128)(2,1)S(1)} %output.4.x_ref, bf16[2,32,512,512]{3,2,1,0:T(8,128)(2,1)} %bitcast.58, f32[144,128]{1,0:T(8,128)S(1)} %get-tuple-element.47.table_ref), custom_call_target="tpu_custom_call" | custom-call | flops 1073741824 | bytes 8388608 | tf_op jit(solution)/shard_map/keys/pallas_call | solution.py:98
  222.6 5.4 %all-to-all-start.3 = ((bf16[64,8,128]{2,1,0:T(8,128)(2,1)}), bf16[64,8,128]{2,1,0:T(8,128)(2,1)}, u32[]{:S(2)}, u32[]{:S(2)}) async-start(bf16[64,8,128]{2,1,0:T(8,128)(2,1)} %bitcast.19), calls=%async_computation.3 | async-start | bytes 262144 | tf_op jit(solution)/shard_map/all_to_all | solution.py:317
  228.0 3.9 %within.5 = (bf16[128,1024]{1,0:T(8,128)(2,1)S(1)}, f32[128,1024]{1,0:T(8,128)S(1)}) custom-call(bf16[128,2048]{1,0:T(8,128)(2,1)S(1)} %get-tuple-element.48.normed_ref, bf16[2,32,512,512]{3,2,1,0:T(8,128)(2,1)} %bitcast.59, bf16[128,2048]{1,0:T(8,128)(2,1)S(1)} %get-tuple-element.49.kv_ref, f32[144,128]{1,0:T(8,128)S(1)} %get-tuple-element.47.table_ref), custom_call_target="tpu_custom_call" | custom-call | flops 637534208 | bytes 6291456 | tf_op jit(solution)/shard_map/within/pallas_call | solution.py:165
  232.6 6.6 %all-to-all-done.3.state_ref = bf16[64,8,128]{2,1,0:T(8,128)(2,1)} async-done(((bf16[64,8,128]{2,1,0:T(8,128)(2,1)}), bf16[64,8,128]{2,1,0:T(8,128)(2,1)}, u32[]{:S(2)}, u32[]{:S(2)}) %all-to-all-start.3) | async-done | bytes 131104 | tf_op jit(solution)/shard_map/all_to_all | solution.py:317
  240.2 16.9 %all_to_all.46 = bf16[64,8,128]{2,1,0:T(8,128)(2,1)S(1)} all-to-all(bf16[64,8,128]{2,1,0:T(8,128)(2,1)S(1)} %carry.5), channel_id=1, replica_groups=mesh['ylo'=2,'core'=2,'yhi'=2,'x'=4,'z'=8] {'yhi','x','z'}, dimensions={0} | all-to-all | bytes 262144 | tf_op jit(solution)/shard_map/all_to_all | solution.py:321
  258.1 3.4 output.5
  263.7 7.2 %collective-permute-done.3.x_ref = bf16[128,2048]{1,0:T(8,128)(2,1)S(1)} collective-permute-done((bf16[128,2048]{1,0:T(8,128)(2,1)S(1)}, bf16[128,2048]{1,0:T(8,128)(2,1)S(1)}, u32[]{:S(2)}, u32[]{:S(2)}) %collective-permute-start.3) | collective-permute-done | bytes 524320 | tf_op jit(solution)/shard_map/ppermute | solution.py:315
  270.9 4.3 %keys.6 = (bf16[128,2048]{1,0:T(8,128)(2,1)S(1)}, bf16[512,128]{1,0:T(8,128)(2,1)S(1)}, bf16[128,2048]{1,0:T(8,128)(2,1)S(1)}) custom-call(bf16[128,2048]{1,0:T(8,128)(2,1)S(1)} %collective-permute-done.3.x_ref, bf16[2,32,512,512]{3,2,1,0:T(8,128)(2,1)} %bitcast.61, f32[144,128]{1,0:T(8,128)S(1)} %get-tuple-element.38.table_ref), custom_call_target="tpu_custom_call" | custom-call | flops 1073741824 | bytes 8388608 | tf_op jit(solution)/shard_map/keys/pallas_call | solution.py:98
  277.5 5.7 %all-to-all-start.5 = ((bf16[64,8,128]{2,1,0:T(8,128)(2,1)}), bf16[64,8,128]{2,1,0:T(8,128)(2,1)}, u32[]{:S(2)}, u32[]{:S(2)}) async-start(bf16[64,8,128]{2,1,0:T(8,128)(2,1)} %bitcast.54), calls=%async_computation.5 | async-start | bytes 262144 | tf_op jit(solution)/shard_map/all_to_all | solution.py:317
  285.3 3.9 %within.6 = (bf16[128,1024]{1,0:T(8,128)(2,1)S(1)}, f32[128,1024]{1,0:T(8,128)S(1)}) custom-call(bf16[128,2048]{1,0:T(8,128)(2,1)S(1)} %copy-done.6, bf16[2,32,512,512]{3,2,1,0:T(8,128)(2,1)} %bitcast.62, bf16[128,2048]{1,0:T(8,128)(2,1)S(1)} %copy-done.4, f32[144,128]{1,0:T(8,128)S(1)} %get-tuple-element.38.table_ref), custom_call_target="tpu_custom_call" | custom-call | flops 637534208 | bytes 6291456 | tf_op jit(solution)/shard_map/within/pallas_call | solution.py:165
  289.9 4.4 %all-to-all-done.5.state_ref = bf16[64,8,128]{2,1,0:T(8,128)(2,1)} async-done(((bf16[64,8,128]{2,1,0:T(8,128)(2,1)}), bf16[64,8,128]{2,1,0:T(8,128)(2,1)}, u32[]{:S(2)}, u32[]{:S(2)}) %all-to-all-start.5) | async-done | bytes 131104 | tf_op jit(solution)/shard_map/all_to_all | solution.py:317
  295.3 19.0 %all_to_all.47 = bf16[64,8,128]{2,1,0:T(8,128)(2,1)S(1)} all-to-all(bf16[64,8,128]{2,1,0:T(8,128)(2,1)S(1)} %carry.6), channel_id=1, replica_groups=mesh['ylo'=2,'core'=2,'yhi'=2,'x'=4,'z'=8] {'yhi','x','z'}, dimensions={0} | all-to-all | bytes 262144 | tf_op jit(solution)/shard_map/all_to_all | solution.py:321
  316.3 3.4 output.6.x_ref
  319.6 5.0 %keys.7 = (bf16[128,2048]{1,0:T(8,128)(2,1)S(1)}, bf16[512,128]{1,0:T(8,128)(2,1)}, bf16[128,2048]{1,0:T(8,128)(2,1)S(1)}) custom-call(bf16[128,2048]{1,0:T(8,128)(2,1)S(1)} %output.6.x_ref, bf16[2,32,512,512]{3,2,1,0:T(8,128)(2,1)} %bitcast.64, f32[144,128]{1,0:T(8,128)S(1)} %get-tuple-element.47.table_ref), custom_call_target="tpu_custom_call" | custom-call | flops 1073741824 | bytes 8388608 | tf_op jit(solution)/shard_map/keys/pallas_call | solution.py:98
  326.2 5.5 %all-to-all-start.7 = ((bf16[64,8,128]{2,1,0:T(8,128)(2,1)}), bf16[64,8,128]{2,1,0:T(8,128)(2,1)}, u32[]{:S(2)}, u32[]{:S(2)}) async-start(bf16[64,8,128]{2,1,0:T(8,128)(2,1)} %bitcast.23), calls=%async_computation.7 | async-start | bytes 262144 | tf_op jit(solution)/shard_map/all_to_all | solution.py:317
  333.8 3.9 %within.7 = (bf16[128,1024]{1,0:T(8,128)(2,1)S(1)}, f32[128,1024]{1,0:T(8,128)S(1)}) custom-call(bf16[128,2048]{1,0:T(8,128)(2,1)S(1)} %copy-done.10, bf16[2,32,512,512]{3,2,1,0:T(8,128)(2,1)} %bitcast.65, bf16[128,2048]{1,0:T(8,128)(2,1)S(1)} %copy-done.8, f32[144,128]{1,0:T(8,128)S(1)} %get-tuple-element.47.table_ref), custom_call_target="tpu_custom_call" | custom-call | flops 637534208 | bytes 6291456 | tf_op jit(solution)/shard_map/within/pallas_call | solution.py:165
  338.4 4.4 %all-to-all-done.7.state_ref = bf16[64,8,128]{2,1,0:T(8,128)(2,1)} async-done(((bf16[64,8,128]{2,1,0:T(8,128)(2,1)}), bf16[64,8,128]{2,1,0:T(8,128)(2,1)}, u32[]{:S(2)}, u32[]{:S(2)}) %all-to-all-start.7) | async-done | bytes 131104 | tf_op jit(solution)/shard_map/all_to_all | solution.py:317
  344.5 7.7 %all-to-all-start.8 = ((bf16[64,8,128]{2,1,0:T(8,128)(2,1)}), bf16[64,8,128]{2,1,0:T(8,128)(2,1)S(1)}, u32[]{:S(2)}, u32[]{:S(2)}) async-start(bf16[64,8,128]{2,1,0:T(8,128)(2,1)} %copy-done.11), calls=%async_computation.8 | async-start | bytes 262144 | tf_op jit(solution)/shard_map/all_to_all | solution.py:321
  352.3 11.5 %all-to-all-done.8 = bf16[64,8,128]{2,1,0:T(8,128)(2,1)S(1)} async-done(((bf16[64,8,128]{2,1,0:T(8,128)(2,1)}), bf16[64,8,128]{2,1,0:T(8,128)(2,1)S(1)}, u32[]{:S(2)}, u32[]{:S(2)}) %all-to-all-start.8) | async-done | bytes 131104 | tf_op jit(solution)/shard_map/all_to_all | solution.py:321
  364.7 3.4 output.7
  368.2 8.4 %collective-permute-start.4 = (bf16[128,2048]{1,0:T(8,128)(2,1)S(1)}, bf16[128,2048]{1,0:T(8,128)(2,1)S(1)}, u32[]{:S(2)}, u32[]{:S(2)}) collective-permute-start(bf16[128,2048]{1,0:T(8,128)(2,1)S(1)} %broadcast_select_fusion.2), channel_id=1, source_target_pairs={{0,64},{64,0},{1,65},{65,1},{2,66},{66,2},{3,67},{67,3},{4,68},{68... | collective-permute-start | bytes 1572872 | tf_op jit(solution)/shard_map/ppermute | solution.py:18
  (92 shorter events, 36.8 us)
Async XLA Ops:
  6.5 18.2 %copy-start = (bf16[2,128,2048]{2,1,0:T(8,128)(2,1)S(1)}, bf16[2,128,2048]{2,1,0:T(8,128)(2,1)}, u32[]{:S(2)}) copy-start(bf16[2,128,2048]{2,1,0:T(8,128)(2,1)} %param.4) | copy-start | bytes 3145732
  6.5 164.1 %all-gather.3.cloned.1.call-start = ((), (), s32[]{:S(2)}) async-start(), calls=%async_computation.9 | async-start | bytes 34078720 | tf_op jit(solution)/shard_map/all_gather | solution.py:276
  7.5 5.5 %collective-permute-start.2 = (bf16[4,16,512]{2,1,0:T(8,128)(2,1)S(1)}, bf16[4,16,512]{2,1,0:T(8,128)(2,1)S(1)}, u32[]{:S(2)}, u32[]{:S(2)}) collective-permute-start(bf16[4,16,512]{2,1,0:T(8,128)(2,1)S(1)} %bitcast.74), channel_id=1, source_target_pairs={{0,32},{32,0},{1,33},{33,1},{2,34},{34,2},{3,35},{35,3},{4,36},{36... | collective-permute-start | bytes 196616 | tf_op jit(solution)/shard_map/ppermute | solution.py:18
  12.5 8.4 %collective-permute-start.1 = (bf16[6,32,512]{2,0,1:T(8,128)(2,1)S(1)}, bf16[6,32,512]{2,0,1:T(8,128)(2,1)S(1)}, u32[]{:S(2)}, u32[]{:S(2)}) collective-permute-start(bf16[6,32,512]{2,0,1:T(8,128)(2,1)S(1)} %bitcast.68), channel_id=1, source_target_pairs={{0,32},{32,0},{1,33},{33,1},{2,34},{34,2},{3,35},{35,3},{4,36},{36... | collective-permute-start | bytes 589832 | tf_op jit(solution)/shard_map/ppermute | solution.py:18
  22.9 2.7 collective-permute-start
  29.1 28.5 %all-to-all-start = ((f32[64,8,128]{2,1,0:T(8,128)}), f32[64,8,128]{2,1,0:T(8,128)S(1)}, u32[]{:S(2)}, u32[]{:S(2)}) async-start(f32[64,8,128]{2,1,0:T(8,128)} %maximum_maximum_fusion), calls=%async_computation | async-start | bytes 524288 | tf_op jit(solution)/shard_map/all_to_all | solution.py:299
  175.6 20.1 %all-to-all-start.1 = ((bf16[64,8,128]{2,1,0:T(8,128)(2,1)}), bf16[64,8,128]{2,1,0:T(8,128)(2,1)}, u32[]{:S(2)}, u32[]{:S(2)}) async-start(bf16[64,8,128]{2,1,0:T(8,128)(2,1)} %bitcast.17), calls=%async_computation.1 | async-start | bytes 262144 | tf_op jit(solution)/shard_map/all_to_all | solution.py:317
  188.1 0.7 copy-start.16
  213.3 1.0 copy-start.17
  222.6 16.6 %all-to-all-start.3 = ((bf16[64,8,128]{2,1,0:T(8,128)(2,1)}), bf16[64,8,128]{2,1,0:T(8,128)(2,1)}, u32[]{:S(2)}, u32[]{:S(2)}) async-start(bf16[64,8,128]{2,1,0:T(8,128)(2,1)} %bitcast.19), calls=%async_computation.3 | async-start | bytes 262144 | tf_op jit(solution)/shard_map/all_to_all | solution.py:317
  231.9 0.7 copy-start.18
  257.2 1.0 copy-start.19
  261.5 9.4 %collective-permute-start.3 = (bf16[128,2048]{1,0:T(8,128)(2,1)S(1)}, bf16[128,2048]{1,0:T(8,128)(2,1)S(1)}, u32[]{:S(2)}, u32[]{:S(2)}) collective-permute-start(bf16[128,2048]{1,0:T(8,128)(2,1)S(1)} %output.5), channel_id=1, source_target_pairs={{0,128},{1,129},{2,130},{3,131},{4,132},{5,133},{6,134},{7,135},{8... | collective-permute-start | bytes 1572872 | tf_op jit(solution)/shard_map/ppermute | solution.py:315
  275.2 0.8 copy-start.3
  276.0 0.8 copy-start.5
  277.5 16.8 %all-to-all-start.5 = ((bf16[64,8,128]{2,1,0:T(8,128)(2,1)}), bf16[64,8,128]{2,1,0:T(8,128)(2,1)}, u32[]{:S(2)}, u32[]{:S(2)}) async-start(bf16[64,8,128]{2,1,0:T(8,128)(2,1)} %bitcast.54), calls=%async_computation.5 | async-start | bytes 262144 | tf_op jit(solution)/shard_map/all_to_all | solution.py:317
  283.2 1.0 copy-start.4
  284.2 1.0 copy-start.6
  289.2 0.7 copy-start.14
  289.9 24.4 %copy-start.1 = (f32[128,1024]{1,0:T(8,128)}, f32[128,1024]{1,0:T(8,128)S(1)}, u32[]{:S(2)}) copy-start(f32[128,1024]{1,0:T(8,128)S(1)} %get-tuple-element.61.within_ref) | copy-start | bytes 1572868
  314.3 1.0 copy-start.2
  315.3 0.9 copy-start.15
  324.6 0.8 copy-start.7
  325.4 0.8 copy-start.9
  326.2 16.6 %all-to-all-start.7 = ((bf16[64,8,128]{2,1,0:T(8,128)(2,1)}), bf16[64,8,128]{2,1,0:T(8,128)(2,1)}, u32[]{:S(2)}, u32[]{:S(2)}) async-start(bf16[64,8,128]{2,1,0:T(8,128)(2,1)} %bitcast.23), calls=%async_computation.7 | async-start | bytes 262144 | tf_op jit(solution)/shard_map/all_to_all | solution.py:317
  331.7 1.0 copy-start.8
  332.7 1.0 copy-start.10
  337.7 0.7 copy-start.12
  343.9 0.7 copy-start.11
  344.5 19.2 %all-to-all-start.8 = ((bf16[64,8,128]{2,1,0:T(8,128)(2,1)}), bf16[64,8,128]{2,1,0:T(8,128)(2,1)S(1)}, u32[]{:S(2)}, u32[]{:S(2)}) async-start(bf16[64,8,128]{2,1,0:T(8,128)(2,1)} %copy-done.11), calls=%async_computation.8 | async-start | bytes 262144 | tf_op jit(solution)/shard_map/all_to_all | solution.py:321
  363.8 1.0 copy-start.13
  368.2 9.9 %collective-permute-start.4 = (bf16[128,2048]{1,0:T(8,128)(2,1)S(1)}, bf16[128,2048]{1,0:T(8,128)(2,1)S(1)}, u32[]{:S(2)}, u32[]{:S(2)}) collective-permute-start(bf16[128,2048]{1,0:T(8,128)(2,1)S(1)} %broadcast_select_fusion.2), channel_id=1, source_target_pairs={{0,64},{64,0},{1,65},{65,1},{2,66},{66,2},{3,67},{67,3},{4,68},{68... | collective-permute-start | bytes 1572872 | tf_op jit(solution)/shard_map/ppermute | solution.py:18
  (1 other events, 0.6 us)
Sparse Core Ops, SparseCore 0:
  22.2 148.3 all-gather.2

commit v3 on v2

--- a/solution.py
+++ b/solution.py
@@ -11,7 +11,7 @@
 SPREAD = ("core", "x", "z")
 NB = 512
 EPS = 1e-05
-VMEM_KEPT = 36 * 2**20
+VMEM_KEPT = 50 * 2**20
 
 
 def swap(value, axis):
@@ -26,19 +26,16 @@
     return jnp.where(low, table[:, 2 * p : 2 * p + 1], table[:, 2 * p + 1 : 2 * p + 2])
 
 
-def share_copies(blocks, layer, w_ref, buffer, sems):
+def share_copies(blocks, w_ref, buffer, sems):
     copies = []
-    for k, (parts, rows) in enumerate(blocks):
+    stride = w_ref.shape[2] // 2
+    for k, (rows, parts) in enumerate(blocks):
         block, at = [], 0
-        for i, (first, column, count) in enumerate(parts):
+        for side, first, column, count in parts:
             for far in range(2):
-                block.append(
-                    pltpu.make_async_copy(
-                        w_ref.at[layer, :, pl.ds(first + far * rows, rows), pl.ds(column, count)],
-                        buffer.at[k, far, :, :, pl.ds(at, count)],
-                        sems.at[k, 2 * i + far],
-                    )
-                )
+                source = w_ref.at[side, :, pl.ds(far * stride + first, rows), pl.ds(column, count)]
+                goal = buffer.at[k, far, :, :, pl.ds(at, count)]
+                block.append(pltpu.make_async_copy(source, goal, sems.at[k, len(block)]))
             at += count
         copies.append(block)
     return copies
@@ -56,14 +53,17 @@
     return jnp.dot(left, buffer[k].reshape(left.shape[1], NB), preferred_element_type=jnp.float32)
 
 
-def keys_kernel(blocks, layer, x_ref, w_ref, table_ref, kv_ref, state_ref, normed_ref, buffer, sems):
-    copies = share_copies(blocks, layer, w_ref, buffer, sems)
+def normalized(x_ref):
+    x = x_ref[...].astype(jnp.float32)
+    return (x * lax.rsqrt(jnp.mean(x * x, axis=-1, keepdims=True) + EPS)).astype(jnp.bfloat16)
+
+
+def keys_kernel(blocks, x_ref, w_ref, table_ref, kv_ref, state_ref, buffer, sems):
+    copies = share_copies(blocks, w_ref, buffer, sems)
     start_all(copies)
     rows = x_ref.shape[0]
     inner = kv_ref.shape[1] // 2
-    x = x_ref[...].astype(jnp.float32)
-    normed = (x * lax.rsqrt(jnp.mean(x * x, axis=-1, keepdims=True) + EPS)).astype(jnp.bfloat16)
-    normed_ref[...] = normed
+    normed = normalized(x_ref)
     low = half_mask(rows, 128, 64)
     scale = table_ref[:rows, 16:32]
     half = NB // 2
@@ -85,24 +85,24 @@
             ).astype(jnp.bfloat16)
 
 
-def project_keys(x, weights, layer, table):
+def project_keys(x, weights, table):
     rows, width = x.shape
     inner = 1024
-    share, half = width // 64, NB // 2
-    row = 2 * share
+    share = width // 64
+    half = NB // 2
     blocks = [
-        ([(row * (2 + g // 2), half * (g % 2), half), (row * (4 + g // 2), half * (g % 2), half)], share)
-        for g in range(4)
+        (share, [(side, share * part, half * i, half) for part in (1, 2)])
+        for side in range(2)
+        for i in range(2)
     ]
     vmem = pl.BlockSpec(memory_space=pltpu.VMEM)
     return pl.pallas_call(
-        functools.partial(keys_kernel, blocks, layer),
+        functools.partial(keys_kernel, blocks),
         in_specs=[vmem, pl.BlockSpec(memory_space=pl.ANY), vmem],
-        out_specs=[vmem] * 3,
+        out_specs=[vmem] * 2,
         out_shape=[
             jax.ShapeDtypeStruct((rows, 2 * inner), jnp.bfloat16),
             jax.ShapeDtypeStruct((inner // 2, 128), jnp.bfloat16),
-            jax.ShapeDtypeStruct((rows, width), jnp.bfloat16),
         ],
         scratch_shapes=[
             pltpu.VMEM((len(blocks), 2, 32, share, NB), jnp.bfloat16),
@@ -116,8 +116,8 @@
     )(x, weights, table)
 
 
-def within_kernel(blocks, layer, normed_ref, w_ref, kv_ref, table_ref, q_ref, out_ref, buffer, sems):
-    copies = share_copies(blocks, layer, w_ref, buffer, sems)
+def within_kernel(blocks, x_ref, w_ref, kv_ref, table_ref, q_ref, out_ref, buffer, sems):
+    copies = share_copies(blocks, w_ref, buffer, sems)
     start_all(copies)
     rows = kv_ref.shape[0]
     inner = kv_ref.shape[1] // 2
@@ -128,7 +128,7 @@
     cum = table_ref[:rows, :16]
     cum_t = table_ref[rows:, :]
     zero = jnp.zeros((rows, 128), jnp.bfloat16)
-    normed = normed_ref[...]
+    normed = normalized(x_ref)
     for p in range(inner // 128):
         if p % (NB // 128) == 0:
             k = 128 * p // NB
@@ -156,14 +156,14 @@
         )
 
 
-def within(normed, weights, layer, kv, table):
-    rows, width = normed.shape
+def within(x, weights, kv, table):
+    rows, width = x.shape
     inner = kv.shape[1] // 2
     share = width // 64
-    blocks = [([(2 * share * n, 0, NB)], share) for n in range(2)]
+    blocks = [(share, [(side, 0, 0, NB)]) for side in range(2)]
     vmem = pl.BlockSpec(memory_space=pltpu.VMEM)
     return pl.pallas_call(
-        functools.partial(within_kernel, blocks, layer),
+        functools.partial(within_kernel, blocks),
         in_specs=[vmem, pl.BlockSpec(memory_space=pl.ANY), vmem, vmem],
         out_specs=[vmem] * 2,
         out_shape=[
@@ -181,19 +181,19 @@
             transcendentals=16 * rows * rows,
         ),
         name="within",
-    )(normed, weights, kv, table)
-
-
-def carry_kernel(layer, state_ref, total_ref, out_ref):
+    )(x, weights, kv, table)
+
+
+def carry_kernel(state_ref, total_ref, out_ref):
     carried = jnp.zeros(state_ref.shape[1:], jnp.float32)
     for c in range(state_ref.shape[0]):
         out_ref[c] = carried.astype(jnp.bfloat16)
-        carried = total_ref[c, layer : layer + 1, :] * carried + state_ref[c].astype(jnp.float32)
-
-
-def carry(states, totals, layer):
+        carried = total_ref[c : c + 1, :] * carried + state_ref[c].astype(jnp.float32)
+
+
+def carry(states, totals):
     return pl.pallas_call(
-        functools.partial(carry_kernel, layer),
+        carry_kernel,
         out_shape=jax.ShapeDtypeStruct(states.shape, jnp.bfloat16),
         compiler_params=pltpu.CompilerParams(vmem_limit_bytes=4 * 2**20),
         cost_estimate=pl.CostEstimate(
@@ -204,9 +204,9 @@
 
 
 def output_kernel(
-    blocks, layer, q_ref, carried_ref, table_ref, within_ref, x_ref, w_ref, out_ref, buffer, sems
+    blocks, q_ref, carried_ref, table_ref, within_ref, x_ref, w_ref, out_ref, buffer, sems
 ):
-    copies = share_copies(blocks, layer, w_ref, buffer, sems)
+    copies = share_copies(blocks, w_ref, buffer, sems)
     start_all(copies)
     rows, inner = within_ref.shape
     low = half_mask(rows, 128, 64)
@@ -236,15 +236,15 @@
         out_ref[:, cols] = (x_ref[:, cols].astype(jnp.float32) + acc).astype(jnp.bfloat16)
 
 
-def output(q, carried, table, inside, x, weights, layer):
+def output(q, carried, table, inside, x, weights):
     rows, width = x.shape
     inner = inside.shape[1]
     share = inner // 64
-    first = 3 * inner // NB * (width // 64) * 2
-    blocks = [([(first + 2 * share * n, 0, NB)], share) for n in range(4)]
+    first = 3 * (width // 64)
+    blocks = [(share, [(n // 2, first + share * (n % 2), 0, NB)]) for n in range(4)]
     vmem = pl.BlockSpec(memory_space=pltpu.VMEM)
     return pl.pallas_call(
-        functools.partial(output_kernel, blocks, layer),
+        functools.partial(output_kernel, blocks),
         in_specs=[vmem] * 5 + [pl.BlockSpec(memory_space=pl.ANY)],
         out_specs=vmem,
         out_shape=jax.ShapeDtypeStruct((rows, width), jnp.bfloat16),
@@ -260,28 +260,48 @@
     )(q, carried, table, inside, x, weights)
 
 
-def in_blocks(value):
-    rows, cols = value.shape
-    return jnp.moveaxis(value.reshape(rows, cols // NB, NB), 1, 0)
-
-
-def shared_weights(qkv, out):
+def paired(low, high, core):
+    keep = jnp.where(core == 0, low, high)
+    other = swap(jnp.where(core == 0, high, low), "core")
+    return jnp.where(core == 0, keep, other), jnp.where(core == 0, other, keep)
+
+
+def across(value, axes):
+    flip = [(0, 3), (1, 2), (2, 1), (3, 0)] if len(axes) == 2 else [(0, 1), (1, 0)]
+    return lax.ppermute(value, axes, flip)
+
+
+def shared_weights(qkv, out, core, level):
+    rows, depth = qkv.shape[0], out.shape[0]
+    inner = qkv.shape[1] // 3
+    halves = []
+    for side in range(2):
+        cut = [qkv[:, inner * i + NB * side : inner * i + NB * (side + 1)] for i in range(3)]
+        first = out.shape[1] // 2 * side
+        cut += [out[:, first + NB * i : first + NB * (i + 1)] for i in range(2)]
+        halves.append(jnp.concatenate(cut, axis=0))
+    first, second = paired(halves[0], halves[1], core)
+    stay = jnp.where(level == 0, first, second)
+    leave = jnp.where(level == 0, second, first)
+    far = across(stay, ("yhi",))
+    come, come_far = across(leave, ("ylo",)), across(leave, ("ylo", "yhi"))
     place = lax.axis_index("yhi")
-    flat = []
-    for part in (in_blocks(qkv), in_blocks(out)):
-        far = swap(part, "yhi")
-        pair = [jnp.where(place == 0, part, far), jnp.where(place == 0, far, part)]
-        flat.append(jnp.stack(pair, axis=1).reshape(-1, NB))
-    own = jnp.concatenate(flat, axis=0)
-    gathered = lax.all_gather(own, SPREAD, axis=0)
-    return gathered.reshape(2, -1, own.shape[0], NB)
-
-
-def decays(log_decay, core):
-    keep = jnp.where(core == 0, log_decay[0], log_decay[1])
-    other = swap(jnp.where(core == 0, log_decay[1], log_decay[0]), "core")
-    both = [jnp.where(core == 0, keep, other), jnp.where(core == 0, other, keep)]
-    rows, heads = keep.shape
+    gathered = []
+    for layer in range(2):
+        staying = level == layer
+        pair = jnp.where(staying, stay, come), jnp.where(staying, far, come_far)
+        own = jnp.concatenate(
+            [jnp.where(place == 0, pair[0], pair[1]), jnp.where(place == 0, pair[1], pair[0])], axis=0
+        )
+        gathered.append(lax.all_gather(own, SPREAD, axis=0).reshape(2, -1, own.shape[0], NB))
+    return gathered
+
+
+def decays(log_decay, core, level):
+    first, second = paired(log_decay[0], log_decay[1], core)
+    come = across(jnp.where(level == 0, second, first), ("ylo",))
+    both = [jnp.where(level == 0, first, come), jnp.where(level == 0, come, second)]
+    rows, heads = first.shape
     lower = jnp.tril(jnp.ones((rows, rows), jnp.float32))
     blocks = lax.axis_size(CTX)
     per_pair = blocks // (heads // 2)
@@ -296,7 +316,8 @@
         wide = jnp.pad(wide, ((0, 0), (0, rows - wide.shape[1])))
         tables.append(jnp.concatenate([wide, cum.T], axis=0))
     sent = jnp.stack(rows_sent + [jnp.zeros_like(rows_sent[0])] * 6, axis=1)
-    return tables, lax.all_to_all(sent, CTX, 0, 0, tiled=True)
+    received = lax.all_to_all(sent, CTX, 0, 0, tiled=True)
+    return tables, [received[:, k, :] for k in range(2)]
 
 
 def shards(tokens, qkv_weight, out_weight, log_decay):
@@ -304,25 +325,26 @@
     level = lax.axis_index("ylo")
     blocks = lax.axis_size(CTX)
     x = lax.dynamic_index_in_dim(tokens, core, 0, False)
-    weights = shared_weights(qkv_weight[0], out_weight[0])
-    tables, totals = decays(log_decay[0], core)
+    weights = shared_weights(qkv_weight[0], out_weight[0], core, level)
+    tables, totals = decays(log_decay[0], core, level)
     x, totals, tables = lax.optimization_barrier((x, totals, tables))
     kept = []
     for step in range(4):
-        layer = step % 2
-        table = tables[layer]
-        if step == 2:
-            x = lax.ppermute(x, "ylo", [(0, 1)])
-        kv, state, normed = project_keys(x, weights, layer, table)
+        layer = step // 2
+        table, w = tables[layer], weights[layer]
+        if step > 0:
+            x = lax.ppermute(x, "ylo", [(1 - step % 2, step % 2)])
+            kept.append(x)
+        kv, state = project_keys(x, w, table)
         slices = lax.all_to_all(state.reshape(blocks, -1, 128), CTX, 0, 0, tiled=True)
-        q, inside = within(normed, weights, layer, kv, table)
+        q, inside = within(x, w, kv, table)
         slices, inside = lax.optimization_barrier((slices, inside))
-        mine = carry(slices, totals, layer)
+        mine = carry(slices, totals[layer])
         carried = lax.all_to_all(mine, CTX, 0, 0, tiled=True).reshape(state.shape)
-        x = output(q, carried, table, inside, x, weights, layer)
+        x = output(q, carried, table, inside, x, w)
         kept.append(x)
-    first = jnp.where(level == 0, kept[0], kept[2])
-    second = jnp.where(level == 0, kept[1], kept[3])
+    first = jnp.where(level == 0, kept[0], kept[5])
+    second = jnp.where(level == 0, kept[3], kept[6])
     other = swap(jnp.where(core == 0, second, first), "core")
     result = jnp.stack([jnp.where(core == 0, first, other), jnp.where(core == 0, other, second)])
     return result[None]

time: 388 us -> 362 us (0.933)
  waiting for transfers between devices: 181 us -> 144 us
  blocking collectives: 52.5 us -> 69.7 us
  local copies, waits for them, and re-layouts: 19.9 us -> 14.9 us
    all_gather x1 -> x2, waiting for transfers between devices: 113 us -> 64.5 us  [shared_weights(): lax.all_gather(own, SPREAD, axis=0).reshape(2, -1, own.shape[0], NB)]
    ppermute x1 -> x7, waiting for transfers between devices: 7.17 us -> 32.7 us  [the longest x3 24.2 us: shards(): x = lax.ppermute(x, 'ylo', [(1 - step % 2, step % 2)])]
    all_to_all x3 -> x4, blocking collectives: 52.5 us -> 69.7 us  [shards(): carried = lax.all_to_all(mine, CTX, 0, 0, tiled=True).reshape(state.shape)]
    all_to_all x2 -> x1, waiting for transfers between devices: 27.6 us -> 15.7 us  [decays(): received = lax.all_to_all(sent, CTX, 0, 0, tiled=True)]
    all_to_all x2 -> x1, starting transfers between devices: 19.7 us -> 12.6 us  [decays(): received = lax.all_to_all(sent, CTX, 0, 0, tiled=True)]
    ppermute x4 -> x3, waiting for transfers between devices: 10.5 us -> 3.35 us  [swap(): return lax.ppermute(value, axis, [(0, 1), (1, 0)])]
    all_to_all x4, waiting for transfers between devices: 22.3 us -> 28.2 us  [shards(): lax.all_to_all(state.reshape(blocks, -1, 128), CTX, 0, 0, tiled=True)]
    ppermute x1 -> x7, starting transfers between devices: 2.25 us -> 8.11 us  [the longest x3 4.76 us: shards(): x = lax.ppermute(x, 'ylo', [(1 - step % 2, step % 2)])]
  transfers between devices with their start and end apart: 12 -> 17, of which waited for: 12 -> 16; matrix products, arithmetic and copies ran while one was open for 2% -> 2% of each run, Pallas kernels for 4% -> 9%
where the time goes in v3:
time: 362 us; the launch traced here: 360 us
  waiting for transfers between devices  144 us (40%)
  blocking collectives  69.7 us (19%)
  starting transfers between devices  59.5 us (16%)
  Pallas kernels  51 us (14%)
  local copies, waits for them, and re-layouts  14.9 us (4%)
  between operations  13.7 us (4%)
  other arithmetic  5.31 us (1%)
    all_to_all x4, blocking collectives, shards(): carried = lax.all_to_all(mine, CTX, 0, 0, tiled=True).reshape(state.shape)  69.7 us
    all_gather x2, waiting for transfers between devices, shared_weights(): lax.all_gather(own, SPREAD, axis=0).reshape(2, -1, own.shape[0], NB)  64.5 us
    all_to_all x4, waiting for transfers between devices, shards(): lax.all_to_all(state.reshape(blocks, -1, 128), CTX, 0, 0, tiled=True)  28.2 us
    all_to_all x4, starting transfers between devices, shards(): lax.all_to_all(state.reshape(blocks, -1, 128), CTX, 0, 0, tiled=True)  25.7 us
    ppermute x3, waiting for transfers between devices, shards(): x = lax.ppermute(x, 'ylo', [(1 - step % 2, step % 2)])  24.2 us
    pallas_call x4, Pallas kernels, project_keys(): pl.pallas_call(functools.partial(keys_kernel, blocks), in_specs=[vmem, pl...  20 us
    pallas_call x4, Pallas kernels, within(): pl.pallas_call(functools.partial(within_kernel, blocks), in_specs=[vmem,...  16.1 us
    all_to_all x1, waiting for transfers between devices, decays(): received = lax.all_to_all(sent, CTX, 0, 0, tiled=True)  15.7 us
  transfers between devices with their start and end apart: 17, of which 16 were waited for; matrix products, arithmetic and copies ran while one was open for 2% of the time, Pallas kernels for 9%

profile of v3, /device:TPU:1, one launch (start us, length us, event | category | flops | bytes accessed | tf_op | source)
XLA Modules:
  0.0 360.5 jit_solution(10397697263656510444)
XLA Ops:
  10.5 3.3 collective-permute-start.2
  35.1 12.6 %all-to-all-start = ((f32[64,8,128]{2,1,0:T(8,128)}), f32[64,8,128]{2,1,0:T(8,128)S(1)}, u32[]{:S(2)}, u32[]{:S(2)}) async-start(f32[64,8,128]{2,1,0:T(8,128)} %maximum_maximum_fusion), calls=%async_computation | async-start | bytes 524288 | tf_op jit(solution)/shard_map/all_to_all | solution.py:319
  48.0 15.7 %all-to-all-done = f32[64,8,128]{2,1,0:T(8,128)S(1)} async-done(((f32[64,8,128]{2,1,0:T(8,128)}), f32[64,8,128]{2,1,0:T(8,128)S(1)}, u32[]{:S(2)}, u32[]{:S(2)}) %all-to-all-start) | async-done | bytes 262176 | tf_op jit(solution)/shard_map/all_to_all | solution.py:319
  63.8 64.5 %all-gather.5.cloned.1.call-done = bf16[16384,512]{1,0:T(8,128)(2,1)} async-done(((bf16[256,512]{1,0:T(8,128)(2,1)}), bf16[16384,512]{1,0:T(8,128)(2,1)}) %all-gather.5.cloned.1.call-update) | async-done | bytes 16777232 | tf_op jit(solution)/shard_map/all_gather | solution.py:296
  128.3 4.9 %keys.4 = (bf16[128,2048]{1,0:T(8,128)(2,1)S(1)}, bf16[512,128]{1,0:T(8,128)(2,1)}) custom-call(bf16[128,2048]{1,0:T(8,128)(2,1)S(1)} %dynamic-slice_bitcast_fusion.x_ref, bf16[2,32,256,512]{3,2,1,0:T(8,128)(2,1)} %bitcast.59, f32[144,128]{1,0:T(8,128)S(1)} %get-tuple-element.35.table_ref), custom_call_target="tpu_custom_call" | custom-call | flops 1073741824 | bytes 8388608 | tf_op jit(solution)/shard_map/keys/pallas_call | solution.py:99
  133.2 8.4 %all-to-all-start.1 = ((bf16[64,8,128]{2,1,0:T(8,128)(2,1)}), bf16[64,8,128]{2,1,0:T(8,128)(2,1)S(1)}, u32[]{:S(2)}, u32[]{:S(2)}) async-start(bf16[64,8,128]{2,1,0:T(8,128)(2,1)} %bitcast.12), calls=%async_computation.1 | async-start | bytes 262144 | tf_op jit(solution)/shard_map/all_to_all | solution.py:339
  141.6 4.0 %within.4 = (bf16[128,1024]{1,0:T(8,128)(2,1)S(1)}, f32[128,1024]{1,0:T(8,128)S(1)}) custom-call(bf16[128,2048]{1,0:T(8,128)(2,1)S(1)} %dynamic-slice_bitcast_fusion.x_ref, bf16[2,32,256,512]{3,2,1,0:T(8,128)(2,1)} %bitcast.60, bf16[128,2048]{1,0:T(8,128)(2,1)S(1)} %get-tuple-element.36.kv_ref, f32[144,128]{1,0:T(8,128)S(1)} %get-tuple-element.35.table_ref), custom_call_target="tpu_custom_call" | custom-call | flops 637534208 | bytes 6291456 | tf_op jit(solution)/shard_map/within/pallas_call | solution.py:165
  145.6 9.1 %all-to-all-done.1.state_ref = bf16[64,8,128]{2,1,0:T(8,128)(2,1)S(1)} async-done(((bf16[64,8,128]{2,1,0:T(8,128)(2,1)}), bf16[64,8,128]{2,1,0:T(8,128)(2,1)S(1)}, u32[]{:S(2)}, u32[]{:S(2)}) %all-to-all-start.1) | async-done | bytes 131104 | tf_op jit(solution)/shard_map/all_to_all | solution.py:339
  154.9 17.2 %all_to_all.45 = bf16[64,8,128]{2,1,0:T(8,128)(2,1)S(1)} all-to-all(bf16[64,8,128]{2,1,0:T(8,128)(2,1)S(1)} %carry.4), channel_id=1, replica_groups=mesh['ylo'=2,'core'=2,'yhi'=2,'x'=4,'z'=8] {'yhi','x','z'}, dimensions={0} | all-to-all | bytes 262144 | tf_op jit(solution)/shard_map/all_to_all | solution.py:343
  173.0 3.4 output.4
  178.6 8.5 %collective-permute-done.6.x_ref = bf16[128,2048]{1,0:T(8,128)(2,1)S(1)} collective-permute-done((bf16[128,2048]{1,0:T(8,128)(2,1)S(1)}, bf16[128,2048]{1,0:T(8,128)(2,1)S(1)}, u32[]{:S(2)}, u32[]{:S(2)}) %collective-permute-start.6) | collective-permute-done | bytes 524320 | tf_op jit(solution)/shard_map/ppermute | solution.py:336
  187.1 5.2 %keys.5 = (bf16[128,2048]{1,0:T(8,128)(2,1)S(1)}, bf16[512,128]{1,0:T(8,128)(2,1)}) custom-call(bf16[128,2048]{1,0:T(8,128)(2,1)S(1)} %collective-permute-done.6.x_ref, bf16[2,32,256,512]{3,2,1,0:T(8,128)(2,1)} %bitcast.62, f32[144,128]{1,0:T(8,128)S(1)} %get-tuple-element.35.table_ref), custom_call_target="tpu_custom_call" | custom-call | flops 1073741824 | bytes 8388608 | tf_op jit(solution)/shard_map/keys/pallas_call | solution.py:99
  193.1 7.0 %all-to-all-start.3 = ((bf16[64,8,128]{2,1,0:T(8,128)(2,1)}), bf16[64,8,128]{2,1,0:T(8,128)(2,1)S(1)}, u32[]{:S(2)}, u32[]{:S(2)}) async-start(bf16[64,8,128]{2,1,0:T(8,128)(2,1)} %bitcast.14), calls=%async_computation.3 | async-start | bytes 262144 | tf_op jit(solution)/shard_map/all_to_all | solution.py:339
  201.1 4.2 %within.5 = (bf16[128,1024]{1,0:T(8,128)(2,1)S(1)}, f32[128,1024]{1,0:T(8,128)S(1)}) custom-call(bf16[128,2048]{1,0:T(8,128)(2,1)S(1)} %collective-permute-done.6.x_ref, bf16[2,32,256,512]{3,2,1,0:T(8,128)(2,1)} %bitcast.63, bf16[128,2048]{1,0:T(8,128)(2,1)S(1)} %copy-done.2, f32[144,128]{1,0:T(8,128)S(1)} %get-tuple-element.35.table_ref), custom_call_target="tpu_custom_call" | custom-call | flops 637534208 | bytes 6291456 | tf_op jit(solution)/shard_map/within/pallas_call | solution.py:165
  206.0 6.7 %all-to-all-done.3.state_ref = bf16[64,8,128]{2,1,0:T(8,128)(2,1)S(1)} async-done(((bf16[64,8,128]{2,1,0:T(8,128)(2,1)}), bf16[64,8,128]{2,1,0:T(8,128)(2,1)S(1)}, u32[]{:S(2)}, u32[]{:S(2)}) %all-to-all-start.3) | async-done | bytes 131104 | tf_op jit(solution)/shard_map/all_to_all | solution.py:339
  212.8 17.9 %all_to_all.46 = bf16[64,8,128]{2,1,0:T(8,128)(2,1)S(1)} all-to-all(bf16[64,8,128]{2,1,0:T(8,128)(2,1)S(1)} %carry.5), channel_id=1, replica_groups=mesh['ylo'=2,'core'=2,'yhi'=2,'x'=4,'z'=8] {'yhi','x','z'}, dimensions={0} | all-to-all | bytes 262144 | tf_op jit(solution)/shard_map/all_to_all | solution.py:343
  231.7 4.3 %output.5 = bf16[128,2048]{1,0:T(8,128)(2,1)} custom-call(bf16[128,1024]{1,0:T(8,128)(2,1)S(1)} %copy-done.6, bf16[512,128]{1,0:T(8,128)(2,1)S(1)} %bitcast.45, f32[144,128]{1,0:T(8,128)S(1)} %get-tuple-element.35.table_ref, f32[128,1024]{1,0:T(8,128)S(1)} %get-tuple-element.48.within_ref, bf16[128,2048]{1,0:T(8,128)(2,1)S(1)} %collective-permute-done.6.x_ref, ...), custom_call_target="tpu_custom_call" | custom-call | flops 536870912 | bytes 4194304 | tf_op jit(solution)/shard_map/output/pallas_call | solution.py:246
  237.4 9.6 %collective-permute-done.7.x_ref = bf16[128,2048]{1,0:T(8,128)(2,1)S(1)} collective-permute-done((bf16[128,2048]{1,0:T(8,128)(2,1)}, bf16[128,2048]{1,0:T(8,128)(2,1)S(1)}, u32[]{:S(2)}, u32[]{:S(2)}) %collective-permute-start.7) | collective-permute-done | bytes 524320 | tf_op jit(solution)/shard_map/ppermute | solution.py:336
  247.0 4.9 %keys.6 = (bf16[128,2048]{1,0:T(8,128)(2,1)S(1)}, bf16[512,128]{1,0:T(8,128)(2,1)}) custom-call(bf16[128,2048]{1,0:T(8,128)(2,1)S(1)} %collective-permute-done.7.x_ref, bf16[2,32,256,512]{3,2,1,0:T(8,128)(2,1)} %bitcast.53, f32[144,128]{1,0:T(8,128)S(1)} %get-tuple-element.49.table_ref), custom_call_target="tpu_custom_call" | custom-call | flops 1073741824 | bytes 8388608 | tf_op jit(solution)/shard_map/keys/pallas_call | solution.py:99
  251.9 5.8 %all-to-all-start.5 = ((bf16[64,8,128]{2,1,0:T(8,128)(2,1)}), bf16[64,8,128]{2,1,0:T(8,128)(2,1)S(1)}, u32[]{:S(2)}, u32[]{:S(2)}) async-start(bf16[64,8,128]{2,1,0:T(8,128)(2,1)} %bitcast.17), calls=%async_computation.5 | async-start | bytes 262144 | tf_op jit(solution)/shard_map/all_to_all | solution.py:339
  257.7 4.0 %within.6 = (bf16[128,1024]{1,0:T(8,128)(2,1)S(1)}, f32[128,1024]{1,0:T(8,128)S(1)}) custom-call(bf16[128,2048]{1,0:T(8,128)(2,1)S(1)} %collective-permute-done.7.x_ref, bf16[2,32,256,512]{3,2,1,0:T(8,128)(2,1)} %bitcast.54, bf16[128,2048]{1,0:T(8,128)(2,1)S(1)} %get-tuple-element.50.kv_ref, f32[144,128]{1,0:T(8,128)S(1)} %get-tuple-element.49.table_ref), custom_call_target="tpu_custom_call" | custom-call | flops 637534208 | bytes 6291456 | tf_op jit(solution)/shard_map/within/pallas_call | solution.py:165
  262.4 6.6 %all-to-all-done.5.state_ref = bf16[64,8,128]{2,1,0:T(8,128)(2,1)S(1)} async-done(((bf16[64,8,128]{2,1,0:T(8,128)(2,1)}), bf16[64,8,128]{2,1,0:T(8,128)(2,1)S(1)}, u32[]{:S(2)}, u32[]{:S(2)}) %all-to-all-start.5) | async-done | bytes 131104 | tf_op jit(solution)/shard_map/all_to_all | solution.py:339
  269.1 16.8 %all_to_all.47 = bf16[64,8,128]{2,1,0:T(8,128)(2,1)S(1)} all-to-all(bf16[64,8,128]{2,1,0:T(8,128)(2,1)S(1)} %carry.6), channel_id=1, replica_groups=mesh['ylo'=2,'core'=2,'yhi'=2,'x'=4,'z'=8] {'yhi','x','z'}, dimensions={0} | all-to-all | bytes 262144 | tf_op jit(solution)/shard_map/all_to_all | solution.py:343
  286.8 3.4 output.6
  291.5 6.1 %collective-permute-done.8.x_ref = bf16[128,2048]{1,0:T(8,128)(2,1)S(1)} collective-permute-done((bf16[128,2048]{1,0:T(8,128)(2,1)S(1)}, bf16[128,2048]{1,0:T(8,128)(2,1)S(1)}, u32[]{:S(2)}, u32[]{:S(2)}) %collective-permute-start.8) | collective-permute-done | bytes 524320 | tf_op jit(solution)/shard_map/ppermute | solution.py:336
  297.6 4.9 %keys.7 = (bf16[128,2048]{1,0:T(8,128)(2,1)S(1)}, bf16[512,128]{1,0:T(8,128)(2,1)}) custom-call(bf16[128,2048]{1,0:T(8,128)(2,1)S(1)} %collective-permute-done.8.x_ref, bf16[2,32,256,512]{3,2,1,0:T(8,128)(2,1)} %bitcast.56, f32[144,128]{1,0:T(8,128)S(1)} %get-tuple-element.49.table_ref), custom_call_target="tpu_custom_call" | custom-call | flops 1073741824 | bytes 8388608 | tf_op jit(solution)/shard_map/keys/pallas_call | solution.py:99
  303.3 4.6 %all-to-all-start.7 = ((bf16[64,8,128]{2,1,0:T(8,128)(2,1)}), bf16[64,8,128]{2,1,0:T(8,128)(2,1)S(1)}, u32[]{:S(2)}, u32[]{:S(2)}) async-start(bf16[64,8,128]{2,1,0:T(8,128)(2,1)} %bitcast.19), calls=%async_computation.7 | async-start | bytes 262144 | tf_op jit(solution)/shard_map/all_to_all | solution.py:339
  309.0 4.0 %within.7 = (bf16[128,1024]{1,0:T(8,128)(2,1)S(1)}, f32[128,1024]{1,0:T(8,128)S(1)}) custom-call(bf16[128,2048]{1,0:T(8,128)(2,1)S(1)} %collective-permute-done.8.x_ref, bf16[2,32,256,512]{3,2,1,0:T(8,128)(2,1)} %bitcast.57, bf16[128,2048]{1,0:T(8,128)(2,1)S(1)} %copy-done.4, f32[144,128]{1,0:T(8,128)S(1)} %get-tuple-element.49.table_ref), custom_call_target="tpu_custom_call" | custom-call | flops 637534208 | bytes 6291456 | tf_op jit(solution)/shard_map/within/pallas_call | solution.py:165
  313.7 5.8 %all-to-all-done.7.state_ref = bf16[64,8,128]{2,1,0:T(8,128)(2,1)S(1)} async-done(((bf16[64,8,128]{2,1,0:T(8,128)(2,1)}), bf16[64,8,128]{2,1,0:T(8,128)(2,1)S(1)}, u32[]{:S(2)}, u32[]{:S(2)}) %all-to-all-start.7) | async-done | bytes 131104 | tf_op jit(solution)/shard_map/all_to_all | solution.py:339
  319.6 17.8 %all_to_all.48 = bf16[64,8,128]{2,1,0:T(8,128)(2,1)S(1)} all-to-all(bf16[64,8,128]{2,1,0:T(8,128)(2,1)S(1)} %carry.7), channel_id=1, replica_groups=mesh['ylo'=2,'core'=2,'yhi'=2,'x'=4,'z'=8] {'yhi','x','z'}, dimensions={0} | all-to-all | bytes 262144 | tf_op jit(solution)/shard_map/all_to_all | solution.py:343
  338.3 3.4 output.7
  341.8 9.1 %collective-permute-start.9 = (bf16[128,2048]{1,0:T(8,128)(2,1)S(1)}, bf16[128,2048]{1,0:T(8,128)(2,1)S(1)}, u32[]{:S(2)}, u32[]{:S(2)}) collective-permute-start(bf16[128,2048]{1,0:T(8,128)(2,1)S(1)} %broadcast_select_fusion.2), channel_id=1, source_target_pairs={{0,64},{64,0},{1,65},{65,1},{2,66},{66,2},{3,67},{67,3},{4,68},{68... | collective-permute-start | bytes 1572872 | tf_op jit(solution)/shard_map/ppermute | solution.py:18
  (92 shorter events, 43.3 us)
Async XLA Ops:
  6.5 22.5 %copy-start = (bf16[2,128,2048]{2,1,0:T(8,128)(2,1)S(1)}, bf16[2,128,2048]{2,1,0:T(8,128)(2,1)}, u32[]{:S(2)}) copy-start(bf16[2,128,2048]{2,1,0:T(8,128)(2,1)} %param.4) | copy-start | bytes 3145732
  6.5 121.8 %all-gather.5.cloned.1.call-start = ((), (), s32[]{:S(2)}) async-start(), calls=%async_computation.9 | async-start | bytes 17039360 | tf_op jit(solution)/shard_map/all_gather | solution.py:296
  10.5 4.3 %collective-permute-start.2 = (bf16[128,512]{1,0:T(8,128)(2,1)S(1)}, bf16[128,512]{1,0:T(8,128)(2,1)S(1)}, u32[]{:S(2)}, u32[]{:S(2)}) collective-permute-start(bf16[128,512]{1,0:T(8,128)(2,1)S(1)} %broadcast_select_fusion.7), channel_id=1, source_target_pairs={{0,64},{64,0},{1,65},{65,1},{2,66},{66,2},{3,67},{67,3},{4,68},{68... | collective-permute-start | bytes 393224 | tf_op jit(solution)/shard_map/ppermute | solution.py:18
  14.8 6.3 %collective-permute-start.4 = (bf16[128,512]{1,0:T(8,128)(2,1)S(1)}, bf16[128,512]{1,0:T(8,128)(2,1)S(1)}, u32[]{:S(2)}, u32[]{:S(2)}) collective-permute-start(bf16[128,512]{1,0:T(8,128)(2,1)S(1)} %broadcast_select_fusion.12), channel_id=1, source_target_pairs={{0,32},{32,0},{1,33},{33,1},{2,34},{34,2},{3,35},{35,3},{4,36},{36... | collective-permute-start | bytes 393224 | tf_op jit(solution)/shard_map/ppermute | solution.py:271
  16.1 6.5 %collective-permute-start.3 = (bf16[128,512]{1,0:T(8,128)(2,1)S(1)}, bf16[128,512]{1,0:T(8,128)(2,1)S(1)}, u32[]{:S(2)}, u32[]{:S(2)}) collective-permute-start(bf16[128,512]{1,0:T(8,128)(2,1)S(1)} %get-tuple-element.67), channel_id=1, source_target_pairs={{0,128},{128,0},{1,129},{129,1},{2,130},{130,2},{3,131},{131,3},{4... | collective-permute-start | bytes 393224 | tf_op jit(solution)/shard_map/ppermute | solution.py:271
  16.5 7.9 %collective-permute-start.5 = (bf16[128,512]{1,0:T(8,128)(2,1)S(1)}, bf16[128,512]{1,0:T(8,128)(2,1)S(1)}, u32[]{:S(2)}, u32[]{:S(2)}) collective-permute-start(bf16[128,512]{1,0:T(8,128)(2,1)S(1)} %get-tuple-element.67), channel_id=1, source_target_pairs={{0,160},{32,128},{128,32},{160,0},{1,161},{33,129},{129,33},{161,1... | collective-permute-start | bytes 393224 | tf_op jit(solution)/shard_map/ppermute | solution.py:271
  25.2 212.1 %all-gather.7.cloned.1.call-start = ((), (), s32[]{:S(2)}) async-start(), calls=%async_computation.10 | async-start | bytes 17039360 | tf_op jit(solution)/shard_map/all_gather | solution.py:296
  26.8 1.5 collective-permute-start
  29.0 2.5 collective-permute-start.1
  35.1 28.7 %all-to-all-start = ((f32[64,8,128]{2,1,0:T(8,128)}), f32[64,8,128]{2,1,0:T(8,128)S(1)}, u32[]{:S(2)}, u32[]{:S(2)}) async-start(f32[64,8,128]{2,1,0:T(8,128)} %maximum_maximum_fusion), calls=%async_computation | async-start | bytes 524288 | tf_op jit(solution)/shard_map/all_to_all | solution.py:319
  133.2 21.5 %all-to-all-start.1 = ((bf16[64,8,128]{2,1,0:T(8,128)(2,1)}), bf16[64,8,128]{2,1,0:T(8,128)(2,1)S(1)}, u32[]{:S(2)}, u32[]{:S(2)}) async-start(bf16[64,8,128]{2,1,0:T(8,128)(2,1)} %bitcast.12), calls=%async_computation.1 | async-start | bytes 262144 | tf_op jit(solution)/shard_map/all_to_all | solution.py:339
  145.6 26.5 %copy-start.9 = (bf16[128,1024]{1,0:T(8,128)(2,1)}, bf16[128,1024]{1,0:T(8,128)(2,1)S(1)}, u32[]{:S(2)}) copy-start(bf16[128,1024]{1,0:T(8,128)(2,1)S(1)} %get-tuple-element.37.q_ref) | copy-start | bytes 786436
  172.1 1.0 copy-start.10
  176.4 10.7 %collective-permute-start.6 = (bf16[128,2048]{1,0:T(8,128)(2,1)S(1)}, bf16[128,2048]{1,0:T(8,128)(2,1)S(1)}, u32[]{:S(2)}, u32[]{:S(2)}) collective-permute-start(bf16[128,2048]{1,0:T(8,128)(2,1)S(1)} %output.4), channel_id=1, source_target_pairs={{0,128},{1,129},{2,130},{3,131},{4,132},{5,133},{6,134},{7,135},{8... | collective-permute-start | bytes 1572872 | tf_op jit(solution)/shard_map/ppermute | solution.py:336
  192.3 0.8 copy-start.1
  193.1 19.6 %all-to-all-start.3 = ((bf16[64,8,128]{2,1,0:T(8,128)(2,1)}), bf16[64,8,128]{2,1,0:T(8,128)(2,1)S(1)}, u32[]{:S(2)}, u32[]{:S(2)}) async-start(bf16[64,8,128]{2,1,0:T(8,128)(2,1)} %bitcast.14), calls=%async_computation.3 | async-start | bytes 262144 | tf_op jit(solution)/shard_map/all_to_all | solution.py:339
  200.1 1.0 copy-start.2
  205.3 0.7 copy-start.5
  230.8 1.0 copy-start.6
  236.0 10.9 %collective-permute-start.7 = (bf16[128,2048]{1,0:T(8,128)(2,1)}, bf16[128,2048]{1,0:T(8,128)(2,1)S(1)}, u32[]{:S(2)}, u32[]{:S(2)}) collective-permute-start(bf16[128,2048]{1,0:T(8,128)(2,1)} %output.5), channel_id=1, source_target_pairs={{128,0},{129,1},{130,2},{131,3},{132,4},{133,5},{134,6},{135,7},{1... | collective-permute-start | bytes 1572872 | tf_op jit(solution)/shard_map/ppermute | solution.py:336
  251.9 17.1 %all-to-all-start.5 = ((bf16[64,8,128]{2,1,0:T(8,128)(2,1)}), bf16[64,8,128]{2,1,0:T(8,128)(2,1)S(1)}, u32[]{:S(2)}, u32[]{:S(2)}) async-start(bf16[64,8,128]{2,1,0:T(8,128)(2,1)} %bitcast.17), calls=%async_computation.5 | async-start | bytes 262144 | tf_op jit(solution)/shard_map/all_to_all | solution.py:339
  261.7 0.7 copy-start.11
  285.9 1.0 copy-start.12
  290.2 7.4 %collective-permute-start.8 = (bf16[128,2048]{1,0:T(8,128)(2,1)S(1)}, bf16[128,2048]{1,0:T(8,128)(2,1)S(1)}, u32[]{:S(2)}, u32[]{:S(2)}) collective-permute-start(bf16[128,2048]{1,0:T(8,128)(2,1)S(1)} %output.6), channel_id=1, source_target_pairs={{0,128},{1,129},{2,130},{3,131},{4,132},{5,133},{6,134},{7,135},{8... | collective-permute-start | bytes 1572872 | tf_op jit(solution)/shard_map/ppermute | solution.py:336
  302.5 0.8 copy-start.3
  303.3 16.1 %all-to-all-start.7 = ((bf16[64,8,128]{2,1,0:T(8,128)(2,1)}), bf16[64,8,128]{2,1,0:T(8,128)(2,1)S(1)}, u32[]{:S(2)}, u32[]{:S(2)}) async-start(bf16[64,8,128]{2,1,0:T(8,128)(2,1)} %bitcast.19), calls=%async_computation.7 | async-start | bytes 262144 | tf_op jit(solution)/shard_map/all_to_all | solution.py:339
  307.9 1.0 copy-start.4
  313.0 0.7 copy-start.7
  337.4 1.0 copy-start.8
  341.8 10.6 %collective-permute-start.9 = (bf16[128,2048]{1,0:T(8,128)(2,1)S(1)}, bf16[128,2048]{1,0:T(8,128)(2,1)S(1)}, u32[]{:S(2)}, u32[]{:S(2)}) collective-permute-start(bf16[128,2048]{1,0:T(8,128)(2,1)S(1)} %broadcast_select_fusion.2), channel_id=1, source_target_pairs={{0,64},{64,0},{1,65},{65,1},{2,66},{66,2},{3,67},{67,3},{4,68},{68... | collective-permute-start | bytes 1572872 | tf_op jit(solution)/shard_map/ppermute | solution.py:18
Sparse Core Ops, SparseCore 0:
  25.3 102.9 all-gather.4
  131.0 105.1 all-gather.6

commit v4 on v3

--- a/solution.py
+++ b/solution.py
@@ -184,23 +184,28 @@
     )(x, weights, kv, table)
 
 
-def carry_kernel(state_ref, total_ref, out_ref):
+def carry_kernel(start_ref, state_ref, total_ref, out_ref):
     carried = jnp.zeros(state_ref.shape[1:], jnp.float32)
-    for c in range(state_ref.shape[0]):
+    count = state_ref.shape[0]
+    start = start_ref[0]
+    for i in range(count):
+        c = start + i if i < count // 2 else i - start
         out_ref[c] = carried.astype(jnp.bfloat16)
-        carried = total_ref[c : c + 1, :] * carried + state_ref[c].astype(jnp.float32)
-
-
-def carry(states, totals):
+        carried = total_ref[pl.ds(c, 1), :] * carried + state_ref[c].astype(jnp.float32)
+
+
+def carry(states, totals, start):
     return pl.pallas_call(
         carry_kernel,
+        in_specs=[pl.BlockSpec(memory_space=pltpu.SMEM)] + [pl.BlockSpec(memory_space=pltpu.VMEM)] * 2,
+        out_specs=pl.BlockSpec(memory_space=pltpu.VMEM),
         out_shape=jax.ShapeDtypeStruct(states.shape, jnp.bfloat16),
         compiler_params=pltpu.CompilerParams(vmem_limit_bytes=4 * 2**20),
         cost_estimate=pl.CostEstimate(
             flops=2 * states.size, bytes_accessed=4 * states.size, transcendentals=0
         ),
         name="carry",
-    )(states, totals)
+    )(start, states, totals)
 
 
 def output_kernel(
@@ -269,6 +274,16 @@
 def across(value, axes):
     flip = [(0, 3), (1, 2), (2, 1), (3, 0)] if len(axes) == 2 else [(0, 1), (1, 0)]
     return lax.ppermute(value, axes, flip)
+
+
+def hand_over(value, hops):
+    pairs = []
+    for level, turn in hops:
+        for core in range(2):
+            for far in range(2):
+                goal = far ^ core if turn else far
+                pairs.append((level * 4 + core * 2 + far, (1 - level) * 4 + core * 2 + goal))
+    return lax.ppermute(value, ("ylo", "core", "yhi"), pairs)
 
 
 def shared_weights(qkv, out, core, level):
@@ -299,7 +314,7 @@
 
 def decays(log_decay, core, level):
     first, second = paired(log_decay[0], log_decay[1], core)
-    come = across(jnp.where(level == 0, second, first), ("ylo",))
+    come = hand_over(jnp.where(level == 0, second, first), [(0, True), (1, False)])
     both = [jnp.where(level == 0, first, come), jnp.where(level == 0, come, second)]
     rows, heads = first.shape
     lower = jnp.tril(jnp.ones((rows, rows), jnp.float32))
@@ -328,18 +343,20 @@
     weights = shared_weights(qkv_weight[0], out_weight[0], core, level)
     tables, totals = decays(log_decay[0], core, level)
     x, totals, tables = lax.optimization_barrier((x, totals, tables))
+    straight = jnp.zeros((1,), jnp.int32)
+    turned = straight + core * (blocks // 2)
     kept = []
     for step in range(4):
         layer = step // 2
         table, w = tables[layer], weights[layer]
         if step > 0:
-            x = lax.ppermute(x, "ylo", [(1 - step % 2, step % 2)])
+            x = hand_over(x, [(1 - step % 2, step < 3)])
             kept.append(x)
         kv, state = project_keys(x, w, table)
         slices = lax.all_to_all(state.reshape(blocks, -1, 128), CTX, 0, 0, tiled=True)
         q, inside = within(x, w, kv, table)
         slices, inside = lax.optimization_barrier((slices, inside))
-        mine = carry(slices, totals[layer])
+        mine = carry(slices, totals[layer], turned if step == 1 else straight)
         carried = lax.all_to_all(mine, CTX, 0, 0, tiled=True).reshape(state.shape)
         x = output(q, carried, table, inside, x, w)
         kept.append(x)

time: 362 us -> 358 us (0.989)
    ppermute x4 -> x3, waiting for transfers between devices: 8.52 us -> 6.25 us  [across(): return lax.ppermute(value, axes, flip)]
    ppermute x3 -> x4, waiting for transfers between devices: 24.2 us -> 22.4 us  [hand_over(): return lax.ppermute(value, ('ylo', 'core', 'yhi'), pairs)]
  transfers between devices with their start and end apart: 17 -> 17, of which waited for: 16 -> 17; matrix products, arithmetic and copies ran while one was open for 2% -> 2% of each run, Pallas kernels for 9% -> 10%
where the time goes in v4:
time: 358 us; the launch traced here: 357 us
  waiting for transfers between devices  142 us (40%)
  blocking collectives  70.2 us (20%)
  starting transfers between devices  58.4 us (16%)
  Pallas kernels  50.8 us (14%)
  local copies, waits for them, and re-layouts  14.8 us (4%)
  between operations  13.7 us (4%)
  other arithmetic  5.31 us (1%)
    all_to_all x4, blocking collectives, shards(): carried = lax.all_to_all(mine, CTX, 0, 0, tiled=True).reshape(state.shape)  70.2 us
    all_gather x2, waiting for transfers between devices, shared_weights(): lax.all_gather(own, SPREAD, axis=0).reshape(2, -1, own.shape[0], NB)  65.8 us
    all_to_all x4, waiting for transfers between devices, shards(): lax.all_to_all(state.reshape(blocks, -1, 128), CTX, 0, 0, tiled=True)  28.3 us
    all_to_all x4, starting transfers between devices, shards(): lax.all_to_all(state.reshape(blocks, -1, 128), CTX, 0, 0, tiled=True)  24.5 us
    ppermute x4, waiting for transfers between devices, hand_over(): return lax.ppermute(value, ('ylo', 'core', 'yhi'), pairs)  22.4 us
    pallas_call x4, Pallas kernels, project_keys(): pl.pallas_call(functools.partial(keys_kernel, blocks), in_specs=[vmem, pl...  20 us
    pallas_call x4, Pallas kernels, within(): pl.pallas_call(functools.partial(within_kernel, blocks), in_specs=[vmem,...  16 us
    all_to_all x1, waiting for transfers between devices, decays(): received = lax.all_to_all(sent, CTX, 0, 0, tiled=True)  15.7 us
  transfers between devices with their start and end apart: 17, of which 17 were waited for; matrix products, arithmetic and copies ran while one was open for 2% of the time, Pallas kernels for 10%

profile of v4, /device:TPU:1, one launch (start us, length us, event | category | flops | bytes accessed | tf_op | source)
XLA Modules:
  0.0 357.0 jit_solution(3005391354452463511)
XLA Ops:
  10.5 3.3 collective-permute-start.2
  35.1 12.6 %all-to-all-start = ((f32[64,8,128]{2,1,0:T(8,128)}), f32[64,8,128]{2,1,0:T(8,128)S(1)}, u32[]{:S(2)}, u32[]{:S(2)}) async-start(f32[64,8,128]{2,1,0:T(8,128)} %maximum_maximum_fusion), calls=%async_computation | async-start | bytes 524288 | tf_op jit(solution)/shard_map/all_to_all | solution.py:334
  48.0 15.7 %all-to-all-done = f32[64,8,128]{2,1,0:T(8,128)S(1)} async-done(((f32[64,8,128]{2,1,0:T(8,128)}), f32[64,8,128]{2,1,0:T(8,128)S(1)}, u32[]{:S(2)}, u32[]{:S(2)}) %all-to-all-start) | async-done | bytes 262176 | tf_op jit(solution)/shard_map/all_to_all | solution.py:334
  63.8 64.7 %all-gather.5.cloned.1.call-done = bf16[16384,512]{1,0:T(8,128)(2,1)} async-done(((bf16[256,512]{1,0:T(8,128)(2,1)}), bf16[16384,512]{1,0:T(8,128)(2,1)}) %all-gather.5.cloned.1.call-update) | async-done | bytes 16777232 | tf_op jit(solution)/shard_map/all_gather | solution.py:311
  128.5 4.9 %keys.4 = (bf16[128,2048]{1,0:T(8,128)(2,1)S(1)}, bf16[512,128]{1,0:T(8,128)(2,1)}) custom-call(bf16[128,2048]{1,0:T(8,128)(2,1)S(1)} %dynamic-slice_bitcast_fusion.x_ref, bf16[2,32,256,512]{3,2,1,0:T(8,128)(2,1)} %bitcast.60, f32[144,128]{1,0:T(8,128)S(1)} %get-tuple-element.35.table_ref), custom_call_target="tpu_custom_call" | custom-call | flops 1073741824 | bytes 8388608 | tf_op jit(solution)/shard_map/keys/pallas_call | solution.py:99
  133.4 8.4 %all-to-all-start.1 = ((bf16[64,8,128]{2,1,0:T(8,128)(2,1)}), bf16[64,8,128]{2,1,0:T(8,128)(2,1)S(1)}, u32[]{:S(2)}, u32[]{:S(2)}) async-start(bf16[64,8,128]{2,1,0:T(8,128)(2,1)} %bitcast.12), calls=%async_computation.1 | async-start | bytes 262144 | tf_op jit(solution)/shard_map/all_to_all | solution.py:356
  141.8 4.0 %within.4 = (bf16[128,1024]{1,0:T(8,128)(2,1)S(1)}, f32[128,1024]{1,0:T(8,128)S(1)}) custom-call(bf16[128,2048]{1,0:T(8,128)(2,1)S(1)} %dynamic-slice_bitcast_fusion.x_ref, bf16[2,32,256,512]{3,2,1,0:T(8,128)(2,1)} %bitcast.61, bf16[128,2048]{1,0:T(8,128)(2,1)S(1)} %get-tuple-element.36.kv_ref, f32[144,128]{1,0:T(8,128)S(1)} %get-tuple-element.35.table_ref), custom_call_target="tpu_custom_call" | custom-call | flops 637534208 | bytes 6291456 | tf_op jit(solution)/shard_map/within/pallas_call | solution.py:165
  145.8 9.2 %all-to-all-done.1.state_ref = bf16[64,8,128]{2,1,0:T(8,128)(2,1)S(1)} async-done(((bf16[64,8,128]{2,1,0:T(8,128)(2,1)}), bf16[64,8,128]{2,1,0:T(8,128)(2,1)S(1)}, u32[]{:S(2)}, u32[]{:S(2)}) %all-to-all-start.1) | async-done | bytes 131104 | tf_op jit(solution)/shard_map/all_to_all | solution.py:356
  155.1 17.7 %all_to_all.45 = bf16[64,8,128]{2,1,0:T(8,128)(2,1)S(1)} all-to-all(bf16[64,8,128]{2,1,0:T(8,128)(2,1)S(1)} %carry.4), channel_id=1, replica_groups=mesh['ylo'=2,'core'=2,'yhi'=2,'x'=4,'z'=8] {'yhi','x','z'}, dimensions={0} | all-to-all | bytes 262144 | tf_op jit(solution)/shard_map/all_to_all | solution.py:360
  173.7 3.4 output.4
  179.5 6.1 %collective-permute-done.6.x_ref = bf16[128,2048]{1,0:T(8,128)(2,1)S(1)} collective-permute-done((bf16[128,2048]{1,0:T(8,128)(2,1)S(1)}, bf16[128,2048]{1,0:T(8,128)(2,1)S(1)}, u32[]{:S(2)}, u32[]{:S(2)}) %collective-permute-start.6) | collective-permute-done | bytes 524320 | tf_op jit(solution)/shard_map/ppermute | solution.py:286
  185.5 5.2 %keys.5 = (bf16[128,2048]{1,0:T(8,128)(2,1)S(1)}, bf16[512,128]{1,0:T(8,128)(2,1)}) custom-call(bf16[128,2048]{1,0:T(8,128)(2,1)S(1)} %collective-permute-done.6.x_ref, bf16[2,32,256,512]{3,2,1,0:T(8,128)(2,1)} %bitcast.63, f32[144,128]{1,0:T(8,128)S(1)} %get-tuple-element.35.table_ref), custom_call_target="tpu_custom_call" | custom-call | flops 1073741824 | bytes 8388608 | tf_op jit(solution)/shard_map/keys/pallas_call | solution.py:99
  191.5 6.5 %all-to-all-start.3 = ((bf16[64,8,128]{2,1,0:T(8,128)(2,1)}), bf16[64,8,128]{2,1,0:T(8,128)(2,1)S(1)}, u32[]{:S(2)}, u32[]{:S(2)}) async-start(bf16[64,8,128]{2,1,0:T(8,128)(2,1)} %bitcast.15), calls=%async_computation.3 | async-start | bytes 262144 | tf_op jit(solution)/shard_map/all_to_all | solution.py:356
  199.1 4.0 %within.5 = (bf16[128,1024]{1,0:T(8,128)(2,1)S(1)}, f32[128,1024]{1,0:T(8,128)S(1)}) custom-call(bf16[128,2048]{1,0:T(8,128)(2,1)S(1)} %collective-permute-done.6.x_ref, bf16[2,32,256,512]{3,2,1,0:T(8,128)(2,1)} %bitcast.64, bf16[128,2048]{1,0:T(8,128)(2,1)S(1)} %copy-done.2, f32[144,128]{1,0:T(8,128)S(1)} %get-tuple-element.35.table_ref), custom_call_target="tpu_custom_call" | custom-call | flops 637534208 | bytes 6291456 | tf_op jit(solution)/shard_map/within/pallas_call | solution.py:165
  203.8 6.9 %all-to-all-done.3.state_ref = bf16[64,8,128]{2,1,0:T(8,128)(2,1)S(1)} async-done(((bf16[64,8,128]{2,1,0:T(8,128)(2,1)}), bf16[64,8,128]{2,1,0:T(8,128)(2,1)S(1)}, u32[]{:S(2)}, u32[]{:S(2)}) %all-to-all-start.3) | async-done | bytes 131104 | tf_op jit(solution)/shard_map/all_to_all | solution.py:356
  210.8 17.9 %all_to_all.46 = bf16[64,8,128]{2,1,0:T(8,128)(2,1)S(1)} all-to-all(bf16[64,8,128]{2,1,0:T(8,128)(2,1)S(1)} %carry.5), channel_id=1, replica_groups=mesh['ylo'=2,'core'=2,'yhi'=2,'x'=4,'z'=8] {'yhi','x','z'}, dimensions={0} | all-to-all | bytes 262144 | tf_op jit(solution)/shard_map/all_to_all | solution.py:360
  229.7 4.3 %output.5 = bf16[128,2048]{1,0:T(8,128)(2,1)} custom-call(bf16[128,1024]{1,0:T(8,128)(2,1)S(1)} %copy-done.6, bf16[512,128]{1,0:T(8,128)(2,1)S(1)} %bitcast.46, f32[144,128]{1,0:T(8,128)S(1)} %get-tuple-element.35.table_ref, f32[128,1024]{1,0:T(8,128)S(1)} %get-tuple-element.48.within_ref, bf16[128,2048]{1,0:T(8,128)(2,1)S(1)} %collective-permute-done.6.x_ref, ...), custom_call_target="tpu_custom_call" | custom-call | flops 536870912 | bytes 4194304 | tf_op jit(solution)/shard_map/output/pallas_call | solution.py:251
  236.4 9.0 %collective-permute-done.7.x_ref = bf16[128,2048]{1,0:T(8,128)(2,1)S(1)} collective-permute-done((bf16[128,2048]{1,0:T(8,128)(2,1)}, bf16[128,2048]{1,0:T(8,128)(2,1)S(1)}, u32[]{:S(2)}, u32[]{:S(2)}) %collective-permute-start.7) | collective-permute-done | bytes 524320 | tf_op jit(solution)/shard_map/ppermute | solution.py:286
  245.3 4.9 %keys.6 = (bf16[128,2048]{1,0:T(8,128)(2,1)S(1)}, bf16[512,128]{1,0:T(8,128)(2,1)}) custom-call(bf16[128,2048]{1,0:T(8,128)(2,1)S(1)} %collective-permute-done.7.x_ref, bf16[2,32,256,512]{3,2,1,0:T(8,128)(2,1)} %bitcast.54, f32[144,128]{1,0:T(8,128)S(1)} %get-tuple-element.49.table_ref), custom_call_target="tpu_custom_call" | custom-call | flops 1073741824 | bytes 8388608 | tf_op jit(solution)/shard_map/keys/pallas_call | solution.py:99
  250.3 5.0 %all-to-all-start.5 = ((bf16[64,8,128]{2,1,0:T(8,128)(2,1)}), bf16[64,8,128]{2,1,0:T(8,128)(2,1)S(1)}, u32[]{:S(2)}, u32[]{:S(2)}) async-start(bf16[64,8,128]{2,1,0:T(8,128)(2,1)} %bitcast.18), calls=%async_computation.5 | async-start | bytes 262144 | tf_op jit(solution)/shard_map/all_to_all | solution.py:356
  255.3 4.0 %within.6 = (bf16[128,1024]{1,0:T(8,128)(2,1)S(1)}, f32[128,1024]{1,0:T(8,128)S(1)}) custom-call(bf16[128,2048]{1,0:T(8,128)(2,1)S(1)} %collective-permute-done.7.x_ref, bf16[2,32,256,512]{3,2,1,0:T(8,128)(2,1)} %bitcast.55, bf16[128,2048]{1,0:T(8,128)(2,1)S(1)} %get-tuple-element.50.kv_ref, f32[144,128]{1,0:T(8,128)S(1)} %get-tuple-element.49.table_ref), custom_call_target="tpu_custom_call" | custom-call | flops 637534208 | bytes 6291456 | tf_op jit(solution)/shard_map/within/pallas_call | solution.py:165
  260.0 6.6 %all-to-all-done.5.state_ref = bf16[64,8,128]{2,1,0:T(8,128)(2,1)S(1)} async-done(((bf16[64,8,128]{2,1,0:T(8,128)(2,1)}), bf16[64,8,128]{2,1,0:T(8,128)(2,1)S(1)}, u32[]{:S(2)}, u32[]{:S(2)}) %all-to-all-start.5) | async-done | bytes 131104 | tf_op jit(solution)/shard_map/all_to_all | solution.py:356
  266.7 16.8 %all_to_all.47 = bf16[64,8,128]{2,1,0:T(8,128)(2,1)S(1)} all-to-all(bf16[64,8,128]{2,1,0:T(8,128)(2,1)S(1)} %carry.6), channel_id=1, replica_groups=mesh['ylo'=2,'core'=2,'yhi'=2,'x'=4,'z'=8] {'yhi','x','z'}, dimensions={0} | all-to-all | bytes 262144 | tf_op jit(solution)/shard_map/all_to_all | solution.py:360
  284.4 3.4 output.6
  289.1 6.1 %collective-permute-done.8.x_ref = bf16[128,2048]{1,0:T(8,128)(2,1)S(1)} collective-permute-done((bf16[128,2048]{1,0:T(8,128)(2,1)S(1)}, bf16[128,2048]{1,0:T(8,128)(2,1)S(1)}, u32[]{:S(2)}, u32[]{:S(2)}) %collective-permute-start.8) | collective-permute-done | bytes 524320 | tf_op jit(solution)/shard_map/ppermute | solution.py:286
  295.2 4.9 %keys.7 = (bf16[128,2048]{1,0:T(8,128)(2,1)S(1)}, bf16[512,128]{1,0:T(8,128)(2,1)}) custom-call(bf16[128,2048]{1,0:T(8,128)(2,1)S(1)} %collective-permute-done.8.x_ref, bf16[2,32,256,512]{3,2,1,0:T(8,128)(2,1)} %bitcast.57, f32[144,128]{1,0:T(8,128)S(1)} %get-tuple-element.49.table_ref), custom_call_target="tpu_custom_call" | custom-call | flops 1073741824 | bytes 8388608 | tf_op jit(solution)/shard_map/keys/pallas_call | solution.py:99
  300.9 4.6 %all-to-all-start.7 = ((bf16[64,8,128]{2,1,0:T(8,128)(2,1)}), bf16[64,8,128]{2,1,0:T(8,128)(2,1)S(1)}, u32[]{:S(2)}, u32[]{:S(2)}) async-start(bf16[64,8,128]{2,1,0:T(8,128)(2,1)} %bitcast.20), calls=%async_computation.7 | async-start | bytes 262144 | tf_op jit(solution)/shard_map/all_to_all | solution.py:356
  306.6 4.0 %within.7 = (bf16[128,1024]{1,0:T(8,128)(2,1)S(1)}, f32[128,1024]{1,0:T(8,128)S(1)}) custom-call(bf16[128,2048]{1,0:T(8,128)(2,1)S(1)} %collective-permute-done.8.x_ref, bf16[2,32,256,512]{3,2,1,0:T(8,128)(2,1)} %bitcast.58, bf16[128,2048]{1,0:T(8,128)(2,1)S(1)} %copy-done.4, f32[144,128]{1,0:T(8,128)S(1)} %get-tuple-element.49.table_ref), custom_call_target="tpu_custom_call" | custom-call | flops 637534208 | bytes 6291456 | tf_op jit(solution)/shard_map/within/pallas_call | solution.py:165
  311.3 5.8 %all-to-all-done.7.state_ref = bf16[64,8,128]{2,1,0:T(8,128)(2,1)S(1)} async-done(((bf16[64,8,128]{2,1,0:T(8,128)(2,1)}), bf16[64,8,128]{2,1,0:T(8,128)(2,1)S(1)}, u32[]{:S(2)}, u32[]{:S(2)}) %all-to-all-start.7) | async-done | bytes 131104 | tf_op jit(solution)/shard_map/all_to_all | solution.py:356
  317.2 17.8 %all_to_all.48 = bf16[64,8,128]{2,1,0:T(8,128)(2,1)S(1)} all-to-all(bf16[64,8,128]{2,1,0:T(8,128)(2,1)S(1)} %carry.7), channel_id=1, replica_groups=mesh['ylo'=2,'core'=2,'yhi'=2,'x'=4,'z'=8] {'yhi','x','z'}, dimensions={0} | all-to-all | bytes 262144 | tf_op jit(solution)/shard_map/all_to_all | solution.py:360
  335.9 3.4 output.7
  339.4 8.0 %collective-permute-start.9 = (bf16[128,2048]{1,0:T(8,128)(2,1)S(1)}, bf16[128,2048]{1,0:T(8,128)(2,1)S(1)}, u32[]{:S(2)}, u32[]{:S(2)}) collective-permute-start(bf16[128,2048]{1,0:T(8,128)(2,1)S(1)} %broadcast_select_fusion.2), channel_id=1, source_target_pairs={{0,64},{64,0},{1,65},{65,1},{2,66},{66,2},{3,67},{67,3},{4,68},{68... | collective-permute-start | bytes 1572872 | tf_op jit(solution)/shard_map/ppermute | solution.py:18
  (92 shorter events, 44.6 us)
Async XLA Ops:
  6.5 23.5 %copy-start = (bf16[2,128,2048]{2,1,0:T(8,128)(2,1)S(1)}, bf16[2,128,2048]{2,1,0:T(8,128)(2,1)}, u32[]{:S(2)}) copy-start(bf16[2,128,2048]{2,1,0:T(8,128)(2,1)} %param.4) | copy-start | bytes 3145732
  6.5 121.9 %all-gather.5.cloned.1.call-start = ((), (), s32[]{:S(2)}) async-start(), calls=%async_computation.9 | async-start | bytes 17039360 | tf_op jit(solution)/shard_map/all_gather | solution.py:311
  10.5 4.3 %collective-permute-start.2 = (bf16[128,512]{1,0:T(8,128)(2,1)S(1)}, bf16[128,512]{1,0:T(8,128)(2,1)S(1)}, u32[]{:S(2)}, u32[]{:S(2)}) collective-permute-start(bf16[128,512]{1,0:T(8,128)(2,1)S(1)} %broadcast_select_fusion.7), channel_id=1, source_target_pairs={{0,64},{64,0},{1,65},{65,1},{2,66},{66,2},{3,67},{67,3},{4,68},{68... | collective-permute-start | bytes 393224 | tf_op jit(solution)/shard_map/ppermute | solution.py:18
  14.8 6.3 %collective-permute-start.4 = (bf16[128,512]{1,0:T(8,128)(2,1)S(1)}, bf16[128,512]{1,0:T(8,128)(2,1)S(1)}, u32[]{:S(2)}, u32[]{:S(2)}) collective-permute-start(bf16[128,512]{1,0:T(8,128)(2,1)S(1)} %broadcast_select_fusion.12), channel_id=1, source_target_pairs={{0,32},{32,0},{1,33},{33,1},{2,34},{34,2},{3,35},{35,3},{4,36},{36... | collective-permute-start | bytes 393224 | tf_op jit(solution)/shard_map/ppermute | solution.py:276
  16.1 6.5 %collective-permute-start.3 = (bf16[128,512]{1,0:T(8,128)(2,1)S(1)}, bf16[128,512]{1,0:T(8,128)(2,1)S(1)}, u32[]{:S(2)}, u32[]{:S(2)}) collective-permute-start(bf16[128,512]{1,0:T(8,128)(2,1)S(1)} %get-tuple-element.67), channel_id=1, source_target_pairs={{0,128},{128,0},{1,129},{129,1},{2,130},{130,2},{3,131},{131,3},{4... | collective-permute-start | bytes 393224 | tf_op jit(solution)/shard_map/ppermute | solution.py:276
  16.5 7.9 %collective-permute-start.5 = (bf16[128,512]{1,0:T(8,128)(2,1)S(1)}, bf16[128,512]{1,0:T(8,128)(2,1)S(1)}, u32[]{:S(2)}, u32[]{:S(2)}) collective-permute-start(bf16[128,512]{1,0:T(8,128)(2,1)S(1)} %get-tuple-element.67), channel_id=1, source_target_pairs={{0,160},{32,128},{128,32},{160,0},{1,161},{33,129},{129,33},{161,1... | collective-permute-start | bytes 393224 | tf_op jit(solution)/shard_map/ppermute | solution.py:276
  25.2 211.2 %all-gather.7.cloned.1.call-start = ((), (), s32[]{:S(2)}) async-start(), calls=%async_computation.10 | async-start | bytes 17039360 | tf_op jit(solution)/shard_map/all_gather | solution.py:311
  26.8 1.5 collective-permute-start
  29.0 2.5 collective-permute-start.1
  35.1 28.7 %all-to-all-start = ((f32[64,8,128]{2,1,0:T(8,128)}), f32[64,8,128]{2,1,0:T(8,128)S(1)}, u32[]{:S(2)}, u32[]{:S(2)}) async-start(f32[64,8,128]{2,1,0:T(8,128)} %maximum_maximum_fusion), calls=%async_computation | async-start | bytes 524288 | tf_op jit(solution)/shard_map/all_to_all | solution.py:334
  133.4 21.5 %all-to-all-start.1 = ((bf16[64,8,128]{2,1,0:T(8,128)(2,1)}), bf16[64,8,128]{2,1,0:T(8,128)(2,1)S(1)}, u32[]{:S(2)}, u32[]{:S(2)}) async-start(bf16[64,8,128]{2,1,0:T(8,128)(2,1)} %bitcast.12), calls=%async_computation.1 | async-start | bytes 262144 | tf_op jit(solution)/shard_map/all_to_all | solution.py:356
  145.8 27.0 %copy-start.9 = (bf16[128,1024]{1,0:T(8,128)(2,1)}, bf16[128,1024]{1,0:T(8,128)(2,1)S(1)}, u32[]{:S(2)}) copy-start(bf16[128,1024]{1,0:T(8,128)(2,1)S(1)} %get-tuple-element.37.q_ref) | copy-start | bytes 786436
  172.8 1.0 copy-start.10
  177.1 8.5 %collective-permute-start.6 = (bf16[128,2048]{1,0:T(8,128)(2,1)S(1)}, bf16[128,2048]{1,0:T(8,128)(2,1)S(1)}, u32[]{:S(2)}, u32[]{:S(2)}) collective-permute-start(bf16[128,2048]{1,0:T(8,128)(2,1)S(1)} %output.4), channel_id=1, source_target_pairs={{0,128},{32,160},{64,224},{96,192},{1,129},{33,161},{65,225},{97,1... | collective-permute-start | bytes 1572872 | tf_op jit(solution)/shard_map/ppermute | solution.py:286
  190.7 0.8 copy-start.1
  191.5 19.1 %all-to-all-start.3 = ((bf16[64,8,128]{2,1,0:T(8,128)(2,1)}), bf16[64,8,128]{2,1,0:T(8,128)(2,1)S(1)}, u32[]{:S(2)}, u32[]{:S(2)}) async-start(bf16[64,8,128]{2,1,0:T(8,128)(2,1)} %bitcast.15), calls=%async_computation.3 | async-start | bytes 262144 | tf_op jit(solution)/shard_map/all_to_all | solution.py:356
  198.1 1.0 copy-start.2
  203.1 0.7 copy-start.5
  228.8 1.0 copy-start.6
  234.0 11.3 %collective-permute-start.7 = (bf16[128,2048]{1,0:T(8,128)(2,1)}, bf16[128,2048]{1,0:T(8,128)(2,1)S(1)}, u32[]{:S(2)}, u32[]{:S(2)}) collective-permute-start(bf16[128,2048]{1,0:T(8,128)(2,1)} %output.5), channel_id=1, source_target_pairs={{128,0},{160,32},{192,96},{224,64},{129,1},{161,33},{193,97},{225,... | collective-permute-start | bytes 1572872 | tf_op jit(solution)/shard_map/ppermute | solution.py:286
  250.3 16.3 %all-to-all-start.5 = ((bf16[64,8,128]{2,1,0:T(8,128)(2,1)}), bf16[64,8,128]{2,1,0:T(8,128)(2,1)S(1)}, u32[]{:S(2)}, u32[]{:S(2)}) async-start(bf16[64,8,128]{2,1,0:T(8,128)(2,1)} %bitcast.18), calls=%async_computation.5 | async-start | bytes 262144 | tf_op jit(solution)/shard_map/all_to_all | solution.py:356
  259.3 0.7 copy-start.11
  283.5 1.0 copy-start.12
  287.8 7.4 %collective-permute-start.8 = (bf16[128,2048]{1,0:T(8,128)(2,1)S(1)}, bf16[128,2048]{1,0:T(8,128)(2,1)S(1)}, u32[]{:S(2)}, u32[]{:S(2)}) collective-permute-start(bf16[128,2048]{1,0:T(8,128)(2,1)S(1)} %output.6), channel_id=1, source_target_pairs={{0,128},{32,160},{64,192},{96,224},{1,129},{33,161},{65,193},{97,2... | collective-permute-start | bytes 1572872 | tf_op jit(solution)/shard_map/ppermute | solution.py:286
  300.1 0.8 copy-start.3
  300.9 16.1 %all-to-all-start.7 = ((bf16[64,8,128]{2,1,0:T(8,128)(2,1)}), bf16[64,8,128]{2,1,0:T(8,128)(2,1)S(1)}, u32[]{:S(2)}, u32[]{:S(2)}) async-start(bf16[64,8,128]{2,1,0:T(8,128)(2,1)} %bitcast.20), calls=%async_computation.7 | async-start | bytes 262144 | tf_op jit(solution)/shard_map/all_to_all | solution.py:356
  305.5 1.0 copy-start.4
  310.6 0.7 copy-start.7
  335.0 1.0 copy-start.8
  339.4 9.5 %collective-permute-start.9 = (bf16[128,2048]{1,0:T(8,128)(2,1)S(1)}, bf16[128,2048]{1,0:T(8,128)(2,1)S(1)}, u32[]{:S(2)}, u32[]{:S(2)}) collective-permute-start(bf16[128,2048]{1,0:T(8,128)(2,1)S(1)} %broadcast_select_fusion.2), channel_id=1, source_target_pairs={{0,64},{64,0},{1,65},{65,1},{2,66},{66,2},{3,67},{67,3},{4,68},{68... | collective-permute-start | bytes 1572872 | tf_op jit(solution)/shard_map/ppermute | solution.py:18
Sparse Core Ops, SparseCore 0:
  25.3 103.0 all-gather.4
  131.2 105.1 all-gather.6

commit v5 on v4

--- a/solution.py
+++ b/solution.py
@@ -58,16 +58,54 @@
     return (x * lax.rsqrt(jnp.mean(x * x, axis=-1, keepdims=True) + EPS)).astype(jnp.bfloat16)
 
 
+def fetch_kernel(blocks, w_ref, out_ref, sems):
+    copies = share_copies(blocks, w_ref, out_ref, sems)
+    start_all(copies)
+    for block in copies:
+        for copy in block:
+            copy.wait()
+
+
+def key_blocks(share):
+    half = NB // 2
+    return [
+        (share, [(side, share * part, half * i, half) for part in (1, 2)])
+        for side in range(2)
+        for i in range(2)
+    ]
+
+
+def fetch_keys(weights, share):
+    return pl.pallas_call(
+        functools.partial(fetch_kernel, key_blocks(share)),
+        in_specs=[pl.BlockSpec(memory_space=pl.ANY)],
+        out_specs=pl.BlockSpec(memory_space=pltpu.VMEM),
+        out_shape=pltpu.VMEM((4, 2, 32, share, NB), jnp.bfloat16),
+        scratch_shapes=[pltpu.SemaphoreType.DMA((4, 4))],
+        compiler_params=pltpu.CompilerParams(vmem_limit_bytes=VMEM_KEPT),
+        cost_estimate=pl.CostEstimate(flops=0, bytes_accessed=4 * 4 * 64 * share * NB, transcendentals=0),
+        name="fetch",
+    )(weights)
+
+
+def fetched_keys_kernel(x_ref, buffer, table_ref, kv_ref, state_ref):
+    keys_of([[]] * buffer.shape[0], x_ref, table_ref, kv_ref, state_ref, buffer)
+
+
 def keys_kernel(blocks, x_ref, w_ref, table_ref, kv_ref, state_ref, buffer, sems):
     copies = share_copies(blocks, w_ref, buffer, sems)
     start_all(copies)
+    keys_of(copies, x_ref, table_ref, kv_ref, state_ref, buffer)
+
+
+def keys_of(copies, x_ref, table_ref, kv_ref, state_ref, buffer):
     rows = x_ref.shape[0]
     inner = kv_ref.shape[1] // 2
     normed = normalized(x_ref)
     low = half_mask(rows, 128, 64)
     scale = table_ref[:rows, 16:32]
     half = NB // 2
-    for k in range(len(blocks)):
+    for k in range(len(copies)):
         part = block_dot(normed, copies, buffer, k).astype(jnp.bfloat16)
         kv_ref[:, half * k : half * (k + 1)] = part[:, :half]
         kv_ref[:, inner + half * k : inner + half * (k + 1)] = part[:, half:]
@@ -89,26 +127,23 @@
     rows, width = x.shape
     inner = 1024
     share = width // 64
-    half = NB // 2
-    blocks = [
-        (share, [(side, share * part, half * i, half) for part in (1, 2)])
-        for side in range(2)
-        for i in range(2)
+    blocks = key_blocks(share)
+    vmem = pl.BlockSpec(memory_space=pltpu.VMEM)
+    fetched = weights.ndim == 5
+    scratch = [
+        pltpu.VMEM((len(blocks), 2, 32, share, NB), jnp.bfloat16),
+        pltpu.SemaphoreType.DMA((len(blocks), 4)),
     ]
-    vmem = pl.BlockSpec(memory_space=pltpu.VMEM)
-    return pl.pallas_call(
-        functools.partial(keys_kernel, blocks),
-        in_specs=[vmem, pl.BlockSpec(memory_space=pl.ANY), vmem],
+    return pl.pallas_call(
+        fetched_keys_kernel if fetched else functools.partial(keys_kernel, blocks),
+        in_specs=[vmem, vmem if fetched else pl.BlockSpec(memory_space=pl.ANY), vmem],
         out_specs=[vmem] * 2,
         out_shape=[
             jax.ShapeDtypeStruct((rows, 2 * inner), jnp.bfloat16),
             jax.ShapeDtypeStruct((inner // 2, 128), jnp.bfloat16),
         ],
-        scratch_shapes=[
-            pltpu.VMEM((len(blocks), 2, 32, share, NB), jnp.bfloat16),
-            pltpu.SemaphoreType.DMA((len(blocks), 4)),
-        ],
-        compiler_params=pltpu.CompilerParams(vmem_limit_bytes=VMEM_KEPT),
+        scratch_shapes=[] if fetched else scratch,
+        compiler_params=pltpu.CompilerParams(vmem_limit_bytes=16 * 2**20 if fetched else VMEM_KEPT),
         cost_estimate=pl.CostEstimate(
             flops=4 * rows * width * inner, bytes_accessed=4 * width * inner, transcendentals=0
         ),
@@ -276,6 +311,36 @@
     return lax.ppermute(value, axes, flip)
 
 
+def split_kernel(core_ref, qkv_ref, out_ref, keep_ref, give_ref):
+    rows, depth = qkv_ref.shape[0], out_ref.shape[0]
+    inner, wide = qkv_ref.shape[1] // 3, out_ref.shape[1] // 2
+    core = core_ref[0]
+    for side in range(2):
+        for mine, goal in ((True, keep_ref), (False, give_ref)):
+
+            @pl.when((core == side) == mine)
+            def _(side=side, goal=goal):
+                for i in range(3):
+                    at = inner * i + NB * side
+                    goal[rows * i : rows * (i + 1), :] = qkv_ref[:, at : at + NB]
+                for i in range(2):
+                    at, row = wide * side + NB * i, 3 * rows + depth * i
+                    goal[row : row + depth, :] = out_ref[:, at : at + NB]
+
+
+def split_halves(qkv, out, core):
+    vmem = pl.BlockSpec(memory_space=pltpu.VMEM)
+    half = jax.ShapeDtypeStruct(((qkv.size + out.size) // (2 * NB), NB), jnp.bfloat16)
+    return pl.pallas_call(
+        split_kernel,
+        in_specs=[pl.BlockSpec(memory_space=pltpu.SMEM), vmem, vmem],
+        out_specs=[vmem] * 2,
+        out_shape=[half] * 2,
+        compiler_params=pltpu.CompilerParams(vmem_limit_bytes=VMEM_KEPT),
+        name="split",
+    )(core.reshape(1).astype(jnp.int32), qkv, out)
+
+
 def hand_over(value, hops):
     pairs = []
     for level, turn in hops:
@@ -287,15 +352,9 @@
 
 
 def shared_weights(qkv, out, core, level):
-    rows, depth = qkv.shape[0], out.shape[0]
-    inner = qkv.shape[1] // 3
-    halves = []
-    for side in range(2):
-        cut = [qkv[:, inner * i + NB * side : inner * i + NB * (side + 1)] for i in range(3)]
-        first = out.shape[1] // 2 * side
-        cut += [out[:, first + NB * i : first + NB * (i + 1)] for i in range(2)]
-        halves.append(jnp.concatenate(cut, axis=0))
-    first, second = paired(halves[0], halves[1], core)
+    keep, give = split_halves(qkv, out, core)
+    other = swap(give, "core")
+    first, second = jnp.where(core == 0, keep, other), jnp.where(core == 0, other, keep)
     stay = jnp.where(level == 0, first, second)
     leave = jnp.where(level == 0, second, first)
     far = across(stay, ("yhi",))
@@ -349,10 +408,13 @@
     for step in range(4):
         layer = step // 2
         table, w = tables[layer], weights[layer]
+        keys_from = w
         if step > 0:
+            _, source = lax.optimization_barrier((x, w))
+            keys_from = fetch_keys(source, x.shape[1] // 64)
             x = hand_over(x, [(1 - step % 2, step < 3)])
             kept.append(x)
-        kv, state = project_keys(x, w, table)
+        kv, state = project_keys(x, keys_from, table)
         slices = lax.all_to_all(state.reshape(blocks, -1, 128), CTX, 0, 0, tiled=True)
         q, inside = within(x, w, kv, table)
         slices, inside = lax.optimization_barrier((slices, inside))

time: 358 us -> 346 us (0.966)
  local copies, waits for them, and re-layouts: 14.8 us -> 3.26 us
  blocking collectives: 70.2 us -> 65.6 us
  Pallas kernels: 50.8 us -> 55.4 us
  waiting for transfers between devices: 142 us -> 138 us
  starting transfers between devices: 58.4 us -> 62.1 us
    ppermute x4, waiting for transfers between devices: 22.4 us -> 7.42 us  [hand_over(): return lax.ppermute(value, ('ylo', 'core', 'yhi'), pairs)]
    unnamed x30 -> x8, local copies, waits for them, and re-layouts: 12.7 us -> 1.86 us
    all_gather x2, waiting for transfers between devices: 65.8 us -> 72.7 us  [shared_weights(): lax.all_gather(own, SPREAD, axis=0).reshape(2, -1, own.shape[0], NB)]
    pallas_call x4 -> x8, Pallas kernels: 20 us -> 25.2 us  [the longest x4 13.6 us: project_keys(): pl.pallas_call(fetched_keys_kernel if fetched else functools.partial(keys...]
    all_to_all x4, blocking collectives: 70.2 us -> 65.6 us  [shards(): carried = lax.all_to_all(mine, CTX, 0, 0, tiled=True).reshape(state.shape)]
    all_to_all x4, waiting for transfers between devices: 28.3 us -> 32.1 us  [shards(): lax.all_to_all(state.reshape(blocks, -1, 128), CTX, 0, 0, tiled=True)]
  transfers between devices with their start and end apart: 17 -> 17, of which waited for: 17 -> 16; matrix products, arithmetic and copies ran while one was open for 2% -> 2% of each run, Pallas kernels for 10% -> 12%
where the time goes in v5:
time: 346 us; the launch traced here: 345 us
  waiting for transfers between devices  138 us (40%)
  blocking collectives  65.6 us (19%)
  starting transfers between devices  62.1 us (18%)
  Pallas kernels  55.4 us (16%)
  between operations  13.7 us (4%)
  other arithmetic  5.29 us (2%)
    all_gather x2, waiting for transfers between devices, shared_weights(): lax.all_gather(own, SPREAD, axis=0).reshape(2, -1, own.shape[0], NB)  72.7 us
    all_to_all x4, blocking collectives, shards(): carried = lax.all_to_all(mine, CTX, 0, 0, tiled=True).reshape(state.shape)  65.6 us
    all_to_all x4, waiting for transfers between devices, shards(): lax.all_to_all(state.reshape(blocks, -1, 128), CTX, 0, 0, tiled=True)  32.1 us
    all_to_all x4, starting transfers between devices, shards(): lax.all_to_all(state.reshape(blocks, -1, 128), CTX, 0, 0, tiled=True)  27.8 us
    pallas_call x4, Pallas kernels, within(): pl.pallas_call(functools.partial(within_kernel, blocks), in_specs=[vmem,...  16.2 us
    all_to_all x1, waiting for transfers between devices, decays(): received = lax.all_to_all(sent, CTX, 0, 0, tiled=True)  15.7 us
    pallas_call x4, Pallas kernels, project_keys(): pl.pallas_call(fetched_keys_kernel if fetched else functools.partial(keys...  13.6 us
    pallas_call x4, Pallas kernels, output(): pl.pallas_call(functools.partial(output_kernel, blocks), in_specs=[vmem]...  13.5 us
  transfers between devices with their start and end apart: 17, of which 16 were waited for; matrix products, arithmetic and copies ran while one was open for 2% of the time, Pallas kernels for 12%

profile of v5, /device:TPU:1, one launch (start us, length us, event | category | flops | bytes accessed | tf_op | source)
XLA Modules:
  0.0 345.3 jit_solution(11291517832795314037)
XLA Ops:
  8.4 3.3 collective-permute-start.2
  17.6 3.6 %collective-permute-done.4 = bf16[128,512]{1,0:T(8,128)(2,1)S(1)} collective-permute-done((bf16[128,512]{1,0:T(8,128)(2,1)S(1)}, bf16[128,512]{1,0:T(8,128)(2,1)S(1)}, u32[]{:S(2)}, u32[]{:S(2)}) %collective-permute-start.4) | collective-permute-done | bytes 131104 | tf_op jit(solution)/shard_map/ppermute | solution.py:311
  34.6 11.7 %all-to-all-start = ((f32[64,8,128]{2,1,0:T(8,128)}), f32[64,8,128]{2,1,0:T(8,128)S(1)}, u32[]{:S(2)}, u32[]{:S(2)}) async-start(f32[64,8,128]{2,1,0:T(8,128)} %maximum_maximum_fusion), calls=%async_computation | async-start | bytes 524288 | tf_op jit(solution)/shard_map/all_to_all | solution.py:393
  46.6 15.7 %all-to-all-done = f32[64,8,128]{2,1,0:T(8,128)S(1)} async-done(((f32[64,8,128]{2,1,0:T(8,128)}), f32[64,8,128]{2,1,0:T(8,128)S(1)}, u32[]{:S(2)}, u32[]{:S(2)}) %all-to-all-start) | async-done | bytes 262176 | tf_op jit(solution)/shard_map/all_to_all | solution.py:393
  62.4 64.7 %all-gather.5.cloned.1.call-done = bf16[16384,512]{1,0:T(8,128)(2,1)} async-done(((bf16[256,512]{1,0:T(8,128)(2,1)}), bf16[16384,512]{1,0:T(8,128)(2,1)}) %all-gather.5.cloned.1.call-update) | async-done | bytes 16777232 | tf_op jit(solution)/shard_map/all_gather | solution.py:370
  127.1 4.9 %keys.4 = (bf16[128,2048]{1,0:T(8,128)(2,1)S(1)}, bf16[512,128]{1,0:T(8,128)(2,1)}) custom-call(bf16[128,2048]{1,0:T(8,128)(2,1)S(1)} %dynamic-slice_bitcast_fusion.x_ref, bf16[2,32,256,512]{3,2,1,0:T(8,128)(2,1)} %bitcast.63, f32[144,128]{1,0:T(8,128)S(1)} %get-tuple-element.42.table_ref), custom_call_target="tpu_custom_call" | custom-call | flops 1073741824 | bytes 8388608 | tf_op jit(solution)/shard_map/keys/pallas_call | solution.py:137
  132.1 8.4 %all-to-all-start.1 = ((bf16[64,8,128]{2,1,0:T(8,128)(2,1)}), bf16[64,8,128]{2,1,0:T(8,128)(2,1)S(1)}, u32[]{:S(2)}, u32[]{:S(2)}) async-start(bf16[64,8,128]{2,1,0:T(8,128)(2,1)} %bitcast.13), calls=%async_computation.1 | async-start | bytes 262144 | tf_op jit(solution)/shard_map/all_to_all | solution.py:418
  140.4 4.0 %within.4 = (bf16[128,1024]{1,0:T(8,128)(2,1)S(1)}, f32[128,1024]{1,0:T(8,128)S(1)}) custom-call(bf16[128,2048]{1,0:T(8,128)(2,1)S(1)} %dynamic-slice_bitcast_fusion.x_ref, bf16[2,32,256,512]{3,2,1,0:T(8,128)(2,1)} %bitcast.64, bf16[128,2048]{1,0:T(8,128)(2,1)S(1)} %get-tuple-element.43.kv_ref, f32[144,128]{1,0:T(8,128)S(1)} %get-tuple-element.42.table_ref), custom_call_target="tpu_custom_call" | custom-call | flops 637534208 | bytes 6291456 | tf_op jit(solution)/shard_map/within/pallas_call | solution.py:200
  144.4 9.2 %all-to-all-done.1.state_ref = bf16[64,8,128]{2,1,0:T(8,128)(2,1)S(1)} async-done(((bf16[64,8,128]{2,1,0:T(8,128)(2,1)}), bf16[64,8,128]{2,1,0:T(8,128)(2,1)S(1)}, u32[]{:S(2)}, u32[]{:S(2)}) %all-to-all-start.1) | async-done | bytes 131104 | tf_op jit(solution)/shard_map/all_to_all | solution.py:418
  153.7 16.9 %all_to_all.45 = bf16[64,8,128]{2,1,0:T(8,128)(2,1)S(1)} all-to-all(bf16[64,8,128]{2,1,0:T(8,128)(2,1)S(1)} %carry.4), channel_id=1, replica_groups=mesh['ylo'=2,'core'=2,'yhi'=2,'x'=4,'z'=8] {'yhi','x','z'}, dimensions={0} | all-to-all | bytes 262144 | tf_op jit(solution)/shard_map/all_to_all | solution.py:422
  170.6 3.4 output.4
  176.9 4.2 %fetch.3.buffer = bf16[4,2,32,32,512]{4,3,2,1,0:T(8,128)(2,1)S(1)} custom-call(bf16[2,32,256,512]{3,2,1,0:T(8,128)(2,1)} %bitcast.66), custom_call_target="tpu_custom_call" | custom-call | bytes 16777216 | tf_op jit(solution)/shard_map/fetch/pallas_call | solution.py:79
  185.8 5.4 %all-to-all-start.3 = ((bf16[64,8,128]{2,1,0:T(8,128)(2,1)}), bf16[64,8,128]{2,1,0:T(8,128)(2,1)S(1)}, u32[]{:S(2)}, u32[]{:S(2)}) async-start(bf16[64,8,128]{2,1,0:T(8,128)(2,1)} %bitcast.16), calls=%async_computation.3 | async-start | bytes 262144 | tf_op jit(solution)/shard_map/all_to_all | solution.py:418
  191.2 4.2 %within.5 = (bf16[128,1024]{1,0:T(8,128)(2,1)S(1)}, f32[128,1024]{1,0:T(8,128)S(1)}) custom-call(bf16[128,2048]{1,0:T(8,128)(2,1)S(1)} %collective-permute-done.6.x_ref, bf16[2,32,256,512]{3,2,1,0:T(8,128)(2,1)} %bitcast.67, bf16[128,2048]{1,0:T(8,128)(2,1)S(1)} %get-tuple-element.51.kv_ref, f32[144,128]{1,0:T(8,128)S(1)} %get-tuple-element.42.table_ref), custom_call_target="tpu_custom_call" | custom-call | flops 637534208 | bytes 6291456 | tf_op jit(solution)/shard_map/within/pallas_call | solution.py:200
  195.4 8.0 %all-to-all-done.3.state_ref = bf16[64,8,128]{2,1,0:T(8,128)(2,1)S(1)} async-done(((bf16[64,8,128]{2,1,0:T(8,128)(2,1)}), bf16[64,8,128]{2,1,0:T(8,128)(2,1)S(1)}, u32[]{:S(2)}, u32[]{:S(2)}) %all-to-all-start.3) | async-done | bytes 131104 | tf_op jit(solution)/shard_map/all_to_all | solution.py:418
  203.5 16.6 %all_to_all.46 = bf16[64,8,128]{2,1,0:T(8,128)(2,1)S(1)} all-to-all(bf16[64,8,128]{2,1,0:T(8,128)(2,1)S(1)} %carry.5), channel_id=1, replica_groups=mesh['ylo'=2,'core'=2,'yhi'=2,'x'=4,'z'=8] {'yhi','x','z'}, dimensions={0} | all-to-all | bytes 262144 | tf_op jit(solution)/shard_map/all_to_all | solution.py:422
  220.1 3.4 output.5
  224.9 8.0 %all-gather.7.cloned.1.call-done = bf16[16384,512]{1,0:T(8,128)(2,1)} async-done(((bf16[256,512]{1,0:T(8,128)(2,1)}), bf16[16384,512]{1,0:T(8,128)(2,1)}) %all-gather.7.cloned.1.call-update) | async-done | bytes 16777232 | tf_op jit(solution)/shard_map/all_gather | solution.py:370
  232.8 3.7 %fetch.4.buffer = bf16[4,2,32,32,512]{4,3,2,1,0:T(8,128)(2,1)S(1)} custom-call(bf16[2,32,256,512]{3,2,1,0:T(8,128)(2,1)} %bitcast.57), custom_call_target="tpu_custom_call" | custom-call | bytes 16777216 | tf_op jit(solution)/shard_map/fetch/pallas_call | solution.py:79
  239.4 8.9 %all-to-all-start.5 = ((bf16[64,8,128]{2,1,0:T(8,128)(2,1)}), bf16[64,8,128]{2,1,0:T(8,128)(2,1)S(1)}, u32[]{:S(2)}, u32[]{:S(2)}) async-start(bf16[64,8,128]{2,1,0:T(8,128)(2,1)} %bitcast.19), calls=%async_computation.5 | async-start | bytes 262144 | tf_op jit(solution)/shard_map/all_to_all | solution.py:418
  248.3 4.0 %within.6 = (bf16[128,1024]{1,0:T(8,128)(2,1)S(1)}, f32[128,1024]{1,0:T(8,128)S(1)}) custom-call(bf16[128,2048]{1,0:T(8,128)(2,1)S(1)} %collective-permute-done.7.x_ref, bf16[2,32,256,512]{3,2,1,0:T(8,128)(2,1)} %bitcast.58, bf16[128,2048]{1,0:T(8,128)(2,1)S(1)} %get-tuple-element.59.kv_ref, f32[144,128]{1,0:T(8,128)S(1)} %get-tuple-element.58.table_ref), custom_call_target="tpu_custom_call" | custom-call | flops 637534208 | bytes 6291456 | tf_op jit(solution)/shard_map/within/pallas_call | solution.py:200
  252.3 7.4 %all-to-all-done.5.state_ref = bf16[64,8,128]{2,1,0:T(8,128)(2,1)S(1)} async-done(((bf16[64,8,128]{2,1,0:T(8,128)(2,1)}), bf16[64,8,128]{2,1,0:T(8,128)(2,1)S(1)}, u32[]{:S(2)}, u32[]{:S(2)}) %all-to-all-start.5) | async-done | bytes 131104 | tf_op jit(solution)/shard_map/all_to_all | solution.py:418
  259.9 16.1 %all_to_all.47 = bf16[64,8,128]{2,1,0:T(8,128)(2,1)S(1)} all-to-all(bf16[64,8,128]{2,1,0:T(8,128)(2,1)S(1)} %carry.6), channel_id=1, replica_groups=mesh['ylo'=2,'core'=2,'yhi'=2,'x'=4,'z'=8] {'yhi','x','z'}, dimensions={0} | all-to-all | bytes 262144 | tf_op jit(solution)/shard_map/all_to_all | solution.py:422
  276.0 3.4 output.6
  282.7 3.7 %fetch.5.buffer = bf16[4,2,32,32,512]{4,3,2,1,0:T(8,128)(2,1)S(1)} custom-call(bf16[2,32,256,512]{3,2,1,0:T(8,128)(2,1)} %bitcast.60), custom_call_target="tpu_custom_call" | custom-call | bytes 16777216 | tf_op jit(solution)/shard_map/fetch/pallas_call | solution.py:79
  286.3 4.9 %collective-permute-done.8.x_ref = bf16[128,2048]{1,0:T(8,128)(2,1)S(1)} collective-permute-done((bf16[128,2048]{1,0:T(8,128)(2,1)S(1)}, bf16[128,2048]{1,0:T(8,128)(2,1)S(1)}, u32[]{:S(2)}, u32[]{:S(2)}) %collective-permute-start.8) | collective-permute-done | bytes 524320 | tf_op jit(solution)/shard_map/ppermute | solution.py:351
  294.2 5.1 %all-to-all-start.7 = ((bf16[64,8,128]{2,1,0:T(8,128)(2,1)}), bf16[64,8,128]{2,1,0:T(8,128)(2,1)S(1)}, u32[]{:S(2)}, u32[]{:S(2)}) async-start(bf16[64,8,128]{2,1,0:T(8,128)(2,1)} %bitcast.21), calls=%async_computation.7 | async-start | bytes 262144 | tf_op jit(solution)/shard_map/all_to_all | solution.py:418
  299.3 4.0 %within.7 = (bf16[128,1024]{1,0:T(8,128)(2,1)S(1)}, f32[128,1024]{1,0:T(8,128)S(1)}) custom-call(bf16[128,2048]{1,0:T(8,128)(2,1)S(1)} %collective-permute-done.8.x_ref, bf16[2,32,256,512]{3,2,1,0:T(8,128)(2,1)} %bitcast.61, bf16[128,2048]{1,0:T(8,128)(2,1)S(1)} %get-tuple-element.67.kv_ref, f32[144,128]{1,0:T(8,128)S(1)} %get-tuple-element.58.table_ref), custom_call_target="tpu_custom_call" | custom-call | flops 637534208 | bytes 6291456 | tf_op jit(solution)/shard_map/within/pallas_call | solution.py:200
  303.3 7.5 %all-to-all-done.7.state_ref = bf16[64,8,128]{2,1,0:T(8,128)(2,1)S(1)} async-done(((bf16[64,8,128]{2,1,0:T(8,128)(2,1)}), bf16[64,8,128]{2,1,0:T(8,128)(2,1)S(1)}, u32[]{:S(2)}, u32[]{:S(2)}) %all-to-all-start.7) | async-done | bytes 131104 | tf_op jit(solution)/shard_map/all_to_all | solution.py:418
  310.9 16.0 %all_to_all.48 = bf16[64,8,128]{2,1,0:T(8,128)(2,1)S(1)} all-to-all(bf16[64,8,128]{2,1,0:T(8,128)(2,1)S(1)} %carry.7), channel_id=1, replica_groups=mesh['ylo'=2,'core'=2,'yhi'=2,'x'=4,'z'=8] {'yhi','x','z'}, dimensions={0} | all-to-all | bytes 262144 | tf_op jit(solution)/shard_map/all_to_all | solution.py:422
  327.0 3.4 output.7
  330.5 5.2 %collective-permute-start.9 = (bf16[128,2048]{1,0:T(8,128)(2,1)S(1)}, bf16[128,2048]{1,0:T(8,128)(2,1)S(1)}, u32[]{:S(2)}, u32[]{:S(2)}) collective-permute-start(bf16[128,2048]{1,0:T(8,128)(2,1)S(1)} %broadcast_select_fusion.2), channel_id=1, source_target_pairs={{0,64},{64,0},{1,65},{65,1},{2,66},{66,2},{3,67},{67,3},{4,68},{68... | collective-permute-start | bytes 1572872 | tf_op jit(solution)/shard_map/ppermute | solution.py:18
  (71 shorter events, 43.0 us)
Async XLA Ops:
  6.5 23.7 %copy-start = (bf16[2,128,2048]{2,1,0:T(8,128)(2,1)S(1)}, bf16[2,128,2048]{2,1,0:T(8,128)(2,1)}, u32[]{:S(2)}) copy-start(bf16[2,128,2048]{2,1,0:T(8,128)(2,1)} %param.4) | copy-start | bytes 3145732
  6.5 120.6 %all-gather.5.cloned.1.call-start = ((), (), s32[]{:S(2)}) async-start(), calls=%async_computation.9 | async-start | bytes 17039360 | tf_op jit(solution)/shard_map/all_gather | solution.py:370
  6.5 1.0 copy-start.2
  7.6 0.8 copy-start.3
  8.4 4.3 %collective-permute-start.2 = (bf16[128,512]{1,0:T(8,128)(2,1)S(1)}, bf16[128,512]{1,0:T(8,128)(2,1)S(1)}, u32[]{:S(2)}, u32[]{:S(2)}) collective-permute-start(bf16[128,512]{1,0:T(8,128)(2,1)S(1)} %get-tuple-element.41), channel_id=1, source_target_pairs={{0,64},{64,0},{1,65},{65,1},{2,66},{66,2},{3,67},{67,3},{4,68},{68... | collective-permute-start | bytes 393224 | tf_op jit(solution)/shard_map/ppermute | solution.py:18
  12.8 4.8 %collective-permute-start.3 = (bf16[128,512]{1,0:T(8,128)(2,1)S(1)}, bf16[128,512]{1,0:T(8,128)(2,1)S(1)}, u32[]{:S(2)}, u32[]{:S(2)}) collective-permute-start(bf16[128,512]{1,0:T(8,128)(2,1)S(1)} %get-tuple-element.83), channel_id=1, source_target_pairs={{0,128},{128,0},{1,129},{129,1},{2,130},{130,2},{3,131},{131,3},{4... | collective-permute-start | bytes 393224 | tf_op jit(solution)/shard_map/ppermute | solution.py:311
  12.9 8.3 %collective-permute-start.4 = (bf16[128,512]{1,0:T(8,128)(2,1)S(1)}, bf16[128,512]{1,0:T(8,128)(2,1)S(1)}, u32[]{:S(2)}, u32[]{:S(2)}) collective-permute-start(bf16[128,512]{1,0:T(8,128)(2,1)S(1)} %get-tuple-element.84), channel_id=1, source_target_pairs={{0,32},{32,0},{1,33},{33,1},{2,34},{34,2},{3,35},{35,3},{4,36},{36... | collective-permute-start | bytes 393224 | tf_op jit(solution)/shard_map/ppermute | solution.py:311
  15.0 8.6 %collective-permute-start.5 = (bf16[128,512]{1,0:T(8,128)(2,1)S(1)}, bf16[128,512]{1,0:T(8,128)(2,1)S(1)}, u32[]{:S(2)}, u32[]{:S(2)}) collective-permute-start(bf16[128,512]{1,0:T(8,128)(2,1)S(1)} %get-tuple-element.83), channel_id=1, source_target_pairs={{0,160},{32,128},{128,32},{160,0},{1,161},{33,129},{129,33},{161,1... | collective-permute-start | bytes 393224 | tf_op jit(solution)/shard_map/ppermute | solution.py:311
  24.4 208.4 %all-gather.7.cloned.1.call-start = ((), (), s32[]{:S(2)}) async-start(), calls=%async_computation.10 | async-start | bytes 17039360 | tf_op jit(solution)/shard_map/all_gather | solution.py:370
  26.0 1.8 collective-permute-start
  28.5 2.5 collective-permute-start.1
  34.6 27.8 %all-to-all-start = ((f32[64,8,128]{2,1,0:T(8,128)}), f32[64,8,128]{2,1,0:T(8,128)S(1)}, u32[]{:S(2)}, u32[]{:S(2)}) async-start(f32[64,8,128]{2,1,0:T(8,128)} %maximum_maximum_fusion), calls=%async_computation | async-start | bytes 524288 | tf_op jit(solution)/shard_map/all_to_all | solution.py:393
  132.1 21.5 %all-to-all-start.1 = ((bf16[64,8,128]{2,1,0:T(8,128)(2,1)}), bf16[64,8,128]{2,1,0:T(8,128)(2,1)S(1)}, u32[]{:S(2)}, u32[]{:S(2)}) async-start(bf16[64,8,128]{2,1,0:T(8,128)(2,1)} %bitcast.13), calls=%async_computation.1 | async-start | bytes 262144 | tf_op jit(solution)/shard_map/all_to_all | solution.py:418
  174.0 9.0 %collective-permute-start.6 = (bf16[128,2048]{1,0:T(8,128)(2,1)S(1)}, bf16[128,2048]{1,0:T(8,128)(2,1)S(1)}, u32[]{:S(2)}, u32[]{:S(2)}) collective-permute-start(bf16[128,2048]{1,0:T(8,128)(2,1)S(1)} %output.4), channel_id=1, source_target_pairs={{0,128},{32,160},{64,224},{96,192},{1,129},{33,161},{65,225},{97,1... | collective-permute-start | bytes 1572872 | tf_op jit(solution)/shard_map/ppermute | solution.py:351
  185.8 17.6 %all-to-all-start.3 = ((bf16[64,8,128]{2,1,0:T(8,128)(2,1)}), bf16[64,8,128]{2,1,0:T(8,128)(2,1)S(1)}, u32[]{:S(2)}, u32[]{:S(2)}) async-start(bf16[64,8,128]{2,1,0:T(8,128)(2,1)} %bitcast.16), calls=%async_computation.3 | async-start | bytes 262144 | tf_op jit(solution)/shard_map/all_to_all | solution.py:418
  223.6 12.9 %collective-permute-start.7 = (bf16[128,2048]{1,0:T(8,128)(2,1)S(1)}, bf16[128,2048]{1,0:T(8,128)(2,1)S(1)}, u32[]{:S(2)}, u32[]{:S(2)}) collective-permute-start(bf16[128,2048]{1,0:T(8,128)(2,1)S(1)} %output.5), channel_id=1, source_target_pairs={{128,0},{160,32},{192,96},{224,64},{129,1},{161,33},{193,97},{225,... | collective-permute-start | bytes 1572872 | tf_op jit(solution)/shard_map/ppermute | solution.py:351
  239.4 20.3 %all-to-all-start.5 = ((bf16[64,8,128]{2,1,0:T(8,128)(2,1)}), bf16[64,8,128]{2,1,0:T(8,128)(2,1)S(1)}, u32[]{:S(2)}, u32[]{:S(2)}) async-start(bf16[64,8,128]{2,1,0:T(8,128)(2,1)} %bitcast.19), calls=%async_computation.5 | async-start | bytes 262144 | tf_op jit(solution)/shard_map/all_to_all | solution.py:418
  279.3 11.9 %collective-permute-start.8 = (bf16[128,2048]{1,0:T(8,128)(2,1)S(1)}, bf16[128,2048]{1,0:T(8,128)(2,1)S(1)}, u32[]{:S(2)}, u32[]{:S(2)}) collective-permute-start(bf16[128,2048]{1,0:T(8,128)(2,1)S(1)} %output.6), channel_id=1, source_target_pairs={{0,128},{32,160},{64,192},{96,224},{1,129},{33,161},{65,193},{97,2... | collective-permute-start | bytes 1572872 | tf_op jit(solution)/shard_map/ppermute | solution.py:351
  294.2 16.6 %all-to-all-start.7 = ((bf16[64,8,128]{2,1,0:T(8,128)(2,1)}), bf16[64,8,128]{2,1,0:T(8,128)(2,1)S(1)}, u32[]{:S(2)}, u32[]{:S(2)}) async-start(bf16[64,8,128]{2,1,0:T(8,128)(2,1)} %bitcast.21), calls=%async_computation.7 | async-start | bytes 262144 | tf_op jit(solution)/shard_map/all_to_all | solution.py:418
  327.0 11.5 %copy-start.1 = (bf16[2,128,2048]{2,1,0:T(8,128)(2,1)S(1)}, bf16[2,128,2048]{2,1,0:T(8,128)(2,1)}, u32[]{:S(2)}) copy-start(bf16[2,128,2048]{2,1,0:T(8,128)(2,1)} %param.4) | copy-start | bytes 3145732
  330.5 6.7 %collective-permute-start.9 = (bf16[128,2048]{1,0:T(8,128)(2,1)S(1)}, bf16[128,2048]{1,0:T(8,128)(2,1)S(1)}, u32[]{:S(2)}, u32[]{:S(2)}) collective-permute-start(bf16[128,2048]{1,0:T(8,128)(2,1)S(1)} %broadcast_select_fusion.2), channel_id=1, source_target_pairs={{0,64},{64,0},{1,65},{65,1},{2,66},{66,2},{3,67},{67,3},{4,68},{68... | collective-permute-start | bytes 1572872 | tf_op jit(solution)/shard_map/ppermute | solution.py:18
Sparse Core Ops, SparseCore 0:
  24.6 102.5 all-gather.4
  129.9 102.9 all-gather.6

commit v6 on v5

--- a/solution.py
+++ b/solution.py
@@ -389,7 +389,7 @@
         wide = jnp.concatenate([cum, jnp.exp(ending - cum), jnp.exp(cum)], axis=1)
         wide = jnp.pad(wide, ((0, 0), (0, rows - wide.shape[1])))
         tables.append(jnp.concatenate([wide, cum.T], axis=0))
-    sent = jnp.stack(rows_sent + [jnp.zeros_like(rows_sent[0])] * 6, axis=1)
+    sent = jnp.stack(rows_sent, axis=1)
     received = lax.all_to_all(sent, CTX, 0, 0, tiled=True)
     return tables, [received[:, k, :] for k in range(2)]
 

time: 346 us -> 345 us (level)
    all_to_all x1, waiting for transfers between devices: 15.7 us -> 10.8 us  [decays(): received = lax.all_to_all(sent, CTX, 0, 0, tiled=True)]
where the time goes in v6:
time: 345 us; the launch traced here: 344 us
  waiting for transfers between devices  136 us (39%)
  blocking collectives  65.7 us (19%)
  starting transfers between devices  62.2 us (18%)
  Pallas kernels  55.7 us (16%)
  between operations  13.6 us (4%)
  other arithmetic  5.17 us (1%)
    all_gather x2, waiting for transfers between devices, shared_weights(): lax.all_gather(own, SPREAD, axis=0).reshape(2, -1, own.shape[0], NB)  76 us
    all_to_all x4, blocking collectives, shards(): carried = lax.all_to_all(mine, CTX, 0, 0, tiled=True).reshape(state.shape)  65.7 us
    all_to_all x4, waiting for transfers between devices, shards(): lax.all_to_all(state.reshape(blocks, -1, 128), CTX, 0, 0, tiled=True)  32 us
    all_to_all x4, starting transfers between devices, shards(): lax.all_to_all(state.reshape(blocks, -1, 128), CTX, 0, 0, tiled=True)  27.5 us
    pallas_call x4, Pallas kernels, within(): pl.pallas_call(functools.partial(within_kernel, blocks), in_specs=[vmem,...  16.2 us
    pallas_call x4, Pallas kernels, project_keys(): pl.pallas_call(fetched_keys_kernel if fetched else functools.partial(keys...  13.7 us
    pallas_call x4, Pallas kernels, output(): pl.pallas_call(functools.partial(output_kernel, blocks), in_specs=[vmem]...  13.5 us
    pallas_call x3, Pallas kernels, fetch_keys(): pl.pallas_call(functools.partial(fetch_kernel, key_blocks(share)), in_spe...  11.8 us
  transfers between devices with their start and end apart: 17, of which 16 were waited for; matrix products, arithmetic and copies ran while one was open for 2% of the time, Pallas kernels for 12%

profile of v6, /device:TPU:1, one launch (start us, length us, event | category | flops | bytes accessed | tf_op | source)
XLA Modules:
  0.0 343.6 jit_solution(8610584001019962595)
XLA Ops:
  17.6 3.6 %collective-permute-done.4 = bf16[128,512]{1,0:T(8,128)(2,1)S(1)} collective-permute-done((bf16[128,512]{1,0:T(8,128)(2,1)S(1)}, bf16[128,512]{1,0:T(8,128)(2,1)S(1)}, u32[]{:S(2)}, u32[]{:S(2)}) %collective-permute-start.4) | collective-permute-done | bytes 131104 | tf_op jit(solution)/shard_map/ppermute | solution.py:311
  34.5 11.7 %all-to-all-start = ((f32[64,2,128]{2,1,0:T(2,128)}), f32[64,2,128]{2,1,0:T(2,128)S(1)}, u32[]{:S(2)}, u32[]{:S(2)}) async-start(f32[64,2,128]{2,1,0:T(2,128)} %pad_maximum_fusion.2), calls=%async_computation | async-start | bytes 131072 | tf_op jit(solution)/shard_map/all_to_all | solution.py:393
  46.5 10.8 %all-to-all-done = f32[64,2,128]{2,1,0:T(2,128)S(1)} async-done(((f32[64,2,128]{2,1,0:T(2,128)}), f32[64,2,128]{2,1,0:T(2,128)S(1)}, u32[]{:S(2)}, u32[]{:S(2)}) %all-to-all-start) | async-done | bytes 65568 | tf_op jit(solution)/shard_map/all_to_all | solution.py:393
  57.3 68.1 %all-gather.5.cloned.1.call-done = bf16[16384,512]{1,0:T(8,128)(2,1)} async-done(((bf16[256,512]{1,0:T(8,128)(2,1)}), bf16[16384,512]{1,0:T(8,128)(2,1)}) %all-gather.5.cloned.1.call-update) | async-done | bytes 16777232 | tf_op jit(solution)/shard_map/all_gather | solution.py:370
  125.4 4.9 %keys.4 = (bf16[128,2048]{1,0:T(8,128)(2,1)S(1)}, bf16[512,128]{1,0:T(8,128)(2,1)}) custom-call(bf16[128,2048]{1,0:T(8,128)(2,1)S(1)} %dynamic-slice_bitcast_fusion.x_ref, bf16[2,32,256,512]{3,2,1,0:T(8,128)(2,1)} %bitcast.63, f32[144,128]{1,0:T(8,128)S(1)} %get-tuple-element.42.table_ref), custom_call_target="tpu_custom_call" | custom-call | flops 1073741824 | bytes 8388608 | tf_op jit(solution)/shard_map/keys/pallas_call | solution.py:137
  130.4 8.4 %all-to-all-start.1 = ((bf16[64,8,128]{2,1,0:T(8,128)(2,1)}), bf16[64,8,128]{2,1,0:T(8,128)(2,1)S(1)}, u32[]{:S(2)}, u32[]{:S(2)}) async-start(bf16[64,8,128]{2,1,0:T(8,128)(2,1)} %bitcast.13), calls=%async_computation.1 | async-start | bytes 262144 | tf_op jit(solution)/shard_map/all_to_all | solution.py:418
  138.7 4.0 %within.4 = (bf16[128,1024]{1,0:T(8,128)(2,1)S(1)}, f32[128,1024]{1,0:T(8,128)S(1)}) custom-call(bf16[128,2048]{1,0:T(8,128)(2,1)S(1)} %dynamic-slice_bitcast_fusion.x_ref, bf16[2,32,256,512]{3,2,1,0:T(8,128)(2,1)} %bitcast.64, bf16[128,2048]{1,0:T(8,128)(2,1)S(1)} %get-tuple-element.43.kv_ref, f32[144,128]{1,0:T(8,128)S(1)} %get-tuple-element.42.table_ref), custom_call_target="tpu_custom_call" | custom-call | flops 637534208 | bytes 6291456 | tf_op jit(solution)/shard_map/within/pallas_call | solution.py:200
  142.7 9.2 %all-to-all-done.1.state_ref = bf16[64,8,128]{2,1,0:T(8,128)(2,1)S(1)} async-done(((bf16[64,8,128]{2,1,0:T(8,128)(2,1)}), bf16[64,8,128]{2,1,0:T(8,128)(2,1)S(1)}, u32[]{:S(2)}, u32[]{:S(2)}) %all-to-all-start.1) | async-done | bytes 131104 | tf_op jit(solution)/shard_map/all_to_all | solution.py:418
  152.1 16.9 %all_to_all.45 = bf16[64,8,128]{2,1,0:T(8,128)(2,1)S(1)} all-to-all(bf16[64,8,128]{2,1,0:T(8,128)(2,1)S(1)} %carry.4), channel_id=1, replica_groups=mesh['ylo'=2,'core'=2,'yhi'=2,'x'=4,'z'=8] {'yhi','x','z'}, dimensions={0} | all-to-all | bytes 262144 | tf_op jit(solution)/shard_map/all_to_all | solution.py:422
  168.9 3.4 output.4
  175.3 4.5 %fetch.3.buffer = bf16[4,2,32,32,512]{4,3,2,1,0:T(8,128)(2,1)S(1)} custom-call(bf16[2,32,256,512]{3,2,1,0:T(8,128)(2,1)} %bitcast.66), custom_call_target="tpu_custom_call" | custom-call | bytes 16777216 | tf_op jit(solution)/shard_map/fetch/pallas_call | solution.py:79
  184.3 5.1 %all-to-all-start.3 = ((bf16[64,8,128]{2,1,0:T(8,128)(2,1)}), bf16[64,8,128]{2,1,0:T(8,128)(2,1)S(1)}, u32[]{:S(2)}, u32[]{:S(2)}) async-start(bf16[64,8,128]{2,1,0:T(8,128)(2,1)} %bitcast.16), calls=%async_computation.3 | async-start | bytes 262144 | tf_op jit(solution)/shard_map/all_to_all | solution.py:418
  189.4 4.2 %within.5 = (bf16[128,1024]{1,0:T(8,128)(2,1)S(1)}, f32[128,1024]{1,0:T(8,128)S(1)}) custom-call(bf16[128,2048]{1,0:T(8,128)(2,1)S(1)} %collective-permute-done.6.x_ref, bf16[2,32,256,512]{3,2,1,0:T(8,128)(2,1)} %bitcast.67, bf16[128,2048]{1,0:T(8,128)(2,1)S(1)} %get-tuple-element.51.kv_ref, f32[144,128]{1,0:T(8,128)S(1)} %get-tuple-element.42.table_ref), custom_call_target="tpu_custom_call" | custom-call | flops 637534208 | bytes 6291456 | tf_op jit(solution)/shard_map/within/pallas_call | solution.py:200
  193.6 7.9 %all-to-all-done.3.state_ref = bf16[64,8,128]{2,1,0:T(8,128)(2,1)S(1)} async-done(((bf16[64,8,128]{2,1,0:T(8,128)(2,1)}), bf16[64,8,128]{2,1,0:T(8,128)(2,1)S(1)}, u32[]{:S(2)}, u32[]{:S(2)}) %all-to-all-start.3) | async-done | bytes 131104 | tf_op jit(solution)/shard_map/all_to_all | solution.py:418
  201.6 16.7 %all_to_all.46 = bf16[64,8,128]{2,1,0:T(8,128)(2,1)S(1)} all-to-all(bf16[64,8,128]{2,1,0:T(8,128)(2,1)S(1)} %carry.5), channel_id=1, replica_groups=mesh['ylo'=2,'core'=2,'yhi'=2,'x'=4,'z'=8] {'yhi','x','z'}, dimensions={0} | all-to-all | bytes 262144 | tf_op jit(solution)/shard_map/all_to_all | solution.py:422
  218.3 3.4 %output.5 = bf16[128,2048]{1,0:T(8,128)(2,1)S(1)} custom-call(bf16[128,1024]{1,0:T(8,128)(2,1)S(1)} %get-tuple-element.52.q_ref, bf16[512,128]{1,0:T(8,128)(2,1)S(1)} %bitcast.47, f32[144,128]{1,0:T(8,128)S(1)} %get-tuple-element.42.table_ref, f32[128,1024]{1,0:T(8,128)S(1)} %get-tuple-element.56.within_ref, ...), custom_call_target="tpu_custom_call" | custom-call | flops 536870912 | bytes 4194304 | tf_op jit(solution)/shard_map/output/pallas_call | solution.py:286
  223.0 7.9 %all-gather.7.cloned.1.call-done = bf16[16384,512]{1,0:T(8,128)(2,1)} async-done(((bf16[256,512]{1,0:T(8,128)(2,1)}), bf16[16384,512]{1,0:T(8,128)(2,1)}) %all-gather.7.cloned.1.call-update) | async-done | bytes 16777232 | tf_op jit(solution)/shard_map/all_gather | solution.py:370
  231.0 3.7 %fetch.4.buffer = bf16[4,2,32,32,512]{4,3,2,1,0:T(8,128)(2,1)S(1)} custom-call(bf16[2,32,256,512]{3,2,1,0:T(8,128)(2,1)} %bitcast.57), custom_call_target="tpu_custom_call" | custom-call | bytes 16777216 | tf_op jit(solution)/shard_map/fetch/pallas_call | solution.py:79
  237.5 8.9 %all-to-all-start.5 = ((bf16[64,8,128]{2,1,0:T(8,128)(2,1)}), bf16[64,8,128]{2,1,0:T(8,128)(2,1)S(1)}, u32[]{:S(2)}, u32[]{:S(2)}) async-start(bf16[64,8,128]{2,1,0:T(8,128)(2,1)} %bitcast.19), calls=%async_computation.5 | async-start | bytes 262144 | tf_op jit(solution)/shard_map/all_to_all | solution.py:418
  246.5 4.0 %within.6 = (bf16[128,1024]{1,0:T(8,128)(2,1)S(1)}, f32[128,1024]{1,0:T(8,128)S(1)}) custom-call(bf16[128,2048]{1,0:T(8,128)(2,1)S(1)} %collective-permute-done.7.x_ref, bf16[2,32,256,512]{3,2,1,0:T(8,128)(2,1)} %bitcast.58, bf16[128,2048]{1,0:T(8,128)(2,1)S(1)} %get-tuple-element.59.kv_ref, f32[144,128]{1,0:T(8,128)S(1)} %get-tuple-element.58.table_ref), custom_call_target="tpu_custom_call" | custom-call | flops 637534208 | bytes 6291456 | tf_op jit(solution)/shard_map/within/pallas_call | solution.py:200
  250.5 7.4 %all-to-all-done.5.state_ref = bf16[64,8,128]{2,1,0:T(8,128)(2,1)S(1)} async-done(((bf16[64,8,128]{2,1,0:T(8,128)(2,1)}), bf16[64,8,128]{2,1,0:T(8,128)(2,1)S(1)}, u32[]{:S(2)}, u32[]{:S(2)}) %all-to-all-start.5) | async-done | bytes 131104 | tf_op jit(solution)/shard_map/all_to_all | solution.py:418
  258.0 16.1 %all_to_all.47 = bf16[64,8,128]{2,1,0:T(8,128)(2,1)S(1)} all-to-all(bf16[64,8,128]{2,1,0:T(8,128)(2,1)S(1)} %carry.6), channel_id=1, replica_groups=mesh['ylo'=2,'core'=2,'yhi'=2,'x'=4,'z'=8] {'yhi','x','z'}, dimensions={0} | all-to-all | bytes 262144 | tf_op jit(solution)/shard_map/all_to_all | solution.py:422
  274.1 3.4 output.6
  277.5 3.5 %collective-permute-start.8 = (bf16[128,2048]{1,0:T(8,128)(2,1)S(1)}, bf16[128,2048]{1,0:T(8,128)(2,1)S(1)}, u32[]{:S(2)}, u32[]{:S(2)}) collective-permute-start(bf16[128,2048]{1,0:T(8,128)(2,1)S(1)} %output.6), channel_id=1, source_target_pairs={{0,128},{32,160},{64,192},{96,224},{1,129},{33,161},{65,193},{97,2... | collective-permute-start | bytes 1572872 | tf_op jit(solution)/shard_map/ppermute | solution.py:351
  281.0 3.7 %fetch.5.buffer = bf16[4,2,32,32,512]{4,3,2,1,0:T(8,128)(2,1)S(1)} custom-call(bf16[2,32,256,512]{3,2,1,0:T(8,128)(2,1)} %bitcast.60), custom_call_target="tpu_custom_call" | custom-call | bytes 16777216 | tf_op jit(solution)/shard_map/fetch/pallas_call | solution.py:79
  284.7 4.9 %collective-permute-done.8.x_ref = bf16[128,2048]{1,0:T(8,128)(2,1)S(1)} collective-permute-done((bf16[128,2048]{1,0:T(8,128)(2,1)S(1)}, bf16[128,2048]{1,0:T(8,128)(2,1)S(1)}, u32[]{:S(2)}, u32[]{:S(2)}) %collective-permute-start.8) | collective-permute-done | bytes 524320 | tf_op jit(solution)/shard_map/ppermute | solution.py:351
  292.5 5.1 %all-to-all-start.7 = ((bf16[64,8,128]{2,1,0:T(8,128)(2,1)}), bf16[64,8,128]{2,1,0:T(8,128)(2,1)S(1)}, u32[]{:S(2)}, u32[]{:S(2)}) async-start(bf16[64,8,128]{2,1,0:T(8,128)(2,1)} %bitcast.21), calls=%async_computation.7 | async-start | bytes 262144 | tf_op jit(solution)/shard_map/all_to_all | solution.py:418
  297.7 4.0 %within.7 = (bf16[128,1024]{1,0:T(8,128)(2,1)S(1)}, f32[128,1024]{1,0:T(8,128)S(1)}) custom-call(bf16[128,2048]{1,0:T(8,128)(2,1)S(1)} %collective-permute-done.8.x_ref, bf16[2,32,256,512]{3,2,1,0:T(8,128)(2,1)} %bitcast.61, bf16[128,2048]{1,0:T(8,128)(2,1)S(1)} %get-tuple-element.67.kv_ref, f32[144,128]{1,0:T(8,128)S(1)} %get-tuple-element.58.table_ref), custom_call_target="tpu_custom_call" | custom-call | flops 637534208 | bytes 6291456 | tf_op jit(solution)/shard_map/within/pallas_call | solution.py:200
  301.7 7.5 %all-to-all-done.7.state_ref = bf16[64,8,128]{2,1,0:T(8,128)(2,1)S(1)} async-done(((bf16[64,8,128]{2,1,0:T(8,128)(2,1)}), bf16[64,8,128]{2,1,0:T(8,128)(2,1)S(1)}, u32[]{:S(2)}, u32[]{:S(2)}) %all-to-all-start.7) | async-done | bytes 131104 | tf_op jit(solution)/shard_map/all_to_all | solution.py:418
  309.3 16.0 %all_to_all.48 = bf16[64,8,128]{2,1,0:T(8,128)(2,1)S(1)} all-to-all(bf16[64,8,128]{2,1,0:T(8,128)(2,1)S(1)} %carry.7), channel_id=1, replica_groups=mesh['ylo'=2,'core'=2,'yhi'=2,'x'=4,'z'=8] {'yhi','x','z'}, dimensions={0} | all-to-all | bytes 262144 | tf_op jit(solution)/shard_map/all_to_all | solution.py:422
  325.4 3.4 output.7
  328.8 5.2 %collective-permute-start.9 = (bf16[128,2048]{1,0:T(8,128)(2,1)S(1)}, bf16[128,2048]{1,0:T(8,128)(2,1)S(1)}, u32[]{:S(2)}, u32[]{:S(2)}) collective-permute-start(bf16[128,2048]{1,0:T(8,128)(2,1)S(1)} %broadcast_select_fusion.2), channel_id=1, source_target_pairs={{0,64},{64,0},{1,65},{65,1},{2,66},{66,2},{3,67},{67,3},{4,68},{68... | collective-permute-start | bytes 1572872 | tf_op jit(solution)/shard_map/ppermute | solution.py:18
  (67 shorter events, 42.7 us)
Async XLA Ops:
  6.5 23.7 %copy-start = (bf16[2,128,2048]{2,1,0:T(8,128)(2,1)S(1)}, bf16[2,128,2048]{2,1,0:T(8,128)(2,1)}, u32[]{:S(2)}) copy-start(bf16[2,128,2048]{2,1,0:T(8,128)(2,1)} %param.4) | copy-start | bytes 3145732
  6.5 118.9 %all-gather.5.cloned.1.call-start = ((), (), s32[]{:S(2)}) async-start(), calls=%async_computation.9 | async-start | bytes 17039360 | tf_op jit(solution)/shard_map/all_gather | solution.py:370
  6.5 1.0 copy-start.2
  7.6 0.8 copy-start.3
  8.4 4.3 %collective-permute-start.2 = (bf16[128,512]{1,0:T(8,128)(2,1)S(1)}, bf16[128,512]{1,0:T(8,128)(2,1)S(1)}, u32[]{:S(2)}, u32[]{:S(2)}) collective-permute-start(bf16[128,512]{1,0:T(8,128)(2,1)S(1)} %get-tuple-element.41), channel_id=1, source_target_pairs={{0,64},{64,0},{1,65},{65,1},{2,66},{66,2},{3,67},{67,3},{4,68},{68... | collective-permute-start | bytes 393224 | tf_op jit(solution)/shard_map/ppermute | solution.py:18
  12.8 4.8 %collective-permute-start.3 = (bf16[128,512]{1,0:T(8,128)(2,1)S(1)}, bf16[128,512]{1,0:T(8,128)(2,1)S(1)}, u32[]{:S(2)}, u32[]{:S(2)}) collective-permute-start(bf16[128,512]{1,0:T(8,128)(2,1)S(1)} %get-tuple-element.83), channel_id=1, source_target_pairs={{0,128},{128,0},{1,129},{129,1},{2,130},{130,2},{3,131},{131,3},{4... | collective-permute-start | bytes 393224 | tf_op jit(solution)/shard_map/ppermute | solution.py:311
  12.9 8.3 %collective-permute-start.4 = (bf16[128,512]{1,0:T(8,128)(2,1)S(1)}, bf16[128,512]{1,0:T(8,128)(2,1)S(1)}, u32[]{:S(2)}, u32[]{:S(2)}) collective-permute-start(bf16[128,512]{1,0:T(8,128)(2,1)S(1)} %get-tuple-element.84), channel_id=1, source_target_pairs={{0,32},{32,0},{1,33},{33,1},{2,34},{34,2},{3,35},{35,3},{4,36},{36... | collective-permute-start | bytes 393224 | tf_op jit(solution)/shard_map/ppermute | solution.py:311
  15.0 8.6 %collective-permute-start.5 = (bf16[128,512]{1,0:T(8,128)(2,1)S(1)}, bf16[128,512]{1,0:T(8,128)(2,1)S(1)}, u32[]{:S(2)}, u32[]{:S(2)}) collective-permute-start(bf16[128,512]{1,0:T(8,128)(2,1)S(1)} %get-tuple-element.83), channel_id=1, source_target_pairs={{0,160},{32,128},{128,32},{160,0},{1,161},{33,129},{129,33},{161,1... | collective-permute-start | bytes 393224 | tf_op jit(solution)/shard_map/ppermute | solution.py:311
  24.4 206.5 %all-gather.7.cloned.1.call-start = ((), (), s32[]{:S(2)}) async-start(), calls=%async_computation.10 | async-start | bytes 17039360 | tf_op jit(solution)/shard_map/all_gather | solution.py:370
  26.0 1.8 collective-permute-start
  28.5 2.5 collective-permute-start.1
  34.5 22.8 %all-to-all-start = ((f32[64,2,128]{2,1,0:T(2,128)}), f32[64,2,128]{2,1,0:T(2,128)S(1)}, u32[]{:S(2)}, u32[]{:S(2)}) async-start(f32[64,2,128]{2,1,0:T(2,128)} %pad_maximum_fusion.2), calls=%async_computation | async-start | bytes 131072 | tf_op jit(solution)/shard_map/all_to_all | solution.py:393
  130.4 21.5 %all-to-all-start.1 = ((bf16[64,8,128]{2,1,0:T(8,128)(2,1)}), bf16[64,8,128]{2,1,0:T(8,128)(2,1)S(1)}, u32[]{:S(2)}, u32[]{:S(2)}) async-start(bf16[64,8,128]{2,1,0:T(8,128)(2,1)} %bitcast.13), calls=%async_computation.1 | async-start | bytes 262144 | tf_op jit(solution)/shard_map/all_to_all | solution.py:418
  172.3 9.1 %collective-permute-start.6 = (bf16[128,2048]{1,0:T(8,128)(2,1)S(1)}, bf16[128,2048]{1,0:T(8,128)(2,1)S(1)}, u32[]{:S(2)}, u32[]{:S(2)}) collective-permute-start(bf16[128,2048]{1,0:T(8,128)(2,1)S(1)} %output.4), channel_id=1, source_target_pairs={{0,128},{32,160},{64,224},{96,192},{1,129},{33,161},{65,225},{97,1... | collective-permute-start | bytes 1572872 | tf_op jit(solution)/shard_map/ppermute | solution.py:351
  184.3 17.2 %all-to-all-start.3 = ((bf16[64,8,128]{2,1,0:T(8,128)(2,1)}), bf16[64,8,128]{2,1,0:T(8,128)(2,1)S(1)}, u32[]{:S(2)}, u32[]{:S(2)}) async-start(bf16[64,8,128]{2,1,0:T(8,128)(2,1)} %bitcast.16), calls=%async_computation.3 | async-start | bytes 262144 | tf_op jit(solution)/shard_map/all_to_all | solution.py:418
  221.7 12.9 %collective-permute-start.7 = (bf16[128,2048]{1,0:T(8,128)(2,1)S(1)}, bf16[128,2048]{1,0:T(8,128)(2,1)S(1)}, u32[]{:S(2)}, u32[]{:S(2)}) collective-permute-start(bf16[128,2048]{1,0:T(8,128)(2,1)S(1)} %output.5), channel_id=1, source_target_pairs={{128,0},{160,32},{192,96},{224,64},{129,1},{161,33},{193,97},{225,... | collective-permute-start | bytes 1572872 | tf_op jit(solution)/shard_map/ppermute | solution.py:351
  237.5 20.3 %all-to-all-start.5 = ((bf16[64,8,128]{2,1,0:T(8,128)(2,1)}), bf16[64,8,128]{2,1,0:T(8,128)(2,1)S(1)}, u32[]{:S(2)}, u32[]{:S(2)}) async-start(bf16[64,8,128]{2,1,0:T(8,128)(2,1)} %bitcast.19), calls=%async_computation.5 | async-start | bytes 262144 | tf_op jit(solution)/shard_map/all_to_all | solution.py:418
  277.5 12.2 %collective-permute-start.8 = (bf16[128,2048]{1,0:T(8,128)(2,1)S(1)}, bf16[128,2048]{1,0:T(8,128)(2,1)S(1)}, u32[]{:S(2)}, u32[]{:S(2)}) collective-permute-start(bf16[128,2048]{1,0:T(8,128)(2,1)S(1)} %output.6), channel_id=1, source_target_pairs={{0,128},{32,160},{64,192},{96,224},{1,129},{33,161},{65,193},{97,2... | collective-permute-start | bytes 1572872 | tf_op jit(solution)/shard_map/ppermute | solution.py:351
  292.5 16.6 %all-to-all-start.7 = ((bf16[64,8,128]{2,1,0:T(8,128)(2,1)}), bf16[64,8,128]{2,1,0:T(8,128)(2,1)S(1)}, u32[]{:S(2)}, u32[]{:S(2)}) async-start(bf16[64,8,128]{2,1,0:T(8,128)(2,1)} %bitcast.21), calls=%async_computation.7 | async-start | bytes 262144 | tf_op jit(solution)/shard_map/all_to_all | solution.py:418
  325.4 11.4 %copy-start.1 = (bf16[2,128,2048]{2,1,0:T(8,128)(2,1)S(1)}, bf16[2,128,2048]{2,1,0:T(8,128)(2,1)}, u32[]{:S(2)}) copy-start(bf16[2,128,2048]{2,1,0:T(8,128)(2,1)} %param.4) | copy-start | bytes 3145732
  328.8 6.7 %collective-permute-start.9 = (bf16[128,2048]{1,0:T(8,128)(2,1)S(1)}, bf16[128,2048]{1,0:T(8,128)(2,1)S(1)}, u32[]{:S(2)}, u32[]{:S(2)}) collective-permute-start(bf16[128,2048]{1,0:T(8,128)(2,1)S(1)} %broadcast_select_fusion.2), channel_id=1, source_target_pairs={{0,64},{64,0},{1,65},{65,1},{2,66},{66,2},{3,67},{67,3},{4,68},{68... | collective-permute-start | bytes 1572872 | tf_op jit(solution)/shard_map/ppermute | solution.py:18
Sparse Core Ops, SparseCore 0:
  24.6 100.8 all-gather.4
  128.2 102.7 all-gather.6

commit v7 on v6

--- a/solution.py
+++ b/solution.py
@@ -8,7 +8,7 @@
 from jax.sharding import Mesh, PartitionSpec as P
 
 CTX = ("yhi", "x", "z")
-SPREAD = ("core", "x", "z")
+SPREAD = ("x", "z", "core")
 NB = 512
 EPS = 1e-05
 VMEM_KEPT = 50 * 2**20
@@ -33,7 +33,7 @@
         block, at = [], 0
         for side, first, column, count in parts:
             for far in range(2):
-                source = w_ref.at[side, :, pl.ds(far * stride + first, rows), pl.ds(column, count)]
+                source = w_ref.at[:, side, pl.ds(far * stride + first, rows), pl.ds(column, count)]
                 goal = buffer.at[k, far, :, :, pl.ds(at, count)]
                 block.append(pltpu.make_async_copy(source, goal, sems.at[k, len(block)]))
             at += count
@@ -367,7 +367,7 @@
         own = jnp.concatenate(
             [jnp.where(place == 0, pair[0], pair[1]), jnp.where(place == 0, pair[1], pair[0])], axis=0
         )
-        gathered.append(lax.all_gather(own, SPREAD, axis=0).reshape(2, -1, own.shape[0], NB))
+        gathered.append(lax.all_gather(own, SPREAD, axis=0).reshape(-1, 2, own.shape[0], NB))
     return gathered
 
 

time: 345 us -> 345 us (level)
  no operation moved by 1% of the time
where the time goes in v7:
time: 345 us; the launch traced here: 344 us
  waiting for transfers between devices  137 us (40%)
  blocking collectives  65.6 us (19%)
  starting transfers between devices  62 us (18%)
  Pallas kernels  55.4 us (16%)
  between operations  13.6 us (4%)
  other arithmetic  5.17 us (1%)
    all_gather x2, waiting for transfers between devices, shared_weights(): lax.all_gather(own, SPREAD, axis=0).reshape(-1, 2, own.shape[0], NB)  76.1 us
    all_to_all x4, blocking collectives, shards(): carried = lax.all_to_all(mine, CTX, 0, 0, tiled=True).reshape(state.shape)  65.6 us
    all_to_all x4, waiting for transfers between devices, shards(): lax.all_to_all(state.reshape(blocks, -1, 128), CTX, 0, 0, tiled=True)  32.1 us
    all_to_all x4, starting transfers between devices, shards(): lax.all_to_all(state.reshape(blocks, -1, 128), CTX, 0, 0, tiled=True)  27.7 us
    pallas_call x4, Pallas kernels, within(): pl.pallas_call(functools.partial(within_kernel, blocks), in_specs=[vmem,...  16.2 us
    pallas_call x4, Pallas kernels, project_keys(): pl.pallas_call(fetched_keys_kernel if fetched else functools.partial(keys...  13.6 us
    pallas_call x4, Pallas kernels, output(): pl.pallas_call(functools.partial(output_kernel, blocks), in_specs=[vmem]...  13.5 us
    all_to_all x1, starting transfers between devices, decays(): received = lax.all_to_all(sent, CTX, 0, 0, tiled=True)  11.7 us
  transfers between devices with their start and end apart: 17, of which 16 were waited for; matrix products, arithmetic and copies ran while one was open for 2% of the time, Pallas kernels for 12%

profile of v7, /device:TPU:1, one launch (start us, length us, event | category | flops | bytes accessed | tf_op | source)
XLA Modules:
  0.0 343.6 jit_solution(16758833632268222087)
XLA Ops:
  8.4 3.3 collective-permute-start.2
  17.6 3.6 %collective-permute-done.4 = bf16[128,512]{1,0:T(8,128)(2,1)S(1)} collective-permute-done((bf16[128,512]{1,0:T(8,128)(2,1)S(1)}, bf16[128,512]{1,0:T(8,128)(2,1)S(1)}, u32[]{:S(2)}, u32[]{:S(2)}) %collective-permute-start.4) | collective-permute-done | bytes 131104 | tf_op jit(solution)/shard_map/ppermute | solution.py:311
  34.5 11.7 %all-to-all-start = ((f32[64,2,128]{2,1,0:T(2,128)}), f32[64,2,128]{2,1,0:T(2,128)S(1)}, u32[]{:S(2)}, u32[]{:S(2)}) async-start(f32[64,2,128]{2,1,0:T(2,128)} %pad_maximum_fusion.2), calls=%async_computation | async-start | bytes 131072 | tf_op jit(solution)/shard_map/all_to_all | solution.py:393
  46.5 10.8 %all-to-all-done = f32[64,2,128]{2,1,0:T(2,128)S(1)} async-done(((f32[64,2,128]{2,1,0:T(2,128)}), f32[64,2,128]{2,1,0:T(2,128)S(1)}, u32[]{:S(2)}, u32[]{:S(2)}) %all-to-all-start) | async-done | bytes 65568 | tf_op jit(solution)/shard_map/all_to_all | solution.py:393
  57.3 68.1 %all-gather.5.cloned.1.call-done = bf16[16384,512]{1,0:T(8,128)(2,1)} async-done(((bf16[256,512]{1,0:T(8,128)(2,1)}), bf16[16384,512]{1,0:T(8,128)(2,1)}) %all-gather.5.cloned.1.call-update) | async-done | bytes 16777232 | tf_op jit(solution)/shard_map/all_gather | solution.py:370
  125.5 4.9 %keys.4 = (bf16[128,2048]{1,0:T(8,128)(2,1)S(1)}, bf16[512,128]{1,0:T(8,128)(2,1)}) custom-call(bf16[128,2048]{1,0:T(8,128)(2,1)S(1)} %dynamic-slice_bitcast_fusion.x_ref, bf16[32,2,256,512]{3,2,1,0:T(8,128)(2,1)} %bitcast.63, f32[144,128]{1,0:T(8,128)S(1)} %get-tuple-element.42.table_ref), custom_call_target="tpu_custom_call" | custom-call | flops 1073741824 | bytes 8388608 | tf_op jit(solution)/shard_map/keys/pallas_call | solution.py:137
  130.4 8.4 %all-to-all-start.1 = ((bf16[64,8,128]{2,1,0:T(8,128)(2,1)}), bf16[64,8,128]{2,1,0:T(8,128)(2,1)S(1)}, u32[]{:S(2)}, u32[]{:S(2)}) async-start(bf16[64,8,128]{2,1,0:T(8,128)(2,1)} %bitcast.13), calls=%async_computation.1 | async-start | bytes 262144 | tf_op jit(solution)/shard_map/all_to_all | solution.py:418
  138.8 4.0 %within.4 = (bf16[128,1024]{1,0:T(8,128)(2,1)S(1)}, f32[128,1024]{1,0:T(8,128)S(1)}) custom-call(bf16[128,2048]{1,0:T(8,128)(2,1)S(1)} %dynamic-slice_bitcast_fusion.x_ref, bf16[32,2,256,512]{3,2,1,0:T(8,128)(2,1)} %bitcast.64, bf16[128,2048]{1,0:T(8,128)(2,1)S(1)} %get-tuple-element.43.kv_ref, f32[144,128]{1,0:T(8,128)S(1)} %get-tuple-element.42.table_ref), custom_call_target="tpu_custom_call" | custom-call | flops 637534208 | bytes 6291456 | tf_op jit(solution)/shard_map/within/pallas_call | solution.py:200
  142.8 9.2 %all-to-all-done.1.state_ref = bf16[64,8,128]{2,1,0:T(8,128)(2,1)S(1)} async-done(((bf16[64,8,128]{2,1,0:T(8,128)(2,1)}), bf16[64,8,128]{2,1,0:T(8,128)(2,1)S(1)}, u32[]{:S(2)}, u32[]{:S(2)}) %all-to-all-start.1) | async-done | bytes 131104 | tf_op jit(solution)/shard_map/all_to_all | solution.py:418
  152.1 16.9 %all_to_all.45 = bf16[64,8,128]{2,1,0:T(8,128)(2,1)S(1)} all-to-all(bf16[64,8,128]{2,1,0:T(8,128)(2,1)S(1)} %carry.4), channel_id=1, replica_groups=mesh['ylo'=2,'core'=2,'yhi'=2,'x'=4,'z'=8] {'yhi','x','z'}, dimensions={0} | all-to-all | bytes 262144 | tf_op jit(solution)/shard_map/all_to_all | solution.py:422
  169.0 3.4 output.4
  175.2 4.2 %fetch.3.buffer = bf16[4,2,32,32,512]{4,3,2,1,0:T(8,128)(2,1)S(1)} custom-call(bf16[32,2,256,512]{3,2,1,0:T(8,128)(2,1)} %bitcast.66), custom_call_target="tpu_custom_call" | custom-call | bytes 16777216 | tf_op jit(solution)/shard_map/fetch/pallas_call | solution.py:79
  184.2 5.2 %all-to-all-start.3 = ((bf16[64,8,128]{2,1,0:T(8,128)(2,1)}), bf16[64,8,128]{2,1,0:T(8,128)(2,1)S(1)}, u32[]{:S(2)}, u32[]{:S(2)}) async-start(bf16[64,8,128]{2,1,0:T(8,128)(2,1)} %bitcast.16), calls=%async_computation.3 | async-start | bytes 262144 | tf_op jit(solution)/shard_map/all_to_all | solution.py:418
  189.4 4.2 %within.5 = (bf16[128,1024]{1,0:T(8,128)(2,1)S(1)}, f32[128,1024]{1,0:T(8,128)S(1)}) custom-call(bf16[128,2048]{1,0:T(8,128)(2,1)S(1)} %collective-permute-done.6.x_ref, bf16[32,2,256,512]{3,2,1,0:T(8,128)(2,1)} %bitcast.67, bf16[128,2048]{1,0:T(8,128)(2,1)S(1)} %get-tuple-element.51.kv_ref, f32[144,128]{1,0:T(8,128)S(1)} %get-tuple-element.42.table_ref), custom_call_target="tpu_custom_call" | custom-call | flops 637534208 | bytes 6291456 | tf_op jit(solution)/shard_map/within/pallas_call | solution.py:200
  193.6 8.1 %all-to-all-done.3.state_ref = bf16[64,8,128]{2,1,0:T(8,128)(2,1)S(1)} async-done(((bf16[64,8,128]{2,1,0:T(8,128)(2,1)}), bf16[64,8,128]{2,1,0:T(8,128)(2,1)S(1)}, u32[]{:S(2)}, u32[]{:S(2)}) %all-to-all-start.3) | async-done | bytes 131104 | tf_op jit(solution)/shard_map/all_to_all | solution.py:418
  201.8 16.6 %all_to_all.46 = bf16[64,8,128]{2,1,0:T(8,128)(2,1)S(1)} all-to-all(bf16[64,8,128]{2,1,0:T(8,128)(2,1)S(1)} %carry.5), channel_id=1, replica_groups=mesh['ylo'=2,'core'=2,'yhi'=2,'x'=4,'z'=8] {'yhi','x','z'}, dimensions={0} | all-to-all | bytes 262144 | tf_op jit(solution)/shard_map/all_to_all | solution.py:422
  218.4 3.4 %output.5 = bf16[128,2048]{1,0:T(8,128)(2,1)S(1)} custom-call(bf16[128,1024]{1,0:T(8,128)(2,1)S(1)} %get-tuple-element.52.q_ref, bf16[512,128]{1,0:T(8,128)(2,1)S(1)} %bitcast.47, f32[144,128]{1,0:T(8,128)S(1)} %get-tuple-element.42.table_ref, f32[128,1024]{1,0:T(8,128)S(1)} %get-tuple-element.56.within_ref, ...), custom_call_target="tpu_custom_call" | custom-call | flops 536870912 | bytes 4194304 | tf_op jit(solution)/shard_map/output/pallas_call | solution.py:286
  223.2 7.9 %all-gather.7.cloned.1.call-done = bf16[16384,512]{1,0:T(8,128)(2,1)} async-done(((bf16[256,512]{1,0:T(8,128)(2,1)}), bf16[16384,512]{1,0:T(8,128)(2,1)}) %all-gather.7.cloned.1.call-update) | async-done | bytes 16777232 | tf_op jit(solution)/shard_map/all_gather | solution.py:370
  231.1 3.7 %fetch.4.buffer = bf16[4,2,32,32,512]{4,3,2,1,0:T(8,128)(2,1)S(1)} custom-call(bf16[32,2,256,512]{3,2,1,0:T(8,128)(2,1)} %bitcast.57), custom_call_target="tpu_custom_call" | custom-call | bytes 16777216 | tf_op jit(solution)/shard_map/fetch/pallas_call | solution.py:79
  237.7 9.0 %all-to-all-start.5 = ((bf16[64,8,128]{2,1,0:T(8,128)(2,1)}), bf16[64,8,128]{2,1,0:T(8,128)(2,1)S(1)}, u32[]{:S(2)}, u32[]{:S(2)}) async-start(bf16[64,8,128]{2,1,0:T(8,128)(2,1)} %bitcast.19), calls=%async_computation.5 | async-start | bytes 262144 | tf_op jit(solution)/shard_map/all_to_all | solution.py:418
  246.7 4.0 %within.6 = (bf16[128,1024]{1,0:T(8,128)(2,1)S(1)}, f32[128,1024]{1,0:T(8,128)S(1)}) custom-call(bf16[128,2048]{1,0:T(8,128)(2,1)S(1)} %collective-permute-done.7.x_ref, bf16[32,2,256,512]{3,2,1,0:T(8,128)(2,1)} %bitcast.58, bf16[128,2048]{1,0:T(8,128)(2,1)S(1)} %get-tuple-element.59.kv_ref, f32[144,128]{1,0:T(8,128)S(1)} %get-tuple-element.58.table_ref), custom_call_target="tpu_custom_call" | custom-call | flops 637534208 | bytes 6291456 | tf_op jit(solution)/shard_map/within/pallas_call | solution.py:200
  250.7 7.4 %all-to-all-done.5.state_ref = bf16[64,8,128]{2,1,0:T(8,128)(2,1)S(1)} async-done(((bf16[64,8,128]{2,1,0:T(8,128)(2,1)}), bf16[64,8,128]{2,1,0:T(8,128)(2,1)S(1)}, u32[]{:S(2)}, u32[]{:S(2)}) %all-to-all-start.5) | async-done | bytes 131104 | tf_op jit(solution)/shard_map/all_to_all | solution.py:418
  258.2 16.1 %all_to_all.47 = bf16[64,8,128]{2,1,0:T(8,128)(2,1)S(1)} all-to-all(bf16[64,8,128]{2,1,0:T(8,128)(2,1)S(1)} %carry.6), channel_id=1, replica_groups=mesh['ylo'=2,'core'=2,'yhi'=2,'x'=4,'z'=8] {'yhi','x','z'}, dimensions={0} | all-to-all | bytes 262144 | tf_op jit(solution)/shard_map/all_to_all | solution.py:422
  274.3 3.4 output.6
  281.0 3.7 %fetch.5.buffer = bf16[4,2,32,32,512]{4,3,2,1,0:T(8,128)(2,1)S(1)} custom-call(bf16[32,2,256,512]{3,2,1,0:T(8,128)(2,1)} %bitcast.60), custom_call_target="tpu_custom_call" | custom-call | bytes 16777216 | tf_op jit(solution)/shard_map/fetch/pallas_call | solution.py:79
  284.7 4.9 %collective-permute-done.8.x_ref = bf16[128,2048]{1,0:T(8,128)(2,1)S(1)} collective-permute-done((bf16[128,2048]{1,0:T(8,128)(2,1)S(1)}, bf16[128,2048]{1,0:T(8,128)(2,1)S(1)}, u32[]{:S(2)}, u32[]{:S(2)}) %collective-permute-start.8) | collective-permute-done | bytes 524320 | tf_op jit(solution)/shard_map/ppermute | solution.py:351
  292.5 5.1 %all-to-all-start.7 = ((bf16[64,8,128]{2,1,0:T(8,128)(2,1)}), bf16[64,8,128]{2,1,0:T(8,128)(2,1)S(1)}, u32[]{:S(2)}, u32[]{:S(2)}) async-start(bf16[64,8,128]{2,1,0:T(8,128)(2,1)} %bitcast.21), calls=%async_computation.7 | async-start | bytes 262144 | tf_op jit(solution)/shard_map/all_to_all | solution.py:418
  297.7 4.0 %within.7 = (bf16[128,1024]{1,0:T(8,128)(2,1)S(1)}, f32[128,1024]{1,0:T(8,128)S(1)}) custom-call(bf16[128,2048]{1,0:T(8,128)(2,1)S(1)} %collective-permute-done.8.x_ref, bf16[32,2,256,512]{3,2,1,0:T(8,128)(2,1)} %bitcast.61, bf16[128,2048]{1,0:T(8,128)(2,1)S(1)} %get-tuple-element.67.kv_ref, f32[144,128]{1,0:T(8,128)S(1)} %get-tuple-element.58.table_ref), custom_call_target="tpu_custom_call" | custom-call | flops 637534208 | bytes 6291456 | tf_op jit(solution)/shard_map/within/pallas_call | solution.py:200
  301.7 7.5 %all-to-all-done.7.state_ref = bf16[64,8,128]{2,1,0:T(8,128)(2,1)S(1)} async-done(((bf16[64,8,128]{2,1,0:T(8,128)(2,1)}), bf16[64,8,128]{2,1,0:T(8,128)(2,1)S(1)}, u32[]{:S(2)}, u32[]{:S(2)}) %all-to-all-start.7) | async-done | bytes 131104 | tf_op jit(solution)/shard_map/all_to_all | solution.py:418
  309.3 16.0 %all_to_all.48 = bf16[64,8,128]{2,1,0:T(8,128)(2,1)S(1)} all-to-all(bf16[64,8,128]{2,1,0:T(8,128)(2,1)S(1)} %carry.7), channel_id=1, replica_groups=mesh['ylo'=2,'core'=2,'yhi'=2,'x'=4,'z'=8] {'yhi','x','z'}, dimensions={0} | all-to-all | bytes 262144 | tf_op jit(solution)/shard_map/all_to_all | solution.py:422
  325.3 3.4 output.7
  328.8 5.2 %collective-permute-start.9 = (bf16[128,2048]{1,0:T(8,128)(2,1)S(1)}, bf16[128,2048]{1,0:T(8,128)(2,1)S(1)}, u32[]{:S(2)}, u32[]{:S(2)}) collective-permute-start(bf16[128,2048]{1,0:T(8,128)(2,1)S(1)} %broadcast_select_fusion.2), channel_id=1, source_target_pairs={{0,64},{64,0},{1,65},{65,1},{2,66},{66,2},{3,67},{67,3},{4,68},{68... | collective-permute-start | bytes 1572872 | tf_op jit(solution)/shard_map/ppermute | solution.py:18
  (67 shorter events, 42.9 us)
Async XLA Ops:
  6.5 23.7 %copy-start = (bf16[2,128,2048]{2,1,0:T(8,128)(2,1)S(1)}, bf16[2,128,2048]{2,1,0:T(8,128)(2,1)}, u32[]{:S(2)}) copy-start(bf16[2,128,2048]{2,1,0:T(8,128)(2,1)} %param.4) | copy-start | bytes 3145732
  6.5 118.9 %all-gather.5.cloned.1.call-start = ((), (), s32[]{:S(2)}) async-start(), calls=%async_computation.9 | async-start | bytes 17039360 | tf_op jit(solution)/shard_map/all_gather | solution.py:370
  6.5 1.0 copy-start.2
  7.6 0.8 copy-start.3
  8.4 4.3 %collective-permute-start.2 = (bf16[128,512]{1,0:T(8,128)(2,1)S(1)}, bf16[128,512]{1,0:T(8,128)(2,1)S(1)}, u32[]{:S(2)}, u32[]{:S(2)}) collective-permute-start(bf16[128,512]{1,0:T(8,128)(2,1)S(1)} %get-tuple-element.41), channel_id=1, source_target_pairs={{0,64},{64,0},{1,65},{65,1},{2,66},{66,2},{3,67},{67,3},{4,68},{68... | collective-permute-start | bytes 393224 | tf_op jit(solution)/shard_map/ppermute | solution.py:18
  12.8 4.8 %collective-permute-start.3 = (bf16[128,512]{1,0:T(8,128)(2,1)S(1)}, bf16[128,512]{1,0:T(8,128)(2,1)S(1)}, u32[]{:S(2)}, u32[]{:S(2)}) collective-permute-start(bf16[128,512]{1,0:T(8,128)(2,1)S(1)} %get-tuple-element.83), channel_id=1, source_target_pairs={{0,128},{128,0},{1,129},{129,1},{2,130},{130,2},{3,131},{131,3},{4... | collective-permute-start | bytes 393224 | tf_op jit(solution)/shard_map/ppermute | solution.py:311
  12.9 8.3 %collective-permute-start.4 = (bf16[128,512]{1,0:T(8,128)(2,1)S(1)}, bf16[128,512]{1,0:T(8,128)(2,1)S(1)}, u32[]{:S(2)}, u32[]{:S(2)}) collective-permute-start(bf16[128,512]{1,0:T(8,128)(2,1)S(1)} %get-tuple-element.84), channel_id=1, source_target_pairs={{0,32},{32,0},{1,33},{33,1},{2,34},{34,2},{3,35},{35,3},{4,36},{36... | collective-permute-start | bytes 393224 | tf_op jit(solution)/shard_map/ppermute | solution.py:311
  15.0 8.6 %collective-permute-start.5 = (bf16[128,512]{1,0:T(8,128)(2,1)S(1)}, bf16[128,512]{1,0:T(8,128)(2,1)S(1)}, u32[]{:S(2)}, u32[]{:S(2)}) collective-permute-start(bf16[128,512]{1,0:T(8,128)(2,1)S(1)} %get-tuple-element.83), channel_id=1, source_target_pairs={{0,160},{32,128},{128,32},{160,0},{1,161},{33,129},{129,33},{161,1... | collective-permute-start | bytes 393224 | tf_op jit(solution)/shard_map/ppermute | solution.py:311
  24.4 206.7 %all-gather.7.cloned.1.call-start = ((), (), s32[]{:S(2)}) async-start(), calls=%async_computation.10 | async-start | bytes 17039360 | tf_op jit(solution)/shard_map/all_gather | solution.py:370
  26.0 1.8 collective-permute-start
  28.5 2.5 collective-permute-start.1
  34.5 22.8 %all-to-all-start = ((f32[64,2,128]{2,1,0:T(2,128)}), f32[64,2,128]{2,1,0:T(2,128)S(1)}, u32[]{:S(2)}, u32[]{:S(2)}) async-start(f32[64,2,128]{2,1,0:T(2,128)} %pad_maximum_fusion.2), calls=%async_computation | async-start | bytes 131072 | tf_op jit(solution)/shard_map/all_to_all | solution.py:393
  130.4 21.6 %all-to-all-start.1 = ((bf16[64,8,128]{2,1,0:T(8,128)(2,1)}), bf16[64,8,128]{2,1,0:T(8,128)(2,1)S(1)}, u32[]{:S(2)}, u32[]{:S(2)}) async-start(bf16[64,8,128]{2,1,0:T(8,128)(2,1)} %bitcast.13), calls=%async_computation.1 | async-start | bytes 262144 | tf_op jit(solution)/shard_map/all_to_all | solution.py:418
  172.3 8.9 %collective-permute-start.6 = (bf16[128,2048]{1,0:T(8,128)(2,1)S(1)}, bf16[128,2048]{1,0:T(8,128)(2,1)S(1)}, u32[]{:S(2)}, u32[]{:S(2)}) collective-permute-start(bf16[128,2048]{1,0:T(8,128)(2,1)S(1)} %output.4), channel_id=1, source_target_pairs={{0,128},{32,160},{64,224},{96,192},{1,129},{33,161},{65,225},{97,1... | collective-permute-start | bytes 1572872 | tf_op jit(solution)/shard_map/ppermute | solution.py:351
  184.2 17.5 %all-to-all-start.3 = ((bf16[64,8,128]{2,1,0:T(8,128)(2,1)}), bf16[64,8,128]{2,1,0:T(8,128)(2,1)S(1)}, u32[]{:S(2)}, u32[]{:S(2)}) async-start(bf16[64,8,128]{2,1,0:T(8,128)(2,1)} %bitcast.16), calls=%async_computation.3 | async-start | bytes 262144 | tf_op jit(solution)/shard_map/all_to_all | solution.py:418
  221.9 12.9 %collective-permute-start.7 = (bf16[128,2048]{1,0:T(8,128)(2,1)S(1)}, bf16[128,2048]{1,0:T(8,128)(2,1)S(1)}, u32[]{:S(2)}, u32[]{:S(2)}) collective-permute-start(bf16[128,2048]{1,0:T(8,128)(2,1)S(1)} %output.5), channel_id=1, source_target_pairs={{128,0},{160,32},{192,96},{224,64},{129,1},{161,33},{193,97},{225,... | collective-permute-start | bytes 1572872 | tf_op jit(solution)/shard_map/ppermute | solution.py:351
  237.7 20.4 %all-to-all-start.5 = ((bf16[64,8,128]{2,1,0:T(8,128)(2,1)}), bf16[64,8,128]{2,1,0:T(8,128)(2,1)S(1)}, u32[]{:S(2)}, u32[]{:S(2)}) async-start(bf16[64,8,128]{2,1,0:T(8,128)(2,1)} %bitcast.19), calls=%async_computation.5 | async-start | bytes 262144 | tf_op jit(solution)/shard_map/all_to_all | solution.py:418
  277.7 11.9 %collective-permute-start.8 = (bf16[128,2048]{1,0:T(8,128)(2,1)S(1)}, bf16[128,2048]{1,0:T(8,128)(2,1)S(1)}, u32[]{:S(2)}, u32[]{:S(2)}) collective-permute-start(bf16[128,2048]{1,0:T(8,128)(2,1)S(1)} %output.6), channel_id=1, source_target_pairs={{0,128},{32,160},{64,192},{96,224},{1,129},{33,161},{65,193},{97,2... | collective-permute-start | bytes 1572872 | tf_op jit(solution)/shard_map/ppermute | solution.py:351
  292.5 16.6 %all-to-all-start.7 = ((bf16[64,8,128]{2,1,0:T(8,128)(2,1)}), bf16[64,8,128]{2,1,0:T(8,128)(2,1)S(1)}, u32[]{:S(2)}, u32[]{:S(2)}) async-start(bf16[64,8,128]{2,1,0:T(8,128)(2,1)} %bitcast.21), calls=%async_computation.7 | async-start | bytes 262144 | tf_op jit(solution)/shard_map/all_to_all | solution.py:418
  325.3 11.4 %copy-start.1 = (bf16[2,128,2048]{2,1,0:T(8,128)(2,1)S(1)}, bf16[2,128,2048]{2,1,0:T(8,128)(2,1)}, u32[]{:S(2)}) copy-start(bf16[2,128,2048]{2,1,0:T(8,128)(2,1)} %param.4) | copy-start | bytes 3145732
  328.8 6.7 %collective-permute-start.9 = (bf16[128,2048]{1,0:T(8,128)(2,1)S(1)}, bf16[128,2048]{1,0:T(8,128)(2,1)S(1)}, u32[]{:S(2)}, u32[]{:S(2)}) collective-permute-start(bf16[128,2048]{1,0:T(8,128)(2,1)S(1)} %broadcast_select_fusion.2), channel_id=1, source_target_pairs={{0,64},{64,0},{1,65},{65,1},{2,66},{66,2},{3,67},{67,3},{4,68},{68... | collective-permute-start | bytes 1572872 | tf_op jit(solution)/shard_map/ppermute | solution.py:18
Sparse Core Ops, SparseCore 0:
  24.6 100.8 all-gather.4
  128.3 102.8 all-gather.6

commit v8 on v7

--- a/solution.py
+++ b/solution.py
@@ -424,7 +424,9 @@
         kept.append(x)
     first = jnp.where(level == 0, kept[0], kept[5])
     second = jnp.where(level == 0, kept[3], kept[6])
-    other = swap(jnp.where(core == 0, second, first), "core")
+    early = lax.ppermute(first, "core", [(1, 0)])
+    late = lax.ppermute(second, "core", [(0, 1)])
+    other = jnp.where(core == 0, early, late)
     result = jnp.stack([jnp.where(core == 0, first, other), jnp.where(core == 0, other, second)])
     return result[None]
 

time: 345 us -> 348 us (level)
  blocking collectives: 65.6 us -> 49.6 us
  waiting for transfers between devices: 137 us -> 146 us
  starting transfers between devices: 62 us -> 69.9 us
    all_to_all x4 -> x3, blocking collectives: 65.6 us -> 49.6 us  [shards(): carried = lax.all_to_all(mine, CTX, 0, 0, tiled=True).reshape(state.shape)]
    ppermute x0 -> x2, starting transfers between devices: none -> 8.34 us  [the longest x1 7.05 us: shards(): early = lax.ppermute(first, 'core', [(1, 0)])]
    ppermute x0 -> x2, waiting for transfers between devices: none -> 6.87 us  [the longest x1 6.87 us: shards(): late = lax.ppermute(second, 'core', [(0, 1)])]
    ppermute x3 -> x2, starting transfers between devices: 9.52 us -> 4.34 us  [swap(): return lax.ppermute(value, axis, [(0, 1), (1, 0)])]
    all_to_all x0 -> x1, starting transfers between devices: none -> 4.76 us  [shards(): carried = lax.all_to_all(mine, CTX, 0, 0, tiled=True).reshape(state.shape)]
    all_to_all x0 -> x1, waiting for transfers between devices: none -> 3.6 us  [shards(): carried = lax.all_to_all(mine, CTX, 0, 0, tiled=True).reshape(state.shape)]
  transfers between devices with their start and end apart: 17 -> 19, of which waited for: 16 -> 17; matrix products, arithmetic and copies ran while one was open for 2% -> 2% of each run, Pallas kernels for 12% -> 13%
where the time goes in v8:
time: 348 us; the launch traced here: 347 us
  waiting for transfers between devices  146 us (42%)
  starting transfers between devices  69.9 us (20%)
  Pallas kernels  56 us (16%)
  blocking collectives  49.6 us (14%)
  between operations  13.7 us (4%)
  other arithmetic  5.92 us (2%)
  local copies, waits for them, and re-layouts  4.16 us (1%)
    all_gather x2, waiting for transfers between devices, shared_weights(): lax.all_gather(own, SPREAD, axis=0).reshape(-1, 2, own.shape[0], NB)  75.9 us
    all_to_all x3, blocking collectives, shards(): carried = lax.all_to_all(mine, CTX, 0, 0, tiled=True).reshape(state.shape)  49.6 us
    all_to_all x4, waiting for transfers between devices, shards(): lax.all_to_all(state.reshape(blocks, -1, 128), CTX, 0, 0, tiled=True)  32.1 us
    all_to_all x4, starting transfers between devices, shards(): lax.all_to_all(state.reshape(blocks, -1, 128), CTX, 0, 0, tiled=True)  27.7 us
    pallas_call x4, Pallas kernels, within(): pl.pallas_call(functools.partial(within_kernel, blocks), in_specs=[vmem,...  16.2 us
    pallas_call x4, Pallas kernels, project_keys(): pl.pallas_call(fetched_keys_kernel if fetched else functools.partial(keys...  13.6 us
    pallas_call x4, Pallas kernels, output(): pl.pallas_call(functools.partial(output_kernel, blocks), in_specs=[vmem]...  13.5 us
    all_to_all x1, starting transfers between devices, decays(): received = lax.all_to_all(sent, CTX, 0, 0, tiled=True)  11.7 us
  transfers between devices with their start and end apart: 19, of which 17 were waited for; matrix products, arithmetic and copies ran while one was open for 2% of the time, Pallas kernels for 13%

profile of v8, /device:TPU:1, one launch (start us, length us, event | category | flops | bytes accessed | tf_op | source)
XLA Modules:
  0.0 346.9 jit_solution(10025065984676938307)
XLA Ops:
  17.6 3.6 %collective-permute-done.4 = bf16[128,512]{1,0:T(8,128)(2,1)S(1)} collective-permute-done((bf16[128,512]{1,0:T(8,128)(2,1)S(1)}, bf16[128,512]{1,0:T(8,128)(2,1)S(1)}, u32[]{:S(2)}, u32[]{:S(2)}) %collective-permute-start.4) | collective-permute-done | bytes 131104 | tf_op jit(solution)/shard_map/ppermute | solution.py:311
  34.5 11.7 %all-to-all-start = ((f32[64,2,128]{2,1,0:T(2,128)}), f32[64,2,128]{2,1,0:T(2,128)S(1)}, u32[]{:S(2)}, u32[]{:S(2)}) async-start(f32[64,2,128]{2,1,0:T(2,128)} %pad_maximum_fusion.2), calls=%async_computation | async-start | bytes 131072 | tf_op jit(solution)/shard_map/all_to_all | solution.py:393
  46.5 10.9 %all-to-all-done = f32[64,2,128]{2,1,0:T(2,128)S(1)} async-done(((f32[64,2,128]{2,1,0:T(2,128)}), f32[64,2,128]{2,1,0:T(2,128)S(1)}, u32[]{:S(2)}, u32[]{:S(2)}) %all-to-all-start) | async-done | bytes 65568 | tf_op jit(solution)/shard_map/all_to_all | solution.py:393
  57.5 68.0 %all-gather.5.cloned.1.call-done = bf16[16384,512]{1,0:T(8,128)(2,1)} async-done(((bf16[256,512]{1,0:T(8,128)(2,1)}), bf16[16384,512]{1,0:T(8,128)(2,1)}) %all-gather.5.cloned.1.call-update) | async-done | bytes 16777232 | tf_op jit(solution)/shard_map/all_gather | solution.py:370
  125.5 4.9 %keys.4 = (bf16[128,2048]{1,0:T(8,128)(2,1)S(1)}, bf16[512,128]{1,0:T(8,128)(2,1)}) custom-call(bf16[128,2048]{1,0:T(8,128)(2,1)S(1)} %dynamic-slice_bitcast_fusion.x_ref, bf16[32,2,256,512]{3,2,1,0:T(8,128)(2,1)} %bitcast.63, f32[144,128]{1,0:T(8,128)S(1)} %get-tuple-element.42.table_ref), custom_call_target="tpu_custom_call" | custom-call | flops 1073741824 | bytes 8388608 | tf_op jit(solution)/shard_map/keys/pallas_call | solution.py:137
  130.4 8.4 %all-to-all-start.1 = ((bf16[64,8,128]{2,1,0:T(8,128)(2,1)}), bf16[64,8,128]{2,1,0:T(8,128)(2,1)S(1)}, u32[]{:S(2)}, u32[]{:S(2)}) async-start(bf16[64,8,128]{2,1,0:T(8,128)(2,1)} %bitcast.13), calls=%async_computation.1 | async-start | bytes 262144 | tf_op jit(solution)/shard_map/all_to_all | solution.py:418
  138.8 4.0 %within.4 = (bf16[128,1024]{1,0:T(8,128)(2,1)S(1)}, f32[128,1024]{1,0:T(8,128)S(1)}) custom-call(bf16[128,2048]{1,0:T(8,128)(2,1)S(1)} %dynamic-slice_bitcast_fusion.x_ref, bf16[32,2,256,512]{3,2,1,0:T(8,128)(2,1)} %bitcast.64, bf16[128,2048]{1,0:T(8,128)(2,1)S(1)} %get-tuple-element.43.kv_ref, f32[144,128]{1,0:T(8,128)S(1)} %get-tuple-element.42.table_ref), custom_call_target="tpu_custom_call" | custom-call | flops 637534208 | bytes 6291456 | tf_op jit(solution)/shard_map/within/pallas_call | solution.py:200
  142.8 9.2 %all-to-all-done.1.state_ref = bf16[64,8,128]{2,1,0:T(8,128)(2,1)S(1)} async-done(((bf16[64,8,128]{2,1,0:T(8,128)(2,1)}), bf16[64,8,128]{2,1,0:T(8,128)(2,1)S(1)}, u32[]{:S(2)}, u32[]{:S(2)}) %all-to-all-start.1) | async-done | bytes 131104 | tf_op jit(solution)/shard_map/all_to_all | solution.py:418
  152.1 16.9 %all_to_all.45 = bf16[64,8,128]{2,1,0:T(8,128)(2,1)S(1)} all-to-all(bf16[64,8,128]{2,1,0:T(8,128)(2,1)S(1)} %carry.4), channel_id=1, replica_groups=mesh['ylo'=2,'core'=2,'yhi'=2,'x'=4,'z'=8] {'yhi','x','z'}, dimensions={0} | all-to-all | bytes 262144 | tf_op jit(solution)/shard_map/all_to_all | solution.py:422
  169.0 3.4 output.4
  175.2 4.2 %fetch.3.buffer = bf16[4,2,32,32,512]{4,3,2,1,0:T(8,128)(2,1)S(1)} custom-call(bf16[32,2,256,512]{3,2,1,0:T(8,128)(2,1)} %bitcast.66), custom_call_target="tpu_custom_call" | custom-call | bytes 16777216 | tf_op jit(solution)/shard_map/fetch/pallas_call | solution.py:79
  184.2 5.2 %all-to-all-start.3 = ((bf16[64,8,128]{2,1,0:T(8,128)(2,1)}), bf16[64,8,128]{2,1,0:T(8,128)(2,1)S(1)}, u32[]{:S(2)}, u32[]{:S(2)}) async-start(bf16[64,8,128]{2,1,0:T(8,128)(2,1)} %bitcast.16), calls=%async_computation.3 | async-start | bytes 262144 | tf_op jit(solution)/shard_map/all_to_all | solution.py:418
  189.4 4.2 %within.5 = (bf16[128,1024]{1,0:T(8,128)(2,1)S(1)}, f32[128,1024]{1,0:T(8,128)S(1)}) custom-call(bf16[128,2048]{1,0:T(8,128)(2,1)S(1)} %collective-permute-done.6.x_ref, bf16[32,2,256,512]{3,2,1,0:T(8,128)(2,1)} %bitcast.67, bf16[128,2048]{1,0:T(8,128)(2,1)S(1)} %get-tuple-element.51.kv_ref, f32[144,128]{1,0:T(8,128)S(1)} %get-tuple-element.42.table_ref), custom_call_target="tpu_custom_call" | custom-call | flops 637534208 | bytes 6291456 | tf_op jit(solution)/shard_map/within/pallas_call | solution.py:200
  193.6 8.1 %all-to-all-done.3.state_ref = bf16[64,8,128]{2,1,0:T(8,128)(2,1)S(1)} async-done(((bf16[64,8,128]{2,1,0:T(8,128)(2,1)}), bf16[64,8,128]{2,1,0:T(8,128)(2,1)S(1)}, u32[]{:S(2)}, u32[]{:S(2)}) %all-to-all-start.3) | async-done | bytes 131104 | tf_op jit(solution)/shard_map/all_to_all | solution.py:418
  201.8 16.6 %all_to_all.46 = bf16[64,8,128]{2,1,0:T(8,128)(2,1)S(1)} all-to-all(bf16[64,8,128]{2,1,0:T(8,128)(2,1)S(1)} %carry.5), channel_id=1, replica_groups=mesh['ylo'=2,'core'=2,'yhi'=2,'x'=4,'z'=8] {'yhi','x','z'}, dimensions={0} | all-to-all | bytes 262144 | tf_op jit(solution)/shard_map/all_to_all | solution.py:422
  218.4 3.4 output.5
  223.2 7.9 %all-gather.7.cloned.1.call-done = bf16[16384,512]{1,0:T(8,128)(2,1)} async-done(((bf16[256,512]{1,0:T(8,128)(2,1)}), bf16[16384,512]{1,0:T(8,128)(2,1)}) %all-gather.7.cloned.1.call-update) | async-done | bytes 16777232 | tf_op jit(solution)/shard_map/all_gather | solution.py:370
  231.1 3.7 %fetch.4.buffer = bf16[4,2,32,32,512]{4,3,2,1,0:T(8,128)(2,1)S(1)} custom-call(bf16[32,2,256,512]{3,2,1,0:T(8,128)(2,1)} %bitcast.57), custom_call_target="tpu_custom_call" | custom-call | bytes 16777216 | tf_op jit(solution)/shard_map/fetch/pallas_call | solution.py:79
  237.7 9.0 %all-to-all-start.5 = ((bf16[64,8,128]{2,1,0:T(8,128)(2,1)}), bf16[64,8,128]{2,1,0:T(8,128)(2,1)S(1)}, u32[]{:S(2)}, u32[]{:S(2)}) async-start(bf16[64,8,128]{2,1,0:T(8,128)(2,1)} %bitcast.19), calls=%async_computation.5 | async-start | bytes 262144 | tf_op jit(solution)/shard_map/all_to_all | solution.py:418
  246.7 4.0 %within.6 = (bf16[128,1024]{1,0:T(8,128)(2,1)S(1)}, f32[128,1024]{1,0:T(8,128)S(1)}) custom-call(bf16[128,2048]{1,0:T(8,128)(2,1)S(1)} %collective-permute-done.7.x_ref, bf16[32,2,256,512]{3,2,1,0:T(8,128)(2,1)} %bitcast.58, bf16[128,2048]{1,0:T(8,128)(2,1)S(1)} %get-tuple-element.59.kv_ref, f32[144,128]{1,0:T(8,128)S(1)} %get-tuple-element.58.table_ref), custom_call_target="tpu_custom_call" | custom-call | flops 637534208 | bytes 6291456 | tf_op jit(solution)/shard_map/within/pallas_call | solution.py:200
  250.7 7.4 %all-to-all-done.5.state_ref = bf16[64,8,128]{2,1,0:T(8,128)(2,1)S(1)} async-done(((bf16[64,8,128]{2,1,0:T(8,128)(2,1)}), bf16[64,8,128]{2,1,0:T(8,128)(2,1)S(1)}, u32[]{:S(2)}, u32[]{:S(2)}) %all-to-all-start.5) | async-done | bytes 131104 | tf_op jit(solution)/shard_map/all_to_all | solution.py:418
  258.2 16.1 %all_to_all.47 = bf16[64,8,128]{2,1,0:T(8,128)(2,1)S(1)} all-to-all(bf16[64,8,128]{2,1,0:T(8,128)(2,1)S(1)} %carry.6), channel_id=1, replica_groups=mesh['ylo'=2,'core'=2,'yhi'=2,'x'=4,'z'=8] {'yhi','x','z'}, dimensions={0} | all-to-all | bytes 262144 | tf_op jit(solution)/shard_map/all_to_all | solution.py:422
  281.0 3.7 %fetch.5.buffer = bf16[4,2,32,32,512]{4,3,2,1,0:T(8,128)(2,1)S(1)} custom-call(bf16[32,2,256,512]{3,2,1,0:T(8,128)(2,1)} %bitcast.60), custom_call_target="tpu_custom_call" | custom-call | bytes 16777216 | tf_op jit(solution)/shard_map/fetch/pallas_call | solution.py:79
  284.7 4.9 %collective-permute-done.8.x_ref = bf16[128,2048]{1,0:T(8,128)(2,1)S(1)} collective-permute-done((bf16[128,2048]{1,0:T(8,128)(2,1)S(1)}, bf16[128,2048]{1,0:T(8,128)(2,1)S(1)}, u32[]{:S(2)}, u32[]{:S(2)}) %collective-permute-start.8) | collective-permute-done | bytes 524320 | tf_op jit(solution)/shard_map/ppermute | solution.py:351
  292.5 5.1 %all-to-all-start.7 = ((bf16[64,8,128]{2,1,0:T(8,128)(2,1)}), bf16[64,8,128]{2,1,0:T(8,128)(2,1)S(1)}, u32[]{:S(2)}, u32[]{:S(2)}) async-start(bf16[64,8,128]{2,1,0:T(8,128)(2,1)} %bitcast.21), calls=%async_computation.7 | async-start | bytes 262144 | tf_op jit(solution)/shard_map/all_to_all | solution.py:418
  297.7 4.0 %within.7 = (bf16[128,1024]{1,0:T(8,128)(2,1)S(1)}, f32[128,1024]{1,0:T(8,128)S(1)}) custom-call(bf16[128,2048]{1,0:T(8,128)(2,1)S(1)} %collective-permute-done.8.x_ref, bf16[32,2,256,512]{3,2,1,0:T(8,128)(2,1)} %bitcast.61, bf16[128,2048]{1,0:T(8,128)(2,1)S(1)} %get-tuple-element.67.kv_ref, f32[144,128]{1,0:T(8,128)S(1)} %get-tuple-element.58.table_ref), custom_call_target="tpu_custom_call" | custom-call | flops 637534208 | bytes 6291456 | tf_op jit(solution)/shard_map/within/pallas_call | solution.py:200
  301.7 7.5 %all-to-all-done.7.state_ref = bf16[64,8,128]{2,1,0:T(8,128)(2,1)S(1)} async-done(((bf16[64,8,128]{2,1,0:T(8,128)(2,1)}), bf16[64,8,128]{2,1,0:T(8,128)(2,1)S(1)}, u32[]{:S(2)}, u32[]{:S(2)}) %all-to-all-start.7) | async-done | bytes 131104 | tf_op jit(solution)/shard_map/all_to_all | solution.py:418
  309.9 4.8 %all-to-all-start.8 = ((bf16[64,8,128]{2,1,0:T(8,128)(2,1)}), bf16[64,8,128]{2,1,0:T(8,128)(2,1)S(1)}, u32[]{:S(2)}, u32[]{:S(2)}) async-start(bf16[64,8,128]{2,1,0:T(8,128)(2,1)} %carry.7), calls=%async_computation.8 | async-start | bytes 262144 | tf_op jit(solution)/shard_map/all_to_all | solution.py:422
  315.6 7.0 %collective-permute-start.9 = (bf16[128,2048]{1,0:T(8,128)(2,1)}, bf16[128,2048]{1,0:T(8,128)(2,1)}, u32[]{:S(2)}, u32[]{:S(2)}) collective-permute-start(bf16[128,2048]{1,0:T(8,128)(2,1)} %broadcast_select_fusion.1), channel_id=1, source_target_pairs={{64,0},{65,1},{66,2},{67,3},{68,4},{69,5},{70,6},{71,7},{72,8},{73... | collective-permute-start | bytes 1572872 | tf_op jit(solution)/shard_map/ppermute | solution.py:427
  322.6 3.6 %all-to-all-done.8 = bf16[64,8,128]{2,1,0:T(8,128)(2,1)S(1)} async-done(((bf16[64,8,128]{2,1,0:T(8,128)(2,1)}), bf16[64,8,128]{2,1,0:T(8,128)(2,1)S(1)}, u32[]{:S(2)}, u32[]{:S(2)}) %all-to-all-start.8) | async-done | bytes 131104 | tf_op jit(solution)/shard_map/all_to_all | solution.py:422
  327.3 3.4 output.7
  332.0 6.9 %collective-permute-done.10 = bf16[128,2048]{1,0:T(8,128)(2,1)S(1)} collective-permute-done((bf16[128,2048]{1,0:T(8,128)(2,1)S(1)}, bf16[128,2048]{1,0:T(8,128)(2,1)S(1)}, u32[]{:S(2)}, u32[]{:S(2)}) %collective-permute-start.10) | collective-permute-done | bytes 524320 | tf_op jit(solution)/shard_map/ppermute | solution.py:428
  (75 shorter events, 51.7 us)
Async XLA Ops:
  6.5 23.6 %copy-start = (bf16[2,128,2048]{2,1,0:T(8,128)(2,1)S(1)}, bf16[2,128,2048]{2,1,0:T(8,128)(2,1)}, u32[]{:S(2)}) copy-start(bf16[2,128,2048]{2,1,0:T(8,128)(2,1)} %param.4) | copy-start | bytes 3145732
  6.5 118.9 %all-gather.5.cloned.1.call-start = ((), (), s32[]{:S(2)}) async-start(), calls=%async_computation.9 | async-start | bytes 17039360 | tf_op jit(solution)/shard_map/all_gather | solution.py:370
  6.5 1.0 copy-start.4
  7.6 0.8 copy-start.5
  8.4 4.3 %collective-permute-start.2 = (bf16[128,512]{1,0:T(8,128)(2,1)S(1)}, bf16[128,512]{1,0:T(8,128)(2,1)S(1)}, u32[]{:S(2)}, u32[]{:S(2)}) collective-permute-start(bf16[128,512]{1,0:T(8,128)(2,1)S(1)} %get-tuple-element.41), channel_id=1, source_target_pairs={{0,64},{64,0},{1,65},{65,1},{2,66},{66,2},{3,67},{67,3},{4,68},{68... | collective-permute-start | bytes 393224 | tf_op jit(solution)/shard_map/ppermute | solution.py:18
  12.8 4.8 %collective-permute-start.3 = (bf16[128,512]{1,0:T(8,128)(2,1)S(1)}, bf16[128,512]{1,0:T(8,128)(2,1)S(1)}, u32[]{:S(2)}, u32[]{:S(2)}) collective-permute-start(bf16[128,512]{1,0:T(8,128)(2,1)S(1)} %get-tuple-element.83), channel_id=1, source_target_pairs={{0,128},{128,0},{1,129},{129,1},{2,130},{130,2},{3,131},{131,3},{4... | collective-permute-start | bytes 393224 | tf_op jit(solution)/shard_map/ppermute | solution.py:311
  12.9 8.3 %collective-permute-start.4 = (bf16[128,512]{1,0:T(8,128)(2,1)S(1)}, bf16[128,512]{1,0:T(8,128)(2,1)S(1)}, u32[]{:S(2)}, u32[]{:S(2)}) collective-permute-start(bf16[128,512]{1,0:T(8,128)(2,1)S(1)} %get-tuple-element.84), channel_id=1, source_target_pairs={{0,32},{32,0},{1,33},{33,1},{2,34},{34,2},{3,35},{35,3},{4,36},{36... | collective-permute-start | bytes 393224 | tf_op jit(solution)/shard_map/ppermute | solution.py:311
  15.0 8.6 %collective-permute-start.5 = (bf16[128,512]{1,0:T(8,128)(2,1)S(1)}, bf16[128,512]{1,0:T(8,128)(2,1)S(1)}, u32[]{:S(2)}, u32[]{:S(2)}) collective-permute-start(bf16[128,512]{1,0:T(8,128)(2,1)S(1)} %get-tuple-element.83), channel_id=1, source_target_pairs={{0,160},{32,128},{128,32},{160,0},{1,161},{33,129},{129,33},{161,1... | collective-permute-start | bytes 393224 | tf_op jit(solution)/shard_map/ppermute | solution.py:311
  24.4 206.7 %all-gather.7.cloned.1.call-start = ((), (), s32[]{:S(2)}) async-start(), calls=%async_computation.10 | async-start | bytes 17039360 | tf_op jit(solution)/shard_map/all_gather | solution.py:370
  26.0 1.8 collective-permute-start
  28.5 2.5 collective-permute-start.1
  34.5 23.0 %all-to-all-start = ((f32[64,2,128]{2,1,0:T(2,128)}), f32[64,2,128]{2,1,0:T(2,128)S(1)}, u32[]{:S(2)}, u32[]{:S(2)}) async-start(f32[64,2,128]{2,1,0:T(2,128)} %pad_maximum_fusion.2), calls=%async_computation | async-start | bytes 131072 | tf_op jit(solution)/shard_map/all_to_all | solution.py:393
  130.4 21.6 %all-to-all-start.1 = ((bf16[64,8,128]{2,1,0:T(8,128)(2,1)}), bf16[64,8,128]{2,1,0:T(8,128)(2,1)S(1)}, u32[]{:S(2)}, u32[]{:S(2)}) async-start(bf16[64,8,128]{2,1,0:T(8,128)(2,1)} %bitcast.13), calls=%async_computation.1 | async-start | bytes 262144 | tf_op jit(solution)/shard_map/all_to_all | solution.py:418
  172.3 8.9 %collective-permute-start.6 = (bf16[128,2048]{1,0:T(8,128)(2,1)S(1)}, bf16[128,2048]{1,0:T(8,128)(2,1)S(1)}, u32[]{:S(2)}, u32[]{:S(2)}) collective-permute-start(bf16[128,2048]{1,0:T(8,128)(2,1)S(1)} %output.4), channel_id=1, source_target_pairs={{0,128},{32,160},{64,224},{96,192},{1,129},{33,161},{65,225},{97,1... | collective-permute-start | bytes 1572872 | tf_op jit(solution)/shard_map/ppermute | solution.py:351
  184.2 17.5 %all-to-all-start.3 = ((bf16[64,8,128]{2,1,0:T(8,128)(2,1)}), bf16[64,8,128]{2,1,0:T(8,128)(2,1)S(1)}, u32[]{:S(2)}, u32[]{:S(2)}) async-start(bf16[64,8,128]{2,1,0:T(8,128)(2,1)} %bitcast.16), calls=%async_computation.3 | async-start | bytes 262144 | tf_op jit(solution)/shard_map/all_to_all | solution.py:418
  221.9 12.9 %collective-permute-start.7 = (bf16[128,2048]{1,0:T(8,128)(2,1)S(1)}, bf16[128,2048]{1,0:T(8,128)(2,1)S(1)}, u32[]{:S(2)}, u32[]{:S(2)}) collective-permute-start(bf16[128,2048]{1,0:T(8,128)(2,1)S(1)} %output.5), channel_id=1, source_target_pairs={{128,0},{160,32},{192,96},{224,64},{129,1},{161,33},{193,97},{225,... | collective-permute-start | bytes 1572872 | tf_op jit(solution)/shard_map/ppermute | solution.py:351
  237.7 20.4 %all-to-all-start.5 = ((bf16[64,8,128]{2,1,0:T(8,128)(2,1)}), bf16[64,8,128]{2,1,0:T(8,128)(2,1)S(1)}, u32[]{:S(2)}, u32[]{:S(2)}) async-start(bf16[64,8,128]{2,1,0:T(8,128)(2,1)} %bitcast.19), calls=%async_computation.5 | async-start | bytes 262144 | tf_op jit(solution)/shard_map/all_to_all | solution.py:418
  277.7 11.9 %collective-permute-start.8 = (bf16[128,2048]{1,0:T(8,128)(2,1)S(1)}, bf16[128,2048]{1,0:T(8,128)(2,1)S(1)}, u32[]{:S(2)}, u32[]{:S(2)}) collective-permute-start(bf16[128,2048]{1,0:T(8,128)(2,1)S(1)} %output.6), channel_id=1, source_target_pairs={{0,128},{32,160},{64,192},{96,224},{1,129},{33,161},{65,193},{97,2... | collective-permute-start | bytes 1572872 | tf_op jit(solution)/shard_map/ppermute | solution.py:351
  292.5 16.6 %all-to-all-start.7 = ((bf16[64,8,128]{2,1,0:T(8,128)(2,1)}), bf16[64,8,128]{2,1,0:T(8,128)(2,1)S(1)}, u32[]{:S(2)}, u32[]{:S(2)}) async-start(bf16[64,8,128]{2,1,0:T(8,128)(2,1)} %bitcast.21), calls=%async_computation.7 | async-start | bytes 262144 | tf_op jit(solution)/shard_map/all_to_all | solution.py:418
  301.7 24.6 %copy-start.2 = (bf16[128,1024]{1,0:T(8,128)(2,1)}, bf16[128,1024]{1,0:T(8,128)(2,1)S(1)}, u32[]{:S(2)}) copy-start(bf16[128,1024]{1,0:T(8,128)(2,1)S(1)} %get-tuple-element.68.q_ref) | copy-start | bytes 786436
  309.9 16.3 %all-to-all-start.8 = ((bf16[64,8,128]{2,1,0:T(8,128)(2,1)}), bf16[64,8,128]{2,1,0:T(8,128)(2,1)S(1)}, u32[]{:S(2)}, u32[]{:S(2)}) async-start(bf16[64,8,128]{2,1,0:T(8,128)(2,1)} %carry.7), calls=%async_computation.8 | async-start | bytes 262144 | tf_op jit(solution)/shard_map/all_to_all | solution.py:422
  315.6 16.4 %collective-permute-start.9 = (bf16[128,2048]{1,0:T(8,128)(2,1)}, bf16[128,2048]{1,0:T(8,128)(2,1)}, u32[]{:S(2)}, u32[]{:S(2)}) collective-permute-start(bf16[128,2048]{1,0:T(8,128)(2,1)} %broadcast_select_fusion.1), channel_id=1, source_target_pairs={{64,0},{65,1},{66,2},{67,3},{68,4},{69,5},{70,6},{71,7},{72,8},{73... | collective-permute-start | bytes 1572872 | tf_op jit(solution)/shard_map/ppermute | solution.py:427
  326.2 13.8 %copy-start.1 = (bf16[2,128,2048]{2,1,0:T(8,128)(2,1)S(1)}, bf16[2,128,2048]{2,1,0:T(8,128)(2,1)}, u32[]{:S(2)}) copy-start(bf16[2,128,2048]{2,1,0:T(8,128)(2,1)} %param.4) | copy-start | bytes 3145732
  326.2 1.0 copy-start.3
  330.7 8.2 %collective-permute-start.10 = (bf16[128,2048]{1,0:T(8,128)(2,1)S(1)}, bf16[128,2048]{1,0:T(8,128)(2,1)S(1)}, u32[]{:S(2)}, u32[]{:S(2)}) collective-permute-start(bf16[128,2048]{1,0:T(8,128)(2,1)S(1)} %broadcast_select_fusion), channel_id=1, source_target_pairs={{0,64},{1,65},{2,66},{3,67},{4,68},{5,69},{6,70},{7,71},{8,72},{9,... | collective-permute-start | bytes 1572872 | tf_op jit(solution)/shard_map/ppermute | solution.py:428
Sparse Core Ops, SparseCore 0:
  24.6 100.8 all-gather.4
  128.3 102.8 all-gather.6

commit v9 on v7

--- a/solution.py
+++ b/solution.py
@@ -346,7 +346,7 @@
     for level, turn in hops:
         for core in range(2):
             for far in range(2):
-                goal = far ^ core if turn else far
+                goal = far ^ (1 - core) if turn else far
                 pairs.append((level * 4 + core * 2 + far, (1 - level) * 4 + core * 2 + goal))
     return lax.ppermute(value, ("ylo", "core", "yhi"), pairs)
 
@@ -403,7 +403,7 @@
     tables, totals = decays(log_decay[0], core, level)
     x, totals, tables = lax.optimization_barrier((x, totals, tables))
     straight = jnp.zeros((1,), jnp.int32)
-    turned = straight + core * (blocks // 2)
+    turned = straight + (1 - core) * (blocks // 2)
     kept = []
     for step in range(4):
         layer = step // 2

time: 345 us -> 344 us (level)
  no operation moved by 1% of the time
where the time goes in v9:
time: 344 us; the launch traced here: 343 us
  waiting for transfers between devices  138 us (40%)
  blocking collectives  65.8 us (19%)
  starting transfers between devices  59.8 us (17%)
  Pallas kernels  55.2 us (16%)
  between operations  13.6 us (4%)
  other arithmetic  5.17 us (2%)
    all_gather x2, waiting for transfers between devices, shared_weights(): lax.all_gather(own, SPREAD, axis=0).reshape(-1, 2, own.shape[0], NB)  76.3 us
    all_to_all x4, blocking collectives, shards(): carried = lax.all_to_all(mine, CTX, 0, 0, tiled=True).reshape(state.shape)  65.8 us
    all_to_all x4, waiting for transfers between devices, shards(): lax.all_to_all(state.reshape(blocks, -1, 128), CTX, 0, 0, tiled=True)  31.8 us
    all_to_all x4, starting transfers between devices, shards(): lax.all_to_all(state.reshape(blocks, -1, 128), CTX, 0, 0, tiled=True)  28 us
    pallas_call x4, Pallas kernels, within(): pl.pallas_call(functools.partial(within_kernel, blocks), in_specs=[vmem,...  16 us
    pallas_call x4, Pallas kernels, project_keys(): pl.pallas_call(fetched_keys_kernel if fetched else functools.partial(keys...  13.6 us
    pallas_call x4, Pallas kernels, output(): pl.pallas_call(functools.partial(output_kernel, blocks), in_specs=[vmem]...  13.4 us
    all_to_all x1, starting transfers between devices, decays(): received = lax.all_to_all(sent, CTX, 0, 0, tiled=True)  11.7 us
  transfers between devices with their start and end apart: 17, of which 16 were waited for; matrix products, arithmetic and copies ran while one was open for 2% of the time, Pallas kernels for 12%

profile of v9, /device:TPU:1, one launch (start us, length us, event | category | flops | bytes accessed | tf_op | source)
XLA Modules:
  0.0 342.9 jit_solution(17087105719098661310)
XLA Ops:
  8.4 3.3 collective-permute-start.2
  17.6 3.6 %collective-permute-done.4 = bf16[128,512]{1,0:T(8,128)(2,1)S(1)} collective-permute-done((bf16[128,512]{1,0:T(8,128)(2,1)S(1)}, bf16[128,512]{1,0:T(8,128)(2,1)S(1)}, u32[]{:S(2)}, u32[]{:S(2)}) %collective-permute-start.4) | collective-permute-done | bytes 131104 | tf_op jit(solution)/shard_map/ppermute | solution.py:311
  34.5 11.7 %all-to-all-start = ((f32[64,2,128]{2,1,0:T(2,128)}), f32[64,2,128]{2,1,0:T(2,128)S(1)}, u32[]{:S(2)}, u32[]{:S(2)}) async-start(f32[64,2,128]{2,1,0:T(2,128)} %pad_maximum_fusion.2), calls=%async_computation | async-start | bytes 131072 | tf_op jit(solution)/shard_map/all_to_all | solution.py:393
  46.5 10.8 %all-to-all-done = f32[64,2,128]{2,1,0:T(2,128)S(1)} async-done(((f32[64,2,128]{2,1,0:T(2,128)}), f32[64,2,128]{2,1,0:T(2,128)S(1)}, u32[]{:S(2)}, u32[]{:S(2)}) %all-to-all-start) | async-done | bytes 65568 | tf_op jit(solution)/shard_map/all_to_all | solution.py:393
  57.3 68.2 %all-gather.5.cloned.1.call-done = bf16[16384,512]{1,0:T(8,128)(2,1)} async-done(((bf16[256,512]{1,0:T(8,128)(2,1)}), bf16[16384,512]{1,0:T(8,128)(2,1)}) %all-gather.5.cloned.1.call-update) | async-done | bytes 16777232 | tf_op jit(solution)/shard_map/all_gather | solution.py:370
  125.5 4.9 %keys.4 = (bf16[128,2048]{1,0:T(8,128)(2,1)S(1)}, bf16[512,128]{1,0:T(8,128)(2,1)}) custom-call(bf16[128,2048]{1,0:T(8,128)(2,1)S(1)} %dynamic-slice_bitcast_fusion.x_ref, bf16[32,2,256,512]{3,2,1,0:T(8,128)(2,1)} %bitcast.63, f32[144,128]{1,0:T(8,128)S(1)} %get-tuple-element.42.table_ref), custom_call_target="tpu_custom_call" | custom-call | flops 1073741824 | bytes 8388608 | tf_op jit(solution)/shard_map/keys/pallas_call | solution.py:137
  130.5 8.3 %all-to-all-start.1 = ((bf16[64,8,128]{2,1,0:T(8,128)(2,1)}), bf16[64,8,128]{2,1,0:T(8,128)(2,1)S(1)}, u32[]{:S(2)}, u32[]{:S(2)}) async-start(bf16[64,8,128]{2,1,0:T(8,128)(2,1)} %bitcast.13), calls=%async_computation.1 | async-start | bytes 262144 | tf_op jit(solution)/shard_map/all_to_all | solution.py:418
  138.8 4.0 %within.4 = (bf16[128,1024]{1,0:T(8,128)(2,1)S(1)}, f32[128,1024]{1,0:T(8,128)S(1)}) custom-call(bf16[128,2048]{1,0:T(8,128)(2,1)S(1)} %dynamic-slice_bitcast_fusion.x_ref, bf16[32,2,256,512]{3,2,1,0:T(8,128)(2,1)} %bitcast.64, bf16[128,2048]{1,0:T(8,128)(2,1)S(1)} %get-tuple-element.43.kv_ref, f32[144,128]{1,0:T(8,128)S(1)} %get-tuple-element.42.table_ref), custom_call_target="tpu_custom_call" | custom-call | flops 637534208 | bytes 6291456 | tf_op jit(solution)/shard_map/within/pallas_call | solution.py:200
  142.8 9.2 %all-to-all-done.1.state_ref = bf16[64,8,128]{2,1,0:T(8,128)(2,1)S(1)} async-done(((bf16[64,8,128]{2,1,0:T(8,128)(2,1)}), bf16[64,8,128]{2,1,0:T(8,128)(2,1)S(1)}, u32[]{:S(2)}, u32[]{:S(2)}) %all-to-all-start.1) | async-done | bytes 131104 | tf_op jit(solution)/shard_map/all_to_all | solution.py:418
  152.2 16.8 %all_to_all.45 = bf16[64,8,128]{2,1,0:T(8,128)(2,1)S(1)} all-to-all(bf16[64,8,128]{2,1,0:T(8,128)(2,1)S(1)} %carry.4), channel_id=1, replica_groups=mesh['ylo'=2,'core'=2,'yhi'=2,'x'=4,'z'=8] {'yhi','x','z'}, dimensions={0} | all-to-all | bytes 262144 | tf_op jit(solution)/shard_map/all_to_all | solution.py:422
  169.0 3.4 output.4
  174.6 4.2 %fetch.3.buffer = bf16[4,2,32,32,512]{4,3,2,1,0:T(8,128)(2,1)S(1)} custom-call(bf16[32,2,256,512]{3,2,1,0:T(8,128)(2,1)} %bitcast.66), custom_call_target="tpu_custom_call" | custom-call | bytes 16777216 | tf_op jit(solution)/shard_map/fetch/pallas_call | solution.py:79
  183.6 5.8 %all-to-all-start.3 = ((bf16[64,8,128]{2,1,0:T(8,128)(2,1)}), bf16[64,8,128]{2,1,0:T(8,128)(2,1)S(1)}, u32[]{:S(2)}, u32[]{:S(2)}) async-start(bf16[64,8,128]{2,1,0:T(8,128)(2,1)} %bitcast.16), calls=%async_computation.3 | async-start | bytes 262144 | tf_op jit(solution)/shard_map/all_to_all | solution.py:418
  189.4 4.1 %within.5 = (bf16[128,1024]{1,0:T(8,128)(2,1)S(1)}, f32[128,1024]{1,0:T(8,128)S(1)}) custom-call(bf16[128,2048]{1,0:T(8,128)(2,1)S(1)} %collective-permute-done.6.x_ref, bf16[32,2,256,512]{3,2,1,0:T(8,128)(2,1)} %bitcast.67, bf16[128,2048]{1,0:T(8,128)(2,1)S(1)} %get-tuple-element.51.kv_ref, f32[144,128]{1,0:T(8,128)S(1)} %get-tuple-element.42.table_ref), custom_call_target="tpu_custom_call" | custom-call | flops 637534208 | bytes 6291456 | tf_op jit(solution)/shard_map/within/pallas_call | solution.py:200
  193.5 7.8 %all-to-all-done.3.state_ref = bf16[64,8,128]{2,1,0:T(8,128)(2,1)S(1)} async-done(((bf16[64,8,128]{2,1,0:T(8,128)(2,1)}), bf16[64,8,128]{2,1,0:T(8,128)(2,1)S(1)}, u32[]{:S(2)}, u32[]{:S(2)}) %all-to-all-start.3) | async-done | bytes 131104 | tf_op jit(solution)/shard_map/all_to_all | solution.py:418
  201.4 16.8 %all_to_all.46 = bf16[64,8,128]{2,1,0:T(8,128)(2,1)S(1)} all-to-all(bf16[64,8,128]{2,1,0:T(8,128)(2,1)S(1)} %carry.5), channel_id=1, replica_groups=mesh['ylo'=2,'core'=2,'yhi'=2,'x'=4,'z'=8] {'yhi','x','z'}, dimensions={0} | all-to-all | bytes 262144 | tf_op jit(solution)/shard_map/all_to_all | solution.py:422
  218.3 3.4 output.5
  223.0 8.1 %all-gather.7.cloned.1.call-done = bf16[16384,512]{1,0:T(8,128)(2,1)} async-done(((bf16[256,512]{1,0:T(8,128)(2,1)}), bf16[16384,512]{1,0:T(8,128)(2,1)}) %all-gather.7.cloned.1.call-update) | async-done | bytes 16777232 | tf_op jit(solution)/shard_map/all_gather | solution.py:370
  231.0 3.7 %fetch.4.buffer = bf16[4,2,32,32,512]{4,3,2,1,0:T(8,128)(2,1)S(1)} custom-call(bf16[32,2,256,512]{3,2,1,0:T(8,128)(2,1)} %bitcast.57), custom_call_target="tpu_custom_call" | custom-call | bytes 16777216 | tf_op jit(solution)/shard_map/fetch/pallas_call | solution.py:79
  237.6 8.8 %all-to-all-start.5 = ((bf16[64,8,128]{2,1,0:T(8,128)(2,1)}), bf16[64,8,128]{2,1,0:T(8,128)(2,1)S(1)}, u32[]{:S(2)}, u32[]{:S(2)}) async-start(bf16[64,8,128]{2,1,0:T(8,128)(2,1)} %bitcast.19), calls=%async_computation.5 | async-start | bytes 262144 | tf_op jit(solution)/shard_map/all_to_all | solution.py:418
  246.4 4.0 %within.6 = (bf16[128,1024]{1,0:T(8,128)(2,1)S(1)}, f32[128,1024]{1,0:T(8,128)S(1)}) custom-call(bf16[128,2048]{1,0:T(8,128)(2,1)S(1)} %collective-permute-done.7.x_ref, bf16[32,2,256,512]{3,2,1,0:T(8,128)(2,1)} %bitcast.58, bf16[128,2048]{1,0:T(8,128)(2,1)S(1)} %get-tuple-element.59.kv_ref, f32[144,128]{1,0:T(8,128)S(1)} %get-tuple-element.58.table_ref), custom_call_target="tpu_custom_call" | custom-call | flops 637534208 | bytes 6291456 | tf_op jit(solution)/shard_map/within/pallas_call | solution.py:200
  250.3 7.3 %all-to-all-done.5.state_ref = bf16[64,8,128]{2,1,0:T(8,128)(2,1)S(1)} async-done(((bf16[64,8,128]{2,1,0:T(8,128)(2,1)}), bf16[64,8,128]{2,1,0:T(8,128)(2,1)S(1)}, u32[]{:S(2)}, u32[]{:S(2)}) %all-to-all-start.5) | async-done | bytes 131104 | tf_op jit(solution)/shard_map/all_to_all | solution.py:418
  257.8 16.1 %all_to_all.47 = bf16[64,8,128]{2,1,0:T(8,128)(2,1)S(1)} all-to-all(bf16[64,8,128]{2,1,0:T(8,128)(2,1)S(1)} %carry.6), channel_id=1, replica_groups=mesh['ylo'=2,'core'=2,'yhi'=2,'x'=4,'z'=8] {'yhi','x','z'}, dimensions={0} | all-to-all | bytes 262144 | tf_op jit(solution)/shard_map/all_to_all | solution.py:422
  273.8 3.4 output.6
  280.3 3.7 %fetch.5.buffer = bf16[4,2,32,32,512]{4,3,2,1,0:T(8,128)(2,1)S(1)} custom-call(bf16[32,2,256,512]{3,2,1,0:T(8,128)(2,1)} %bitcast.60), custom_call_target="tpu_custom_call" | custom-call | bytes 16777216 | tf_op jit(solution)/shard_map/fetch/pallas_call | solution.py:79
  284.0 4.9 %collective-permute-done.8.x_ref = bf16[128,2048]{1,0:T(8,128)(2,1)S(1)} collective-permute-done((bf16[128,2048]{1,0:T(8,128)(2,1)S(1)}, bf16[128,2048]{1,0:T(8,128)(2,1)S(1)}, u32[]{:S(2)}, u32[]{:S(2)}) %collective-permute-start.8) | collective-permute-done | bytes 524320 | tf_op jit(solution)/shard_map/ppermute | solution.py:351
  291.8 5.1 %all-to-all-start.7 = ((bf16[64,8,128]{2,1,0:T(8,128)(2,1)}), bf16[64,8,128]{2,1,0:T(8,128)(2,1)S(1)}, u32[]{:S(2)}, u32[]{:S(2)}) async-start(bf16[64,8,128]{2,1,0:T(8,128)(2,1)} %bitcast.21), calls=%async_computation.7 | async-start | bytes 262144 | tf_op jit(solution)/shard_map/all_to_all | solution.py:418
  297.0 4.0 %within.7 = (bf16[128,1024]{1,0:T(8,128)(2,1)S(1)}, f32[128,1024]{1,0:T(8,128)S(1)}) custom-call(bf16[128,2048]{1,0:T(8,128)(2,1)S(1)} %collective-permute-done.8.x_ref, bf16[32,2,256,512]{3,2,1,0:T(8,128)(2,1)} %bitcast.61, bf16[128,2048]{1,0:T(8,128)(2,1)S(1)} %get-tuple-element.67.kv_ref, f32[144,128]{1,0:T(8,128)S(1)} %get-tuple-element.58.table_ref), custom_call_target="tpu_custom_call" | custom-call | flops 637534208 | bytes 6291456 | tf_op jit(solution)/shard_map/within/pallas_call | solution.py:200
  301.0 7.5 %all-to-all-done.7.state_ref = bf16[64,8,128]{2,1,0:T(8,128)(2,1)S(1)} async-done(((bf16[64,8,128]{2,1,0:T(8,128)(2,1)}), bf16[64,8,128]{2,1,0:T(8,128)(2,1)S(1)}, u32[]{:S(2)}, u32[]{:S(2)}) %all-to-all-start.7) | async-done | bytes 131104 | tf_op jit(solution)/shard_map/all_to_all | solution.py:418
  308.6 16.1 %all_to_all.48 = bf16[64,8,128]{2,1,0:T(8,128)(2,1)S(1)} all-to-all(bf16[64,8,128]{2,1,0:T(8,128)(2,1)S(1)} %carry.7), channel_id=1, replica_groups=mesh['ylo'=2,'core'=2,'yhi'=2,'x'=4,'z'=8] {'yhi','x','z'}, dimensions={0} | all-to-all | bytes 262144 | tf_op jit(solution)/shard_map/all_to_all | solution.py:422
  324.7 3.4 output.7
  328.2 5.2 %collective-permute-start.9 = (bf16[128,2048]{1,0:T(8,128)(2,1)S(1)}, bf16[128,2048]{1,0:T(8,128)(2,1)S(1)}, u32[]{:S(2)}, u32[]{:S(2)}) collective-permute-start(bf16[128,2048]{1,0:T(8,128)(2,1)S(1)} %broadcast_select_fusion.2), channel_id=1, source_target_pairs={{0,64},{64,0},{1,65},{65,1},{2,66},{66,2},{3,67},{67,3},{4,68},{68... | collective-permute-start | bytes 1572872 | tf_op jit(solution)/shard_map/ppermute | solution.py:18
  (67 shorter events, 42.1 us)
Async XLA Ops:
  6.5 22.0 %copy-start = (bf16[2,128,2048]{2,1,0:T(8,128)(2,1)S(1)}, bf16[2,128,2048]{2,1,0:T(8,128)(2,1)}, u32[]{:S(2)}) copy-start(bf16[2,128,2048]{2,1,0:T(8,128)(2,1)} %param.4) | copy-start | bytes 3145732
  6.5 119.0 %all-gather.5.cloned.1.call-start = ((), (), s32[]{:S(2)}) async-start(), calls=%async_computation.9 | async-start | bytes 17039360 | tf_op jit(solution)/shard_map/all_gather | solution.py:370
  6.5 1.0 copy-start.2
  7.6 0.8 copy-start.3
  8.4 4.3 %collective-permute-start.2 = (bf16[128,512]{1,0:T(8,128)(2,1)S(1)}, bf16[128,512]{1,0:T(8,128)(2,1)S(1)}, u32[]{:S(2)}, u32[]{:S(2)}) collective-permute-start(bf16[128,512]{1,0:T(8,128)(2,1)S(1)} %get-tuple-element.41), channel_id=1, source_target_pairs={{0,64},{64,0},{1,65},{65,1},{2,66},{66,2},{3,67},{67,3},{4,68},{68... | collective-permute-start | bytes 393224 | tf_op jit(solution)/shard_map/ppermute | solution.py:18
  12.8 4.8 %collective-permute-start.3 = (bf16[128,512]{1,0:T(8,128)(2,1)S(1)}, bf16[128,512]{1,0:T(8,128)(2,1)S(1)}, u32[]{:S(2)}, u32[]{:S(2)}) collective-permute-start(bf16[128,512]{1,0:T(8,128)(2,1)S(1)} %get-tuple-element.83), channel_id=1, source_target_pairs={{0,128},{128,0},{1,129},{129,1},{2,130},{130,2},{3,131},{131,3},{4... | collective-permute-start | bytes 393224 | tf_op jit(solution)/shard_map/ppermute | solution.py:311
  12.9 8.3 %collective-permute-start.4 = (bf16[128,512]{1,0:T(8,128)(2,1)S(1)}, bf16[128,512]{1,0:T(8,128)(2,1)S(1)}, u32[]{:S(2)}, u32[]{:S(2)}) collective-permute-start(bf16[128,512]{1,0:T(8,128)(2,1)S(1)} %get-tuple-element.84), channel_id=1, source_target_pairs={{0,32},{32,0},{1,33},{33,1},{2,34},{34,2},{3,35},{35,3},{4,36},{36... | collective-permute-start | bytes 393224 | tf_op jit(solution)/shard_map/ppermute | solution.py:311
  15.0 8.6 %collective-permute-start.5 = (bf16[128,512]{1,0:T(8,128)(2,1)S(1)}, bf16[128,512]{1,0:T(8,128)(2,1)S(1)}, u32[]{:S(2)}, u32[]{:S(2)}) collective-permute-start(bf16[128,512]{1,0:T(8,128)(2,1)S(1)} %get-tuple-element.83), channel_id=1, source_target_pairs={{0,160},{32,128},{128,32},{160,0},{1,161},{33,129},{129,33},{161,1... | collective-permute-start | bytes 393224 | tf_op jit(solution)/shard_map/ppermute | solution.py:311
  24.4 206.6 %all-gather.7.cloned.1.call-start = ((), (), s32[]{:S(2)}) async-start(), calls=%async_computation.10 | async-start | bytes 17039360 | tf_op jit(solution)/shard_map/all_gather | solution.py:370
  26.0 1.8 collective-permute-start
  28.5 2.5 collective-permute-start.1
  34.5 22.8 %all-to-all-start = ((f32[64,2,128]{2,1,0:T(2,128)}), f32[64,2,128]{2,1,0:T(2,128)S(1)}, u32[]{:S(2)}, u32[]{:S(2)}) async-start(f32[64,2,128]{2,1,0:T(2,128)} %pad_maximum_fusion.2), calls=%async_computation | async-start | bytes 131072 | tf_op jit(solution)/shard_map/all_to_all | solution.py:393
  130.5 21.5 %all-to-all-start.1 = ((bf16[64,8,128]{2,1,0:T(8,128)(2,1)}), bf16[64,8,128]{2,1,0:T(8,128)(2,1)S(1)}, u32[]{:S(2)}, u32[]{:S(2)}) async-start(bf16[64,8,128]{2,1,0:T(8,128)(2,1)} %bitcast.13), calls=%async_computation.1 | async-start | bytes 262144 | tf_op jit(solution)/shard_map/all_to_all | solution.py:418
  172.4 8.3 %collective-permute-start.6 = (bf16[128,2048]{1,0:T(8,128)(2,1)S(1)}, bf16[128,2048]{1,0:T(8,128)(2,1)S(1)}, u32[]{:S(2)}, u32[]{:S(2)}) collective-permute-start(bf16[128,2048]{1,0:T(8,128)(2,1)S(1)} %output.4), channel_id=1, source_target_pairs={{0,160},{32,128},{64,192},{96,224},{1,161},{33,129},{65,193},{97,2... | collective-permute-start | bytes 1572872 | tf_op jit(solution)/shard_map/ppermute | solution.py:351
  183.6 17.7 %all-to-all-start.3 = ((bf16[64,8,128]{2,1,0:T(8,128)(2,1)}), bf16[64,8,128]{2,1,0:T(8,128)(2,1)S(1)}, u32[]{:S(2)}, u32[]{:S(2)}) async-start(bf16[64,8,128]{2,1,0:T(8,128)(2,1)} %bitcast.16), calls=%async_computation.3 | async-start | bytes 262144 | tf_op jit(solution)/shard_map/all_to_all | solution.py:418
  221.7 13.0 %collective-permute-start.7 = (bf16[128,2048]{1,0:T(8,128)(2,1)S(1)}, bf16[128,2048]{1,0:T(8,128)(2,1)S(1)}, u32[]{:S(2)}, u32[]{:S(2)}) collective-permute-start(bf16[128,2048]{1,0:T(8,128)(2,1)S(1)} %output.5), channel_id=1, source_target_pairs={{128,32},{160,0},{192,64},{224,96},{129,33},{161,1},{193,65},{225,... | collective-permute-start | bytes 1572872 | tf_op jit(solution)/shard_map/ppermute | solution.py:351
  237.6 20.1 %all-to-all-start.5 = ((bf16[64,8,128]{2,1,0:T(8,128)(2,1)}), bf16[64,8,128]{2,1,0:T(8,128)(2,1)S(1)}, u32[]{:S(2)}, u32[]{:S(2)}) async-start(bf16[64,8,128]{2,1,0:T(8,128)(2,1)} %bitcast.19), calls=%async_computation.5 | async-start | bytes 262144 | tf_op jit(solution)/shard_map/all_to_all | solution.py:418
  277.2 11.7 %collective-permute-start.8 = (bf16[128,2048]{1,0:T(8,128)(2,1)S(1)}, bf16[128,2048]{1,0:T(8,128)(2,1)S(1)}, u32[]{:S(2)}, u32[]{:S(2)}) collective-permute-start(bf16[128,2048]{1,0:T(8,128)(2,1)S(1)} %output.6), channel_id=1, source_target_pairs={{0,128},{32,160},{64,192},{96,224},{1,129},{33,161},{65,193},{97,2... | collective-permute-start | bytes 1572872 | tf_op jit(solution)/shard_map/ppermute | solution.py:351
  291.8 16.6 %all-to-all-start.7 = ((bf16[64,8,128]{2,1,0:T(8,128)(2,1)}), bf16[64,8,128]{2,1,0:T(8,128)(2,1)S(1)}, u32[]{:S(2)}, u32[]{:S(2)}) async-start(bf16[64,8,128]{2,1,0:T(8,128)(2,1)} %bitcast.21), calls=%async_computation.7 | async-start | bytes 262144 | tf_op jit(solution)/shard_map/all_to_all | solution.py:418
  324.7 11.4 %copy-start.1 = (bf16[2,128,2048]{2,1,0:T(8,128)(2,1)S(1)}, bf16[2,128,2048]{2,1,0:T(8,128)(2,1)}, u32[]{:S(2)}) copy-start(bf16[2,128,2048]{2,1,0:T(8,128)(2,1)} %param.4) | copy-start | bytes 3145732
  328.2 6.7 %collective-permute-start.9 = (bf16[128,2048]{1,0:T(8,128)(2,1)S(1)}, bf16[128,2048]{1,0:T(8,128)(2,1)S(1)}, u32[]{:S(2)}, u32[]{:S(2)}) collective-permute-start(bf16[128,2048]{1,0:T(8,128)(2,1)S(1)} %broadcast_select_fusion.2), channel_id=1, source_target_pairs={{0,64},{64,0},{1,65},{65,1},{2,66},{66,2},{3,67},{67,3},{4,68},{68... | collective-permute-start | bytes 1572872 | tf_op jit(solution)/shard_map/ppermute | solution.py:18
Sparse Core Ops, SparseCore 0:
  24.6 100.9 all-gather.4
  128.3 102.6 all-gather.6
